TPU v7x, 32 devices: a whole 2x2x4 slice. The times are simulated.
32 devices in a mesh: group: 2 (over y), row: 4 (over x, core), head: 4 (over z).
Axes of the slice: x: 2, y: 2, z: 4, core: 2. Of those that a mesh axis runs over, the one named last changes fastest.
Arguments:
- latent: bfloat16 [1024, 3072], P('row', 'head'), may hold values from -6 to 6
- hint: bfloat16 [1024, 3072], P('row', 'head'), may hold values from -6 to 6
- timestep: int32 [1], replicated, may hold values from 0 to 7
- modulation: float32 [2, 8, 3, 3072], P('group'), may hold values from -3 to 3
- qkv_weight: bfloat16 [2, 3, 3072, 3072], P('group', None, None, 'head'), may hold values from -0.109375 to 0.109375
- out_weight: bfloat16 [2, 3072, 3072], P('group', None, 'head'), may hold values from -0.109375 to 0.109375
- zero_weight: bfloat16 [3072, 3072], P(None, 'head'), may hold values from -0.109375 to 0.109375
- cotangent: bfloat16 [1024, 3072], P('row', 'head'), may hold values from -6 to 6
Outputs:
- mixed: bfloat16 [1024, 3072], P('row', 'head')
- latent_grad: float32 [4, 2, 128, 3072], P('row', 'group', None, 'head')
- hint_grad: float32 [4, 2, 128, 3072], P('row', 'group', None, 'head')
- qkv_grad: float32 [3072, 3, 3072], P(('group', 'row'), None, 'head')
- out_grad: float32 [3072, 3072], P(('group', 'row'), 'head')
- zero_grad: float32 [3072, 3072], P(('group', 'row'), 'head')
All inputs are finite; a program needn't handle non-finite values.
Results may differ from a plain program's by a relative error of at most 0.015.
Values may be sent and summed in bfloat16 or wider, within the bound.
A program may use at most 128 MiB of HBM per device.

v0:
```python
import jax
import jax.numpy as jnp
from jax import lax
from jax.sharding import PartitionSpec as P

HD = 128


EPS = 1e-06


def from_partner(block, axis, distance):
    count = lax.axis_size(axis)
    route = []
    for low in range(count):
        high = low | 1 << distance
        if high != low and high < count:
            route += [(low, high), (high, low)]
    return lax.ppermute(block, axis, route)


def on_device(latent, hint, timestep, modulation, qkv_weight, out_weight, zero_weight, cotangent):
    tok, width = latent.shape
    heads_dev = width // HD
    scaling = HD ** (-0.5)
    control = lax.axis_index("group") == 0
    ctrl_mask = control.astype(jnp.float32)
    head_pos = lax.axis_index("head")
    steps_count = modulation.shape[1]
    pick = (lax.broadcasted_iota(jnp.int32, (steps_count,), 0) == timestep[0]).astype(jnp.float32)
    mods = jnp.sum(modulation[0] * pick[:, None, None], axis=0)
    shift, scale, gate = (mods[0], mods[1], mods[2])
    gate_dev = lax.dynamic_slice_in_dim(gate, head_pos * width, width, 0)
    scale_dev = lax.dynamic_slice_in_dim(scale, head_pos * width, width, 0)
    summed = (latent.astype(jnp.float32) + hint.astype(jnp.float32)).astype(jnp.bfloat16)
    inputs = jnp.where(control, summed, latent)
    whole = lax.all_gather(inputs, "head", axis=1, tiled=True)
    full_width = whole.shape[1]
    whole_f = whole.astype(jnp.float32)
    mean = jnp.mean(whole_f, axis=-1, keepdims=True)
    centred = whole_f - mean
    var = jnp.mean(centred * centred, axis=-1, keepdims=True)
    rstd = lax.rsqrt(var + EPS)
    nhat = centred * rstd
    normed = (nhat * (1.0 + scale) + shift).astype(jnp.bfloat16)
    w_qkv = qkv_weight[0]
    projected_qkv = jnp.einsum(
        "td,pde->pte", normed, w_qkv, preferred_element_type=jnp.float32
    ).astype(jnp.bfloat16)
    query, keys, values = (projected_qkv[0], projected_qkv[1], projected_qkv[2])
    q_heads = query.reshape(tok, heads_dev, HD)
    start_carry = (
        jnp.full((heads_dev, tok), -1e30, jnp.float32),
        jnp.zeros((heads_dev, tok), jnp.float32),
        jnp.zeros((tok, heads_dev, HD), jnp.float32),
    )

    def attend(carry, block):
        peak, total, acc = carry
        k_heads = block[0].reshape(-1, heads_dev, HD)
        v_heads = block[1].reshape(-1, heads_dev, HD)
        scores = (
            jnp.einsum("thd,shd->hts", q_heads, k_heads, preferred_element_type=jnp.float32)
            * scaling
        )
        new_peak = jnp.maximum(peak, jnp.max(scores, axis=-1))
        factor = jnp.exp(peak - new_peak)
        weights = jnp.exp(scores - new_peak[:, :, None])
        total = total * factor + jnp.sum(weights, axis=-1)
        acc = acc * factor.T[:, :, None] + jnp.einsum(
            "hts,shd->thd",
            weights.astype(jnp.bfloat16),
            v_heads,
            preferred_element_type=jnp.float32,
        )
        return ((new_peak, total, acc), None)

    carry = start_carry
    key_rows = lax.all_gather(keys, "row", axis=0, tiled=True)
    rows = key_rows.shape[0]
    count = max(rows // tok, 1)
    size = rows // count
    blocks = (
        key_rows.reshape(count, size, width),
        lax.all_gather(values, "row", axis=0, tiled=True).reshape(count, size, width),
    )
    carry, unused = lax.scan(attend, carry, blocks)
    peak, total, acc = carry
    attn = (acc / total.T[:, :, None]).reshape(tok, width).astype(jnp.bfloat16)
    lse = peak + jnp.log(total)
    w_out = out_weight[0]
    branch_term = lax.dot_general(
        attn, w_out, (((1,), (1,)), ((), ())), preferred_element_type=jnp.float32
    )
    branch = lax.psum_scatter(branch_term, "head", scatter_dimension=1, tiled=True)
    state = (inputs.astype(jnp.float32) + gate_dev * branch).astype(jnp.bfloat16)
    other_state = from_partner(state, "group", 0)
    control_out = jnp.where(control, state, other_state)
    main_out = jnp.where(control, other_state, state)
    hint_term = lax.dot_general(
        control_out, zero_weight, (((1,), (1,)), ((), ())), preferred_element_type=jnp.float32
    )
    projected = lax.psum_scatter(hint_term, "head", scatter_dimension=1, tiled=True)
    mixed = (main_out.astype(jnp.float32) + projected).astype(jnp.bfloat16)
    cot_full = lax.all_gather(cotangent, "head", axis=1, tiled=True)
    hint_back = jnp.dot(cot_full, zero_weight, preferred_element_type=jnp.float32).astype(
        jnp.bfloat16
    )
    incoming = jnp.where(control, hint_back, cotangent)
    gated = (gate_dev * incoming.astype(jnp.float32)).astype(jnp.bfloat16)
    gated_full = lax.all_gather(gated, "head", axis=1, tiled=True)
    attn_grad = jnp.dot(gated_full, w_out, preferred_element_type=jnp.float32).astype(jnp.bfloat16)
    dsum = jnp.sum(
        (attn_grad.astype(jnp.float32) * attn.astype(jnp.float32)).reshape(tok, heads_dev, HD),
        axis=-1,
    )
    g_heads = attn_grad.reshape(tok, heads_dev, HD)
    full_keys, full_values = (
        lax.all_gather(keys, "row", axis=0, tiled=True),
        lax.all_gather(values, "row", axis=0, tiled=True),
    )
    block_count = full_keys.shape[0] // tok
    key_blocks = (
        full_keys.reshape(block_count, tok, width),
        full_values.reshape(block_count, tok, width),
    )

    def backward_step(dq_acc, block):
        k_heads = block[0].reshape(tok, heads_dev, HD)
        v_heads = block[1].reshape(tok, heads_dev, HD)
        scores = (
            jnp.einsum("thd,shd->hts", q_heads, k_heads, preferred_element_type=jnp.float32)
            * scaling
        )
        probs = jnp.exp(scores - lse[:, :, None])
        dprobs = jnp.einsum("thd,shd->hts", g_heads, v_heads, preferred_element_type=jnp.float32)
        dscores = (probs * (dprobs - dsum.T[:, :, None])).astype(jnp.bfloat16)
        dq_acc = dq_acc + jnp.einsum(
            "hts,shd->thd", dscores, k_heads, preferred_element_type=jnp.float32
        )
        dkey = (
            jnp.einsum("hts,thd->shd", dscores, q_heads, preferred_element_type=jnp.float32)
            * scaling
        )
        dval = jnp.einsum(
            "hts,thd->shd", probs.astype(jnp.bfloat16), g_heads, preferred_element_type=jnp.float32
        )
        return (dq_acc, (dkey.reshape(tok, width), dval.reshape(tok, width)))

    dq_acc, key_terms = lax.scan(
        backward_step, jnp.zeros((tok, heads_dev, HD), jnp.float32), key_blocks
    )
    dquery = (dq_acc * scaling).reshape(tok, width).astype(jnp.bfloat16)
    dkey_sum, dval_sum = (
        lax.psum_scatter(key_terms[0].reshape(-1, width), "row", scatter_dimension=0, tiled=True),
        lax.psum_scatter(key_terms[1].reshape(-1, width), "row", scatter_dimension=0, tiled=True),
    )
    grads = jnp.stack([dquery, dkey_sum.astype(jnp.bfloat16), dval_sum.astype(jnp.bfloat16)])
    norm_term = jnp.einsum("pte,pde->td", grads, w_qkv, preferred_element_type=jnp.float32)
    nhat_dev = lax.dynamic_slice_in_dim(nhat, head_pos * width, width, 1)
    dnorm = lax.psum_scatter(norm_term, "head", scatter_dimension=1, tiled=True)
    scaled = dnorm * (1.0 + scale_dev)
    first, second = lax.psum(
        (jnp.sum(scaled, axis=-1), jnp.sum(scaled * nhat_dev, axis=-1)), "head"
    )
    first = first[:, None] / full_width
    second = second[:, None] / full_width
    d_in = incoming.astype(jnp.float32) + rstd * (scaled - first - nhat_dev * second)
    half = tok // 2
    group_pos = lax.axis_index("group")
    own_half = lax.dynamic_slice_in_dim(d_in, group_pos * half, half, 0)
    sent_half = lax.dynamic_slice_in_dim(d_in, (1 - group_pos) * half, half, 0)
    other_half = from_partner(sent_half, "group", 0)
    latent_grad = (own_half + other_half)[None, None]
    hint_grad = jnp.where(control, own_half, other_half)[None, None]
    offset = group_pos * half
    cot_half = lax.dynamic_slice_in_dim(cot_full, offset, half, 0)
    control_half = lax.dynamic_slice_in_dim(control_out, offset, half, 0)
    columns = normed
    qkv_grad = lax.psum_scatter(
        jnp.einsum("tc,pte->cpe", columns, grads, preferred_element_type=jnp.float32) * ctrl_mask,
        ("group", "row"),
        scatter_dimension=0,
        tiled=True,
    )
    columns = gated_full
    out_grad = lax.psum_scatter(
        lax.dot_general(columns, attn, (((0,), (0,)), ((), ())), preferred_element_type=jnp.float32)
        * ctrl_mask,
        ("group", "row"),
        scatter_dimension=0,
        tiled=True,
    )
    columns = cot_half
    zero_grad = lax.psum_scatter(
        lax.dot_general(
            columns, control_half, (((0,), (0,)), ((), ())), preferred_element_type=jnp.float32
        ),
        ("group", "row"),
        scatter_dimension=0,
        tiled=True,
    )
    return (mixed, latent_grad, hint_grad, qkv_grad, out_grad, zero_grad)


def solution(mesh):
    placed = (
        P("row", "head"),
        P("row", "head"),
        P(),
        P("group", None, None, None),
        P("group", None, None, "head"),
        P("group", None, "head"),
        P(None, "head"),
        P("row", "head"),
    )
    return jax.shard_map(
        on_device,
        mesh=mesh,
        in_specs=placed,
        out_specs=(
            P("row", "head"),
            P("row", "group", None, "head"),
            P("row", "group", None, "head"),
            P(("group", "row"), None, "head"),
            P(("group", "row"), "head"),
            P(("group", "row"), "head"),
        ),
        check_vma=False,
    )
```

profile of v0, /device:TPU:0, one launch (start us, length us, event | category | flops | bytes accessed | tf_op | source)
XLA Modules:
  0.0 839.1 jit_solution(3586530188123506919)
XLA Ops:
  7.2 2.1 fusion.39
  10.1 1.1 fusion.40
  11.8 38.1 %all-gather.8.cloned.1.call-done = bf16[256,3072]{1,0:T(8,128)(2,1)} async-done(((bf16[256,768]{1,0:T(8,128)(2,1)}), bf16[256,3072]{1,0:T(8,128)(2,1)}) %all-gather.8.cloned.1.call-update) | async-done | bytes 1572880 | tf_op jit(solution)/shard_map/all_gather | solution.py:37
  50.0 1.8 convert_reduce_fusion
  51.8 2.0 fusion.24
  53.8 7.5 fusion.29
  61.4 1.0 fusion.49
  64.1 16.9 %all-gather.16.cloned.1.call-done = bf16[1,1024,768]{2,1,0:T(8,128)(2,1)} async-done(((bf16[1,256,768]{2,1,0:T(8,128)(2,1)}), bf16[1,1024,768]{2,1,0:T(8,128)(2,1)}) %all-gather.16.cloned.1.call-update) | async-done | bytes 1572880 | tf_op jit(solution)/shard_map/all_gather | solution.py:85
  81.0 2.6 copy.36
  83.6 19.3 %all-gather.14.cloned.1.call-done = bf16[1,1024,768]{2,1,0:T(8,128)(2,1)} async-done(((bf16[1,256,768]{2,1,0:T(8,128)(2,1)}), bf16[1,1024,768]{2,1,0:T(8,128)(2,1)}) %all-gather.14.cloned.1.call-update) | async-done | bytes 1572880 | tf_op jit(solution)/shard_map/all_gather | solution.py:79
  102.9 2.6 copy.34
  105.5 9.7 %while.30 = (s32[]{:T(128)}, f32[6,256]{1,0:T(8,128)S(1)}, f32[6,256]{1,0:T(8,128)S(1)}, f32[256,6,128]{0,2,1:T(8,128)S(1)}, bf16[4,256,768]{1,2,0:T(8,128)(2,1)...) while((s32[]{:T(128)}, f32[6,256]{1,0:T(8,128)S(1)}, ...), condition=%wide.region_6.7_spmd.clone, body=%wide.region_3.6_spmd.clone.sunk | while | flops 204284928 | bytes 9142389 | solution.py:87
  105.5 1.2 constant_dynamic-slice_fusion.8
  107.9 1.2 constant_dynamic-slice_fusion.8
  110.3 1.2 constant_dynamic-slice_fusion.8
  112.8 1.2 constant_dynamic-slice_fusion.8
  115.3 5.6 fusion.17
  121.0 20.4 %all-gather.10.cloned.1.call-done = bf16[256,3072]{1,0:T(8,128)(2,1)} async-done(((bf16[256,768]{1,0:T(8,128)(2,1)}), bf16[256,3072]{1,0:T(8,128)(2,1)}) %all-gather.10.cloned.1.call-update) | async-done | bytes 1572880 | tf_op jit(solution)/shard_map/all_gather | solution.py:105
  141.4 61.9 %reduce-scatter.9.cloned.1.call-done = f32[256,768]{1,0:T(8,128)} async-done(((f32[256,3072]{1,0:T(8,128)}), f32[256,768]{1,0:T(8,128)}) %reduce-scatter.9.cloned.1.call-update) | async-done | bytes 786448 | tf_op jit(solution)/shard_map/reduce_scatter | solution.py:95
  203.3 5.5 multiply_convert_fusion.2
  209.3 36.8 %all-gather.12.cloned.1.call-done = bf16[256,3072]{1,0:T(8,128)(2,1)} async-done(((bf16[256,768]{1,0:T(8,128)(2,1)}), bf16[256,3072]{1,0:T(8,128)(2,1)}) %all-gather.12.cloned.1.call-update) | async-done | bytes 1572880 | tf_op jit(solution)/shard_map/all_gather | solution.py:111
  246.1 4.2 convert_multiply_fusion
  250.9 30.1 %while.31 = (s32[]{:T(128)}, f32[256,6,128]{0,2,1:T(8,128)}, f32[4,256,768]{2,1,0:T(8,128)}, f32[4,256,768]{2,1,0:T(8,128)}, bf16[4,256,768]{1,2,0:T(8,128)(2,1)...) while((s32[]{:T(128)}, f32[256,6,128]{0,2,1:T(8,128)}, ...), condition=%wide.region_11.12_spmd.clone, body=%wide.region_10.11_spmd.clone.sunk | while | flops 506265600 | bytes 20852884 | solution.py:150
  250.9 1.0 constant_dynamic-slice_fusion.10
  251.9 1.0 constant_dynamic-slice_fusion.9
  254.5 1.2 fusion.110
  256.3 1.2 constant_dynamic-update-slice_fusion.3
  257.6 1.0 constant_dynamic-slice_fusion.10
  258.6 1.0 constant_dynamic-slice_fusion.9
  261.2 2.3 fusion.110
  264.1 1.2 constant_dynamic-update-slice_fusion.3
  265.4 1.0 constant_dynamic-slice_fusion.10
  266.4 1.0 constant_dynamic-slice_fusion.9
  269.0 2.3 fusion.110
  271.9 1.2 constant_dynamic-update-slice_fusion.3
  273.2 1.0 constant_dynamic-slice_fusion.10
  274.2 1.0 constant_dynamic-slice_fusion.9
  276.8 2.3 fusion.110
  279.8 1.2 constant_dynamic-update-slice_fusion.3
  282.4 35.6 %reduce-scatter.15.cloned.1.call-done = f32[256,768]{1,0:T(8,128)} async-done(((f32[1024,768]{1,0:T(8,128)}), f32[256,768]{1,0:T(8,128)}) %reduce-scatter.15.cloned.1.call-update) | async-done | bytes 786448 | tf_op jit(solution)/shard_map/reduce_scatter | solution.py:156
  318.0 1.2 convert_bitcast_fusion
  319.2 40.1 %reduce-scatter.13.cloned.1.call-done = f32[256,768]{1,0:T(8,128)} async-done(((f32[1024,768]{1,0:T(8,128)}), f32[256,768]{1,0:T(8,128)}) %reduce-scatter.13.cloned.1.call-update) | async-done | bytes 786448 | tf_op jit(solution)/shard_map/reduce_scatter | solution.py:155
  359.3 1.2 convert_bitcast_fusion.1
  360.5 10.5 %fusion.19 = f32[256,3072]{1,0:T(8,128)} fusion(bf16[1,3,3072,768]{3,2,1,0:T(8,128)(2,1)} %param.16, bf16[1,256,768]{2,1,0:T(8,128)(2,1)S(1)} %convert_bitcast_fusion, bf16[1,256,768]{2,1,0:T(8,128)(2,1)S(1)} %convert_bitcast_fusion.1, bf16[1,256,768]{2,1,0:T(8,128)(2,1)S(1)} %copy.44), kind=kOutput, calls=%fused_computation.38 | convolution fusion | flops 3625058304 | bytes 18481152 | tf_op jit(solution)/shard_map/pte,pde->td/dot_general | solution.py:159
  371.9 1.5 collective-permute-start
  373.4 9.4 %collective-permute-done = bf16[256,768]{1,0:T(8,128)(2,1)S(1)} collective-permute-done((bf16[256,768]{1,0:T(8,128)(2,1)S(1)}, bf16[256,768]{1,0:T(8,128)(2,1)S(1)}, u32[]{:S(2)}, u32[]{:S(2)}) %collective-permute-start) | collective-permute-done | bytes 393248 | tf_op jit(solution)/shard_map/ppermute | solution.py:19
  382.8 5.5 fusion.51
  388.5 1.4 copy-done.11
  389.8 5.1 fusion.37
  396.5 5.1 convolution_multiply_fusion.2
  401.9 1.1 copy-done.2
  403.0 11.7 %broadcast_multiply_fusion = f32[3072,3,768]{2,0,1:T(8,128)} fusion(f32[]{:T(128)S(6)} %convert_element_type.120, bf16[1,256,768]{2,1,0:T(8,128)(2,1)S(1)} %convert_bitcast_fusion, bf16[1,256,768]{2,1,0:T(8,128)(2,1)S(1)} %convert_bitcast_fusion.1, bf16[1,256,768]{2,1,0:T(8,128)(2,1)S(1)} %copy.44, f32[3072]{0:T(1024)S(1)} %bitcast.180, ...), kind=kOutput, calls=%fused_computation.32 | convolution fusion | flops 3639214080 | bytes 31090692 | tf_op jit(solution)/shard_map/tc,pte->cpe/dot_general | solution.py:181
  415.4 2.3 fusion.22
  417.7 13.7 %reduce-scatter.17.cloned.1.call-done = f32[256,768]{1,0:T(8,128)} async-done(((f32[256,3072]{1,0:T(8,128)}), f32[256,768]{1,0:T(8,128)}) %reduce-scatter.17.cloned.1.call-update) | async-done | bytes 786448 | tf_op jit(solution)/shard_map/reduce_scatter | solution.py:161
  431.4 1.6 multiply_reduce_fusion.1
  433.0 10.6 %all-reduce = (f32[256]{0:T(256)S(1)}, f32[256]{0:T(256)S(1)}) all-reduce(f32[256]{0:T(256)S(1)} %get-tuple-element.197, f32[256]{0:T(256)S(1)} %get-tuple-element.196), channel_id=1, replica_groups=mesh['group'=2,'row'=4,'head'=4] {'head'}, use_global_device_ids=true, to_apply=%region_18.19 | all-reduce | flops 512 | bytes 4096 | tf_op jit(solution)/shard_map/psum | solution.py:163
  443.6 1.6 multiply_add_fusion
  445.2 1.8 collective-permute-start.1
  447.0 46.9 %reduce-scatter.11.cloned.1.call-done = f32[256,768]{1,0:T(8,128)} async-done(((f32[256,3072]{1,0:T(8,128)}), f32[256,768]{1,0:T(8,128)}) %reduce-scatter.11.cloned.1.call-update) | async-done | bytes 786448 | tf_op jit(solution)/shard_map/reduce_scatter | solution.py:103
  493.9 2.0 add_convert_fusion.1
  495.9 0.9 select_bitcast_fusion
  496.8 77.7 %reduce-scatter.23.cloned.1.call-done = f32[384,768]{1,0:T(8,128)} async-done(((f32[3072,768]{1,0:T(8,128)}), f32[384,768]{1,0:T(8,128)}) %reduce-scatter.23.cloned.1.call-update) | async-done | bytes 1179664 | tf_op jit(solution)/shard_map/reduce_scatter | solution.py:195
  574.5 80.5 %reduce-scatter.21.cloned.1.call-done = f32[384,768]{1,0:T(8,128)} async-done(((f32[3072,768]{1,0:T(8,128)}), f32[384,768]{1,0:T(8,128)}) %reduce-scatter.21.cloned.1.call-update) | async-done | bytes 1179664 | tf_op jit(solution)/shard_map/reduce_scatter | solution.py:187
  655.0 177.6 %reduce-scatter.19.cloned.1.call-done = f32[384,3,768]{2,0,1:T(8,128)} async-done(((f32[3072,3,768]{2,0,1:T(8,128)}), f32[384,3,768]{2,0,1:T(8,128)}) %reduce-scatter.19.cloned.1.call-update) | async-done | bytes 3538960 | tf_op jit(solution)/shard_map/reduce_scatter | solution.py:180
  (140 shorter events, 22.0 us)
Async XLA Ops:
  7.2 42.8 %all-gather.8.cloned.1.call-start = ((), (), s32[]{:S(2)}) async-start(), calls=%async_computation.8 | async-start | bytes 1966080 | tf_op jit(solution)/shard_map/all_gather | solution.py:37
  9.4 71.7 %all-gather.16.cloned.1.call-start = ((), (), s32[]{:S(2)}) async-start(), calls=%async_computation.20 | async-start | bytes 1966080 | tf_op jit(solution)/shard_map/all_gather | solution.py:85
  11.8 49.5 %copy-start.13 = (f32[1,3072]{1,0:T(1,128)}, f32[1,3072]{1,0:T(1,128)S(1)}, u32[]{:S(2)}) copy-start(f32[1,3072]{1,0:T(1,128)S(1)} %get-tuple-element.248) | copy-start | bytes 36868
  11.8 49.5 %copy-start.15 = (f32[1,3072]{1,0:T(1,128)}, f32[1,3072]{1,0:T(1,128)S(1)}, u32[]{:S(2)}) copy-start(f32[1,3072]{1,0:T(1,128)S(1)} %get-tuple-element.249) | copy-start | bytes 36868
  50.0 3.8 copy-start.1
  51.8 9.6 %copy-start.19 = (f32[256]{0:T(256)}, f32[256]{0:T(256)S(1)}, u32[]{:S(2)}) copy-start(f32[256]{0:T(256)S(1)} %broadcast_multiply_fusion.3) | copy-start | bytes 3076
  53.8 7.6 copy-start.17
  62.4 40.5 %all-gather.14.cloned.1.call-start = ((), (), s32[]{:S(2)}) async-start(), calls=%async_computation.19 | async-start | bytes 1966080 | tf_op jit(solution)/shard_map/all_gather | solution.py:79
  63.1 78.3 %all-gather.10.cloned.1.call-start = ((), (), s32[]{:S(2)}) async-start(), calls=%async_computation.11 | async-start | bytes 1966080 | tf_op jit(solution)/shard_map/all_gather | solution.py:105
  63.7 139.6 %reduce-scatter.9.cloned.1.call-start = ((), (), s32[]{:S(2)}) async-start(), calls=%async_computation.9 | async-start | bytes 3932160 | tf_op jit(solution)/shard_map/reduce_scatter | solution.py:95
  115.3 93.9 %copy-start.3 = (bf16[256,6,128]{0,2,1:T(8,128)(2,1)}, bf16[256,6,128]{0,2,1:T(8,128)(2,1)S(1)}, u32[]{:S(2)}) copy-start(bf16[256,6,128]{0,2,1:T(8,128)(2,1)S(1)} %divide_convert_fusion) | copy-start | bytes 1179652
  120.9 82.4 %copy-start.6 = (bf16[256,768]{1,0:T(8,128)(2,1)S(1)}, bf16[256,768]{1,0:T(8,128)(2,1)}, u32[]{:S(2)}) copy-start(bf16[256,768]{1,0:T(8,128)(2,1)} %fusion.39) | copy-start | bytes 1179652
  120.9 82.4 %copy-start.12 = (bf16[256,768]{1,0:T(8,128)(2,1)S(1)}, bf16[256,768]{1,0:T(8,128)(2,1)}, u32[]{:S(2)}) copy-start(bf16[256,768]{1,0:T(8,128)(2,1)} %param.19) | copy-start | bytes 1179652
  120.9 125.2 %all-gather.12.cloned.1.call-start = ((), (), s32[]{:S(2)}) async-start(), calls=%async_computation.12 | async-start | bytes 1966080 | tf_op jit(solution)/shard_map/all_gather | solution.py:111
  208.9 109.1 %reduce-scatter.15.cloned.1.call-start = ((), (), s32[]{:S(2)}) async-start(), calls=%async_computation.14 | async-start | bytes 3932160 | tf_op jit(solution)/shard_map/reduce_scatter | solution.py:156
  281.0 1.1 copy-start
  281.0 78.2 %reduce-scatter.13.cloned.1.call-start = ((), (), s32[]{:S(2)}) async-start(), calls=%async_computation.13 | async-start | bytes 3932160 | tf_op jit(solution)/shard_map/reduce_scatter | solution.py:155
  281.8 149.6 %reduce-scatter.17.cloned.1.call-start = ((), (), s32[]{:S(2)}) async-start(), calls=%async_computation.15 | async-start | bytes 3932160 | tf_op jit(solution)/shard_map/reduce_scatter | solution.py:161
  371.0 1.0 copy-start.7
  371.0 122.9 %reduce-scatter.11.cloned.1.call-start = ((), (), s32[]{:S(2)}) async-start(), calls=%async_computation.10 | async-start | bytes 3932160 | tf_op jit(solution)/shard_map/reduce_scatter | solution.py:103
  371.9 10.8 %collective-permute-start = (bf16[256,768]{1,0:T(8,128)(2,1)S(1)}, bf16[256,768]{1,0:T(8,128)(2,1)S(1)}, u32[]{:S(2)}, u32[]{:S(2)}) collective-permute-start(bf16[256,768]{1,0:T(8,128)(2,1)S(1)} %copy-done.7), channel_id=1, source_target_pairs={{0,16},{16,0},{1,17},{17,1},{2,18},{18,2},{3,19},{19,3},{4,20},{20... | collective-permute-start | bytes 1179656 | tf_op jit(solution)/shard_map/ppermute | solution.py:19
  382.8 5.6 copy-start.8
  388.4 1.4 copy-start.11
  388.4 186.1 %reduce-scatter.23.cloned.1.call-start = ((), (), s32[]{:S(2)}) async-start(), calls=%async_computation.18 | async-start | bytes 10616832 | tf_op jit(solution)/shard_map/reduce_scatter | solution.py:195
  394.9 1.0 copy-start.4
  394.9 1.5 copy-start.5
  394.9 260.1 %reduce-scatter.21.cloned.1.call-start = ((), (), s32[]{:S(2)}) async-start(), calls=%async_computation.17 | async-start | bytes 10616832 | tf_op jit(solution)/shard_map/reduce_scatter | solution.py:187
  401.5 1.4 copy-start.2
  401.5 1.4 copy-start.14
  401.6 1.4 copy-start.16
  401.6 1.4 copy-start.18
  401.6 1.4 copy-start.20
  401.6 431.0 %reduce-scatter.19.cloned.1.call-start = ((), (), s32[]{:S(2)}) async-start(), calls=%async_computation.16 | async-start | bytes 31850496 | tf_op jit(solution)/shard_map/reduce_scatter | solution.py:180
  415.4 28.2 %copy-start.10 = (f32[256,768]{1,0:T(8,128)S(1)}, f32[256,768]{1,0:T(8,128)}, u32[]{:S(2)}) copy-start(f32[256,768]{1,0:T(8,128)} %get-tuple-element.253) | copy-start | bytes 2359300
  417.7 76.2 %copy-start.9 = (bf16[256,768]{1,0:T(8,128)(2,1)S(1)}, bf16[256,768]{1,0:T(8,128)(2,1)}, u32[]{:S(2)}) copy-start(bf16[256,768]{1,0:T(8,128)(2,1)} %copy-done.8) | copy-start | bytes 1179652
  445.2 50.7 %collective-permute-start.1 = (f32[128,768]{1,0:T(8,128)S(1)}, f32[128,768]{1,0:T(8,128)S(1)}, u32[]{:S(2)}, u32[]{:S(2)}) collective-permute-start(f32[128,768]{1,0:T(8,128)S(1)} %constant_dynamic-slice_fusion.4), channel_id=1, source_target_pairs={{0,16},{16,0},{1,17},{17,1},{2,18},{18,2},{3,19},{19,3},{4,20},{20... | collective-permute-start | bytes 1179656 | tf_op jit(solution)/shard_map/ppermute | solution.py:19
Sparse Core Ops, SparseCore 0:
  10.1 39.7 all-gather.7
  62.5 18.5 all-gather.15
  83.2 19.6 all-gather.13
  104.3 37.0 all-gather.9
  144.1 59.1 reduce-scatter.8
  209.0 37.0 all-gather.11
  281.2 36.7 reduce-scatter.14
  321.3 37.9 reduce-scatter.12
  371.1 60.2 reduce-scatter.16
  433.6 60.2 reduce-scatter.10
  497.9 76.5 reduce-scatter.22
  578.5 76.5 reduce-scatter.20
  659.3 173.2 reduce-scatter.18
where the time goes:
time: 840 us; the launch traced here: 839 us
  waiting for transfers between devices  677 us (81%)
  matrix products  79.1 us (9%)
  local copies, waits for them, and re-layouts  32.6 us (4%)
  other arithmetic  20.3 us (2%)
  between operations  14.9 us (2%)
  blocking collectives  10.6 us (1%)
    reduce_scatter x1, waiting for transfers between devices, on_device(): lax.psum_scatter(jnp.einsum('tc,pte->cpe', columns, grads, preferred_elem...  178 us
    reduce_scatter x1, waiting for transfers between devices, on_device(): lax.psum_scatter(lax.dot_general(columns, attn, (((0,), (0,)), ((), ())),...  80.5 us
    reduce_scatter x1, waiting for transfers between devices, on_device(): lax.psum_scatter(lax.dot_general(columns, control_half, (((0,), (0,)), ((...  77.7 us
    reduce_scatter x1, waiting for transfers between devices, on_device(): lax.psum_scatter(branch_term, 'head', scatter_dimension=1, tiled=True)  61.9 us
    reduce_scatter x1, waiting for transfers between devices, on_device(): lax.psum_scatter(hint_term, 'head', scatter_dimension=1, tiled=True)  46.9 us
    reduce_scatter x1, waiting for transfers between devices, on_device(): lax.psum_scatter(key_terms[0].reshape(-1, width), 'row', scatter_dimensio...  40.1 us
    all_gather x1, waiting for transfers between devices, on_device(): whole = lax.all_gather(inputs, 'head', axis=1, tiled=True)  38.1 us
    all_gather x1, waiting for transfers between devices, on_device(): gated_full = lax.all_gather(gated, 'head', axis=1, tiled=True)  36.8 us
  transfers between devices with their start and end apart: 15, of which 14 were waited for; matrix products, arithmetic and copies ran while one was open for 7% of the time, Pallas kernels for 0%

commit v1 on v0

v1 whole, which is shorter than its diff:
```python
import functools
import math

import jax
import jax.numpy as jnp
from jax import lax
from jax.experimental import pallas as pl
from jax.experimental.pallas import tpu as pltpu
from jax.sharding import PartitionSpec as P

HD = 128


EPS = 1e-06

MESH = pl.DeviceIdType.MESH


def place(axes, sizes):
    index = 0
    for axis, size in zip(axes, sizes):
        index = index * size + lax.axis_index(axis)
    return index


def coords(index, axes, sizes):
    spot = {}
    for axis, size in reversed(list(zip(axes, sizes))):
        spot[axis] = lax.rem(index, size)
        index = index // size
    return spot


def exchange_kernel(plans, *refs):
    count = len(plans)
    ins, outs = refs[:count], refs[count : 2 * count]
    sems = refs[2 * count :]
    group = lax.axis_index("group")
    barrier = pltpu.get_barrier_semaphore()
    greeted = 0
    seen = set()
    for kind, axes, sizes, source in plans:
        if axes in seen:
            continue
        seen.add(axes)
        total = math.prod(sizes)
        me = place(axes, sizes)
        for step in range(1, total):
            pl.semaphore_signal(
                barrier,
                inc=1,
                device_id=coords(lax.rem(me + step, total), axes, sizes),
                device_id_type=MESH,
            )
        greeted += total - 1
    pl.semaphore_wait(barrier, greeted)

    def each(plan, number, action):
        kind, axes, sizes, source = plan
        x, out = ins[number], outs[number]
        send, recv, local = sems[3 * number : 3 * number + 3]
        total = math.prod(sizes)
        me = place(axes, sizes)
        spread = kind.startswith("spread")
        dealt = kind.endswith("deal")
        per = total // sizes[0] if spread else total
        mine = lax.rem(me, per)

        def when(index):
            if source is None:
                return None
            if spread:
                return index // per == source
            return group == source

        def guarded(condition, work):
            if condition is None:
                work()
            else:
                pl.when(condition)(work)

        def own():
            copy = pltpu.make_async_copy(x.at[me] if dealt else x, out.at[mine], local)
            copy.start() if action == "start" else copy.wait()

        for step in range(1, total):
            there = lax.rem(me + step, total)
            origin = lax.rem(me + total - step, total)

            def copy_of(slot, block):
                return pltpu.make_async_remote_copy(
                    src_ref=x.at[block] if dealt else x,
                    dst_ref=out.at[slot],
                    send_sem=send.at[step],
                    recv_sem=recv.at[step],
                    device_id=coords(there, axes, sizes),
                    device_id_type=MESH,
                )

            if action == "start":
                guarded(when(me), lambda: copy_of(mine, there).start())
            else:
                guarded(when(me), lambda: copy_of(mine, there).wait_send())
                guarded(
                    when(origin), lambda: copy_of(lax.rem(origin, per), there).wait_recv()
                )
        guarded(when(me), own)

    for number, plan in enumerate(plans):
        each(plan, number, "start")
    for number, plan in enumerate(plans):
        each(plan, number, "wait")


def exchange(number, name, *wants):
    plans, arrays, shapes, scratch = [], [], [], []
    for kind, x, axes, source in wants:
        sizes = tuple(lax.axis_size(axis) for axis in axes)
        total = math.prod(sizes)
        per = total // sizes[0] if kind.startswith("spread") else total
        block = x.shape[1:] if kind.endswith("deal") else x.shape
        plans.append((kind, axes, sizes, source))
        arrays.append(x)
        shapes.append(jax.ShapeDtypeStruct((per,) + block, x.dtype))
        scratch += [
            pltpu.SemaphoreType.DMA((total,)),
            pltpu.SemaphoreType.DMA((total,)),
            pltpu.SemaphoreType.DMA,
        ]
    return pl.pallas_call(
        functools.partial(exchange_kernel, tuple(plans)),
        out_shape=shapes,
        in_specs=[pl.BlockSpec(memory_space=pl.ANY)] * len(arrays),
        out_specs=[pl.BlockSpec(memory_space=pl.ANY)] * len(arrays),
        scratch_shapes=scratch,
        compiler_params=pltpu.CompilerParams(collective_id=number, has_side_effects=True),
        name=name,
    )(*arrays)


def attention_kernel(q_ref, k_ref, v_ref, g_ref, o_ref, dq_ref, dk_ref, dv_ref):
    scaling = HD ** (-0.5)
    query, cot = q_ref[...], g_ref[...]
    keys = k_ref[...].reshape(-1, HD)
    values = v_ref[...].reshape(-1, HD)
    last = (((1,), (1,)), ((), ()))
    first = (((0,), (0,)), ((), ()))
    scores = lax.dot_general(query, keys, last, preferred_element_type=jnp.float32) * scaling
    top = jnp.max(scores, axis=-1, keepdims=True)
    weights = jnp.exp(scores - top)
    inverse = 1.0 / jnp.sum(weights, axis=-1, keepdims=True)
    out = jnp.dot(weights.astype(jnp.bfloat16), values, preferred_element_type=jnp.float32)
    out = (out * inverse).astype(jnp.bfloat16)
    o_ref[...] = out
    dsum = jnp.sum(cot.astype(jnp.float32) * out.astype(jnp.float32), axis=-1, keepdims=True)
    probs = weights * inverse
    dprobs = lax.dot_general(cot, values, last, preferred_element_type=jnp.float32)
    dscores = (probs * (dprobs - dsum)).astype(jnp.bfloat16)
    dquery = jnp.dot(dscores, keys, preferred_element_type=jnp.float32) * scaling
    dq_ref[...] = dquery.astype(jnp.bfloat16)
    dkey = lax.dot_general(dscores, query, first, preferred_element_type=jnp.float32) * scaling
    dk_ref[...] = dkey.astype(jnp.bfloat16).reshape(dk_ref.shape)
    dval = lax.dot_general(
        probs.astype(jnp.bfloat16), cot, first, preferred_element_type=jnp.float32
    )
    dv_ref[...] = dval.astype(jnp.bfloat16).reshape(dv_ref.shape)


def attention(query, keys, values, cot):
    tok, width = query.shape
    rows = keys.shape[0]
    own = pl.BlockSpec((tok, HD), lambda h: (0, h))
    every = pl.BlockSpec((rows, tok, HD), lambda h: (0, 0, h))
    small = jax.ShapeDtypeStruct((tok, width), jnp.bfloat16)
    large = jax.ShapeDtypeStruct((rows, tok, width), jnp.bfloat16)
    return pl.pallas_call(
        attention_kernel,
        grid=(width // HD,),
        out_shape=[small, small, large, large],
        in_specs=[own, every, every, own],
        out_specs=[own, own, every, every],
        compiler_params=pltpu.CompilerParams(vmem_limit_bytes=50 * 1024 * 1024),
        name="attention",
    )(query, keys, values, cot)


def from_partner(block, axis, distance):
    count = lax.axis_size(axis)
    route = []
    for low in range(count):
        high = low | 1 << distance
        if high != low and high < count:
            route += [(low, high), (high, low)]
    return lax.ppermute(block, axis, route)


def dot(a, b, dims):
    return lax.dot_general(a, b, (dims, ((), ())), preferred_element_type=jnp.float32)


def on_device(latent, hint, timestep, modulation, qkv_weight, out_weight, zero_weight, cotangent):
    f32, bf16 = jnp.float32, jnp.bfloat16
    tok, width = latent.shape
    half = tok // 2
    n_head, n_row = lax.axis_size("head"), lax.axis_size("row")
    full_width = n_head * width
    parts = 2 * n_row
    plane = ("group", "row")
    group_pos = lax.axis_index("group")
    control = group_pos == 0
    head_pos = lax.axis_index("head")
    steps_count = modulation.shape[1]
    pick = (lax.broadcasted_iota(jnp.int32, (steps_count,), 0) == timestep[0]).astype(f32)
    mods = jnp.sum(modulation[0] * pick[:, None, None], axis=0)
    shift, scale, gate = (mods[0], mods[1], mods[2])
    gate_dev = lax.dynamic_slice_in_dim(gate, head_pos * width, width, 0)
    scale_dev = lax.dynamic_slice_in_dim(scale, head_pos * width, width, 0)
    w_qkv, w_out = qkv_weight[0], out_weight[0]

    def widen(blocks):
        return blocks.transpose(1, 0, 2).reshape(blocks.shape[1], -1)

    def deal_out(x):
        return x.reshape(x.shape[0], parts, -1).transpose(1, 0, 2)

    summed = (latent.astype(f32) + hint.astype(f32)).astype(bf16)
    inputs = jnp.where(control, summed, latent)
    cot_own = lax.dynamic_slice_in_dim(cotangent, group_pos * half, half, 0)
    whole, cot_half = exchange(
        0,
        "gather_inputs",
        ("gather", cot_own, ("head",), None),
        ("gather", inputs, ("head",), None),
    )[::-1]
    cot_half = widen(cot_half)
    hint_half = dot(cot_half, zero_weight, ((1,), (0,))).astype(bf16)
    hint_other = from_partner(hint_half, "group", 0)
    cot_other = from_partner(cot_half, "group", 0)

    whole_f = widen(whole).astype(f32)
    mean = jnp.mean(whole_f, axis=-1, keepdims=True)
    centred = whole_f - mean
    var = jnp.mean(centred * centred, axis=-1, keepdims=True)
    rstd = lax.rsqrt(var + EPS)
    nhat = centred * rstd
    normed = (nhat * (1.0 + scale) + shift).astype(bf16)
    query, keys, values = [
        dot(normed, w_qkv[index], ((1,), (0,))).astype(bf16) for index in range(3)
    ]

    hint_back = jnp.concatenate([hint_half, hint_other])
    incoming = jnp.where(control, hint_back, cotangent)
    gated = (gate_dev * hint_back.astype(f32)).astype(bf16)
    gated_blocks, all_keys, all_values, cot_parts, normed_parts = exchange(
        1,
        "gather_keys",
        ("gather", gated, ("head",), 0),
        ("gather", keys, ("row",), None),
        ("gather", values, ("row",), None),
        ("deal", deal_out(cot_half), plane, None),
        ("spread_deal", deal_out(normed), plane, 0),
    )
    gated_main = (gate * jnp.concatenate([cot_other, cot_half]).astype(f32)).astype(bf16)
    gated_full = jnp.where(control, widen(gated_blocks), gated_main)
    attn_grad = dot(gated_full, w_out, ((1,), (0,))).astype(bf16)
    attn, dquery, key_terms, value_terms = attention(query, all_keys, all_values, attn_grad)
    branch_term = jnp.stack(
        [
            dot(attn, w_out[index * width : (index + 1) * width], ((1,), (1,))).astype(bf16)
            for index in range(n_head)
        ]
    )
    branch_parts, key_parts, value_parts, all_attn, gated_parts = exchange(
        2,
        "sum_branch",
        ("deal", branch_term, ("head",), None),
        ("deal", key_terms, ("row",), None),
        ("deal", value_terms, ("row",), None),
        ("spread", attn, plane, 0),
        ("spread_deal", deal_out(gated_full), plane, 0),
    )
    branch = jnp.sum(branch_parts.astype(f32), axis=0)
    state = (inputs.astype(f32) + gate_dev * branch).astype(bf16)
    dkey = jnp.sum(key_parts.astype(f32), axis=0).astype(bf16)
    dval = jnp.sum(value_parts.astype(f32), axis=0).astype(bf16)
    grads = jnp.stack([dquery, dkey, dval])

    scaled_nhat = nhat * (1.0 + scale)
    terms = []
    first, second = 0.0, 0.0
    for index in range(n_head):
        cols = slice(index * width, (index + 1) * width)
        term = sum(dot(grads[c], w_qkv[c, cols], ((1,), (1,))) for c in range(3))
        first = first + jnp.sum(term * (1.0 + scale[cols]), axis=-1)
        second = second + jnp.sum(term * scaled_nhat[:, cols], axis=-1)
        terms.append(term.astype(bf16))
    norm_parts, sum_parts, all_state, near_grads, main_state = exchange(
        3,
        "sum_norm",
        ("deal", jnp.stack(terms), ("head",), None),
        ("gather", jnp.stack([first, second]), ("head",), None),
        ("spread", state, plane, 0),
        ("spread", grads, ("group",), 0),
        ("spread", state[:half], ("group",), 1),
    )
    dnorm = jnp.sum(norm_parts.astype(f32), axis=0)
    sums = jnp.sum(sum_parts, axis=0) / full_width
    nhat_dev = lax.dynamic_slice_in_dim(nhat, head_pos * width, width, 1)
    scaled = dnorm * (1.0 + scale_dev)
    d_in = incoming.astype(f32) + rstd * (
        scaled - sums[0][:, None] - nhat_dev * sums[1][:, None]
    )
    own_half = lax.dynamic_slice_in_dim(d_in, group_pos * half, half, 0)
    sent_half = lax.dynamic_slice_in_dim(d_in, (1 - group_pos) * half, half, 0)

    row_pos = lax.axis_index("row")
    state_row = lax.dynamic_index_in_dim(all_state, row_pos, 0, keepdims=False)
    state_half = lax.dynamic_slice_in_dim(state_row, group_pos * half, half, 0)
    hint_term = jnp.stack(
        [
            dot(state_half, zero_weight[index * width : (index + 1) * width], ((1,), (1,)))
            .astype(bf16)
            for index in range(n_head)
        ]
    )
    hint_parts, other_parts, all_grads = exchange(
        4,
        "sum_hint",
        ("deal", hint_term, ("head",), None),
        ("gather", sent_half.astype(bf16), ("group",), None),
        ("gather", near_grads[0], ("row",), None),
    )
    projected = jnp.sum(hint_parts.astype(f32), axis=0)
    main_half = jnp.where(control, main_state[0], state[half:])
    mixed_half = (main_half.astype(f32) + projected).astype(bf16)
    mixed_other = from_partner(mixed_half, "group", 0)
    mixed = jnp.where(
        control,
        jnp.concatenate([mixed_half, mixed_other]),
        jnp.concatenate([mixed_other, mixed_half]),
    )
    other_half = lax.dynamic_index_in_dim(other_parts, 1 - group_pos, 0, keepdims=False).astype(f32)
    latent_grad = (own_half + other_half)[None, None]
    hint_grad = jnp.where(control, own_half, other_half)[None, None]

    normed_cols = normed_parts.reshape(n_row * tok, -1)
    qkv_grad = jnp.stack(
        [
            dot(normed_cols, all_grads[:, c].reshape(n_row * tok, width), ((0,), (0,)))
            for c in range(3)
        ],
        axis=1,
    )
    out_grad = dot(
        gated_parts.reshape(n_row * tok, -1), all_attn.reshape(n_row * tok, width), ((0,), (0,))
    )
    cot_cols = cot_parts.reshape(2, n_row, half, -1).transpose(1, 0, 2, 3)
    zero_grad = dot(
        cot_cols.reshape(n_row * tok, -1), all_state.reshape(n_row * tok, width), ((0,), (0,))
    )
    return (mixed, latent_grad, hint_grad, qkv_grad, out_grad, zero_grad)


def solution(mesh):
    placed = (
        P("row", "head"),
        P("row", "head"),
        P(),
        P("group", None, None, None),
        P("group", None, None, "head"),
        P("group", None, "head"),
        P(None, "head"),
        P("row", "head"),
    )
    return jax.shard_map(
        on_device,
        mesh=mesh,
        in_specs=placed,
        out_specs=(
            P("row", "head"),
            P("row", "group", None, "head"),
            P("row", "group", None, "head"),
            P(("group", "row"), None, "head"),
            P(("group", "row"), "head"),
            P(("group", "row"), "head"),
        ),
        check_vma=False,
    )
```

time: 840 us -> 486 us (0.58)
  waiting for transfers between devices: 677 us -> 0.01 us
  Pallas kernels: 0 us -> 336 us
  other arithmetic: 20.3 us -> 38.7 us
  between operations: 14.9 us -> 1.97 us
  blocking collectives: 10.6 us -> 0 us
    reduce_scatter x8 -> x0, waiting for transfers between devices: 534 us -> none  [the longest x1 178 us: on_device(): lax.psum_scatter(jnp.einsum('tc,pte->cpe', columns, grads, preferred_elem...]
    pallas_call x0 -> x6, Pallas kernels: none -> 336 us  [the longest x5 326 us: exchange(): pl.pallas_call(functools.partial(exchange_kernel, tuple(plans)), out_shap...]
    all_gather x5 -> x0, waiting for transfers between devices: 132 us -> none  [the longest x1 38.1 us: on_device(): whole = lax.all_gather(inputs, 'head', axis=1, tiled=True)]
    dynamic_slice x14 -> x1, local copies, waits for them, and re-layouts: 13 us -> 1.62 us  [on_device(): cot_own = lax.dynamic_slice_in_dim(cotangent, group_pos * half, half, 0)]
    psum x1 -> x0, blocking collectives: 10.6 us -> none  [on_device(): lax.psum((jnp.sum(scaled, axis=-1), jnp.sum(scaled * nhat_dev, axis=-1)),...]
    ppermute x2 -> x3, waiting for transfers between devices: 9.37 us -> 0.01 us  [from_partner(): return lax.ppermute(block, axis, route)]
    dot_general x37 -> x30, matrix products: 79.1 us -> 71.7 us  [dot(): lax.dot_general(a, b, (dims, ((), ())), preferred_element_type=jnp.float32)]
  transfers between devices with their start and end apart: 15 -> 3, of which waited for: 14 -> 0; matrix products, arithmetic and copies ran while one was open for 7% -> 12% of each run, Pallas kernels for 0% -> 14%
where the time goes in v1:
time: 486 us; the launch traced here: 484 us
  Pallas kernels  336 us (69%)
  matrix products  71.7 us (15%)
  other arithmetic  38.7 us (8%)
  local copies, waits for them, and re-layouts  31.7 us (7%)
    pallas_call x5, Pallas kernels, exchange(): pl.pallas_call(functools.partial(exchange_kernel, tuple(plans)), out_shap...  326 us
    dot_general x30, matrix products, dot(): lax.dot_general(a, b, (dims, ((), ())), preferred_element_type=jnp.float32)  71.7 us
    pallas_call x1, Pallas kernels, attention(): pl.pallas_call(attention_kernel, grid=(width // HD,), out_shape=[small, s...  10.4 us
  transfers between devices with their start and end apart: 3, of which 0 were waited for; matrix products, arithmetic and copies ran while one was open for 12% of the time, Pallas kernels for 14%

profile of v1, /device:TPU:0, one launch (start us, length us, event | category | flops | bytes accessed | tf_op | source)
XLA Modules:
  0.0 484.2 jit_solution(15224848042379803489)
XLA Ops:
  0.6 1.6 constant_dynamic-slice_fusion.refs_0_
  2.3 2.1 fusion.86.refs_1_
  4.4 48.7 %gather_inputs.1 = (bf16[4,128,768]{2,1,0:T(8,128)(2,1)}, bf16[4,256,768]{2,1,0:T(8,128)(2,1)}) custom-call(bf16[128,768]{1,0:T(8,128)(2,1)} %constant_dynamic-slice_fusion.refs_0_, bf16[256,768]{1,0:T(8,128)(2,1)} %fusion.86.refs_1_), custom_call_target="tpu_custom_call" | custom-call | tf_op jit(solution)/shard_map/gather_inputs/pallas_call | solution.py:130
  53.1 2.3 copy.17
  55.4 1.5 collective-permute-start.1
  56.9 4.1 convolution_convert_fusion.4
  61.8 3.3 convert_bitcast_fusion
  67.1 1.2 slice_reduce_fusion
  69.8 5.1 %fusion.25.refs_1_ = bf16[256,768]{1,0:T(8,128)(2,1)} fusion(bf16[256,3072]{0,1:T(8,128)(2,1)S(1)} %bitcast.234, bf16[1,3,3072,768]{3,2,1,0:T(8,128)(2,1)} %param.12), kind=kOutput, calls=%fused_computation.50 | convolution fusion | flops 1208156160 | bytes 6684672 | tf_op jit(solution)/shard_map/dot_general | solution.py:198
  74.9 4.7 fusion.28.refs_2_
  80.0 3.5 broadcast_multiply_fusion
  83.5 3.9 fusion.22.q_ref
  88.0 2.4 copy.20
  90.3 2.4 copy.21
  93.3 2.5 fusion.17.refs_4_
  95.9 2.3 copy.19
  98.8 1.3 add_reduce_fusion
  100.1 1.4 fusion.100
  101.5 1.8 multiply_convert_fusion.2.refs_0_
  103.4 69.3 %gather_keys.1 = (bf16[4,256,768]{2,1,0:T(8,128)(2,1)}, bf16[4,256,768]{2,1,0:T(8,128)(2,1)}, bf16[4,256,768]{2,1,0:T(8,128)(2,1)}, bf16[8,128,384]{2,1,0:T(8,128)(2,1)}, bf16[4,256,384]{2,1,0:T(8,128)(2,1)}) custom-call(bf16[256,768]{1,0:T(8,128)(2,1)} %multiply_convert_fusion.2.refs_0_, bf16[256,768]{1,0:T(8,128)(2,1)} %fusion.25.refs_1_, ...), custom_call_target="tpu_custom_call" | custom-call | tf_op jit(solution)/shard_map/gather_keys/pallas_call | solution.py:130
  172.6 1.7 copy.24
  175.2 2.2 copy.30
  177.5 2.3 copy.22
  179.7 3.0 fusion.18
  182.7 1.7 copy.23
  184.4 3.9 fusion.31.g_ref
  188.4 10.4 %attention.1 = (bf16[256,768]{1,0:T(8,128)(2,1)S(1)}, bf16[256,768]{1,0:T(8,128)(2,1)S(1)}, bf16[4,256,768]{2,1,0:T(8,128)(2,1)S(1)}, bf16[4,256,768]{2,1,0:T(8,128)(2,1)}) custom-call(bf16[256,768]{1,0:T(8,128)(2,1)S(1)} %fusion.22.q_ref, bf16[4,256,768]{2,1,0:T(8,128)(2,1)} %get-tuple-element.32.k_ref, bf16[4,256,768]{2,1,0:T(8,128)(2,1)} %get-tuple-element.33.v_ref, ...), custom_call_target="tpu_custom_call" | custom-call | tf_op jit(solution)/shard_map/attention/pallas_call | solution.py:176
  198.8 2.5 fusion.34
  201.3 1.8 fusion.35
  203.1 1.3 fusion.36
  204.3 1.3 fusion.37
  205.6 2.7 fusion.41
  208.3 2.7 fusion.39
  210.9 2.7 fusion.38
  213.6 2.7 fusion.40
  216.3 2.3 copy.25
  218.6 2.8 fusion.20.refs_4_
  221.5 1.4 pad_maximum_fusion.1.refs_0_
  222.9 90.4 %sum_branch.1 = (bf16[4,256,768]{2,1,0:T(8,128)(2,1)}, bf16[4,256,768]{2,1,0:T(8,128)(2,1)}, bf16[4,256,768]{2,1,0:T(8,128)(2,1)}, bf16[4,256,768]{2,1,0:T(8,128)(2,1)}, bf16[4,256,384]{2,1,0:T(8,128)(2,1)}) custom-call(bf16[4,256,768]{2,1,0:T(8,128)(2,1)} %pad_maximum_fusion.1.refs_0_, bf16[4,256,768]{2,1,0:T(8,128)(2,1)} %copy-done, ...), custom_call_target="tpu_custom_call" | custom-call | tf_op jit(solution)/shard_map/sum_branch/pallas_call | solution.py:130
  313.3 1.9 reduce_sum.162
  315.7 1.9 convolution_add_fusion.7
  317.6 1.8 convolution_add_fusion.3
  319.5 1.8 convolution_add_fusion.1
  321.3 1.8 convolution_add_fusion.2
  323.1 1.9 convolution_add_fusion
  324.9 1.8 convolution_add_fusion.5
  326.7 1.9 convolution_add_fusion.4
  330.5 3.4 fusion.84
  334.6 1.1 pad_maximum_fusion.3.refs_3_
  335.7 1.3 pad_maximum_fusion.2.refs_0_
  337.0 63.9 %sum_norm.1 = (bf16[4,256,768]{2,1,0:T(8,128)(2,1)}, f32[4,2,256]{2,1,0:T(2,128)}, bf16[4,256,768]{2,1,0:T(8,128)(2,1)}, bf16[1,3,256,768]{3,2,1,0:T(8,128)(2,1)}, bf16[1,128,768]{2,1,0:T(8,128)(2,1)}) custom-call(bf16[4,256,768]{2,1,0:T(8,128)(2,1)} %pad_maximum_fusion.2.refs_0_, f32[2,256]{1,0:T(2,128)} %pad_maximum_fusion.6.refs_1_, ...), custom_call_target="tpu_custom_call" | custom-call | tf_op jit(solution)/shard_map/sum_norm/pallas_call | solution.py:130
  401.0 2.7 fusion.73
  403.7 2.5 fusion.76
  406.2 2.6 fusion.79
  408.8 2.5 fusion.70
  412.4 1.6 multiply_add_fusion
  414.6 1.0 pad_maximum_fusion.4.refs_0_
  415.6 53.7 %sum_hint.1 = (bf16[4,128,768]{2,1,0:T(8,128)(2,1)}, bf16[2,128,768]{2,1,0:T(8,128)(2,1)}, bf16[4,3,256,768]{3,2,1,0:T(8,128)(2,1)}) custom-call(bf16[4,128,768]{2,1,0:T(8,128)(2,1)} %pad_maximum_fusion.4.refs_0_, bf16[128,768]{1,0:T(8,128)(2,1)} %dynamic-slice_convert_fusion.refs_1_, bf16[3,256,768]{2,1,0:T(8,128)(2,1)} %bitcast.238), custom_call_target="tpu_custom_call" | custom-call | tf_op jit(solution)/shard_map/sum_hint/pallas_call | solution.py:130
  469.4 2.7 fusion.107
  475.1 1.6 collective-permute-start.2
  476.7 1.8 fusion.109
  478.6 1.8 convolution_bitcast_fusion
  480.4 0.9 fusion.88
  481.3 2.0 pad_maximum_fusion
  (139 shorter events, 15.1 us)
Async XLA Ops:
  55.4 6.1 %copy-start.2 = (bf16[4,256,768]{2,1,0:T(8,128)(2,1)S(1)}, bf16[4,256,768]{2,1,0:T(8,128)(2,1)}, u32[]{:S(2)}) copy-start(bf16[4,256,768]{2,1,0:T(8,128)(2,1)} %get-tuple-element.30) | copy-start | bytes 4718596
  55.4 122.1 %collective-permute-start.1 = (bf16[128,3072]{0,1:T(8,128)(2,1)}, bf16[128,3072]{0,1:T(8,128)(2,1)}, u32[]{:S(2)}, u32[]{:S(2)}) collective-permute-start(bf16[128,3072]{0,1:T(8,128)(2,1)} %bitcast.6), channel_id=1, source_target_pairs={{0,16},{16,0},{1,17},{17,1},{2,18},{18,2},{3,19},{19,3},{4,20},{20... | collective-permute-start | bytes 2359304 | tf_op jit(solution)/shard_map/ppermute | solution.py:194
  61.0 40.5 %collective-permute-start = (bf16[128,768]{1,0:T(8,128)(2,1)}, bf16[128,768]{1,0:T(8,128)(2,1)}, u32[]{:S(2)}, u32[]{:S(2)}) collective-permute-start(bf16[128,768]{1,0:T(8,128)(2,1)} %convolution_convert_fusion.4), channel_id=1, source_target_pairs={{0,16},{16,0},{1,17},{17,1},{2,18},{18,2},{3,19},{19,3},{4,20},{20... | collective-permute-start | bytes 589832 | tf_op jit(solution)/shard_map/ppermute | solution.py:194
  65.1 1.3 copy-start.28
  65.1 14.9 %copy-start.41 = (f32[256]{0:T(256)}, f32[256]{0:T(256)S(1)}, u32[]{:S(2)}) copy-start(f32[256]{0:T(256)S(1)} %broadcast_multiply_fusion.2) | copy-start | bytes 3076
  65.7 27.7 %copy-start.39 = (f32[256]{0:T(256)}, f32[256]{0:T(256)S(1)}, u32[]{:S(2)}) copy-start(f32[256]{0:T(256)S(1)} %add_rsqrt_fusion) | copy-start | bytes 3076
  66.5 0.6 copy-start.34
  69.8 5.1 %copy-start.20 = (bf16[256,4,768]{0,2,1:T(8,128)(2,1)}, bf16[256,4,768]{0,2,1:T(8,128)(2,1)S(1)}, u32[]{:S(2)}) copy-start(bf16[256,4,768]{0,2,1:T(8,128)(2,1)S(1)} %copy.16) | copy-start | bytes 4718596
  74.9 4.7 copy-start.4
  80.0 3.5 copy-start.21
  83.5 4.5 copy-start.3
  90.3 2.4 copy-start.38
  95.9 2.3 copy-start.36
  95.9 2.3 copy-start.37
  175.2 4.5 copy-start.7
  184.4 18.6 %slice-start = ((s8[4718592]{0:T(1024)(128)(4,1)}), s8[4194304]{0:T(1024)(128)(4,1)S(1)}, s32[]{:S(2)}) async-start(s8[4718592]{0:T(1024)(128)(4,1)} %bitcast.248), calls=%async_computation | async-start | bytes 8388608
  188.4 14.7 %slice-start.1 = ((s8[4718592]{0:T(1024)(128)(4,1)}), s8[524288]{0:T(1024)(128)(4,1)S(1)}, s32[]{:S(2)}) async-start(s8[4718592]{0:T(1024)(128)(4,1)} %bitcast.248), calls=%async_computation.1 | async-start | bytes 1048576
  198.8 4.3 copy-start
  198.8 5.6 %copy-start.1 = (bf16[256,768]{1,0:T(8,128)(2,1)}, bf16[256,768]{1,0:T(8,128)(2,1)S(1)}, u32[]{:S(2)}) copy-start(bf16[256,768]{1,0:T(8,128)(2,1)S(1)} %get-tuple-element.36.refs_3_) | copy-start | bytes 1179652
  213.6 5.1 %copy-start.6 = (bf16[128,8,384]{2,0,1:T(8,128)(2,1)S(1)}, bf16[128,8,384]{2,0,1:T(8,128)(2,1)}, u32[]{:S(2)}) copy-start(bf16[128,8,384]{2,0,1:T(8,128)(2,1)} %copy.19) | copy-start | bytes 2359300
  218.6 2.8 copy-start.26
  218.6 2.8 copy-start.27
  313.3 2.0 copy-start.22
  313.3 2.4 copy-start.15
  315.7 1.9 copy-start.14
  317.6 1.9 copy-start.13
  323.1 1.9 copy-start.12
  326.7 1.9 copy-start.18
  328.7 1.0 copy-start.8
  329.7 0.9 copy-start.42
  329.7 0.9 copy-start.43
  329.7 0.9 copy-start.44
  329.7 0.9 copy-start.45
  329.8 4.2 copy-start.9
  401.0 2.7 copy-start.17
  406.2 5.1 %copy-start.19 = (bf16[4,256,768]{2,1,0:T(8,128)(2,1)S(1)}, bf16[4,256,768]{2,1,0:T(8,128)(2,1)}, u32[]{:S(2)}) copy-start(bf16[4,256,768]{2,1,0:T(8,128)(2,1)} %get-tuple-element.44) | copy-start | bytes 4718596
  411.3 0.7 copy-start.47
  411.3 1.0 copy-start.23
  411.3 1.0 copy-start.40
  411.3 1.0 copy-start.46
  412.3 2.3 copy-start.30
  412.3 2.3 copy-start.31
  412.3 2.3 copy-start.32
  412.3 2.3 copy-start.33
  469.4 2.8 copy-start.5
  473.8 1.1 copy-start.25
  473.8 1.2 copy-start.10
  473.8 1.3 copy-start.29
  474.6 2.1 copy-start.11
  475.1 8.2 %collective-permute-start.2 = (bf16[128,768]{1,0:T(8,128)(2,1)S(1)}, bf16[128,768]{1,0:T(8,128)(2,1)S(1)}, u32[]{:S(2)}, u32[]{:S(2)}) collective-permute-start(bf16[128,768]{1,0:T(8,128)(2,1)S(1)} %add_convert_fusion.3), channel_id=1, source_target_pairs={{0,16},{16,0},{1,17},{17,1},{2,18},{18,2},{3,19},{19,3},{4,20},{20... | collective-permute-start | bytes 589832 | tf_op jit(solution)/shard_map/ppermute | solution.py:194
  476.7 1.8 copy-start.16
  476.7 1.8 copy-start.24
  478.6 1.8 copy-start.35

commit v2 on v1

v2 whole, which is shorter than its diff:
```python
import functools

import jax
import jax.numpy as jnp
from jax import lax
from jax.experimental import pallas as pl
from jax.experimental.pallas import tpu as pltpu
from jax.sharding import PartitionSpec as P

HD = 128


EPS = 1e-06

MESH = pl.DeviceIdType.MESH


def greet(peers):
    barrier = pltpu.get_barrier_semaphore()
    for peer in peers:
        pl.semaphore_signal(barrier, inc=1, device_id={"head": peer}, device_id_type=MESH)
    pl.semaphore_wait(barrier, len(peers))


def others(me, n):
    return [lax.rem(me + step, n) for step in range(1, n)]


def line_gather_kernel(n, sources, *refs):
    count = len(sources)
    ins, outs, sems = refs[:count], refs[count : 2 * count], refs[2 * count :]
    me = lax.axis_index("head")
    greet(others(me, n))
    group = lax.axis_index("group")

    def copy_of(number, block, way):
        x, out = ins[number], outs[number]
        send, recv = sems[3 * number : 3 * number + 2]
        side = 0 if way > 0 else 1
        return pltpu.make_async_remote_copy(
            src_ref=out.at[block],
            dst_ref=out.at[block],
            send_sem=send.at[side, block],
            recv_sem=recv.at[side, block],
            device_id={"head": me + way},
            device_id_type=MESH,
        )

    def own_copy(number, way):
        x, out = ins[number], outs[number]
        send, recv = sems[3 * number : 3 * number + 2]
        side = 0 if way > 0 else 1
        return pltpu.make_async_remote_copy(
            src_ref=x,
            dst_ref=out.at[me],
            send_sem=send.at[side, me],
            recv_sem=recv.at[side, me],
            device_id={"head": me + way},
            device_id_type=MESH,
        )

    def active(number, work):
        source = sources[number]
        if source is None:
            work()
        else:
            pl.when(group == source)(work)

    def local_copy(number):
        return pltpu.make_async_copy(ins[number], outs[number].at[me], sems[3 * number + 2])

    def begin(number):
        pl.when(me < n - 1)(lambda: own_copy(number, 1).start())
        pl.when(me > 0)(lambda: own_copy(number, -1).start())
        local_copy(number).start()

    def hop(number, distance):
        @pl.when(me >= distance)
        def _():
            copy = copy_of(number, me - distance, 1)
            copy.wait_recv()
            pl.when(me < n - 1)(copy.start)

        @pl.when(me + distance < n)
        def _():
            copy = copy_of(number, me + distance, -1)
            copy.wait_recv()
            pl.when(me > 0)(copy.start)

    def finish(number):
        for distance in range(n):
            @pl.when((me >= distance) & (me < n - 1))
            def _():
                copy_of(number, me - distance, 1).wait_send()

            @pl.when((me + distance < n) & (me > 0))
            def _():
                copy_of(number, me + distance, -1).wait_send()
        local_copy(number).wait()

    for number in range(count):
        active(number, functools.partial(begin, number))
    for distance in range(1, n):
        for number in range(count):
            active(number, functools.partial(hop, number, distance))
    for number in range(count):
        active(number, functools.partial(finish, number))


def line_gather(number, name, *wants):
    n = lax.axis_size("head")
    scratch = []
    for x, source in wants:
        scratch += [
            pltpu.SemaphoreType.DMA((2, n)),
            pltpu.SemaphoreType.DMA((2, n)),
            pltpu.SemaphoreType.DMA,
        ]
    arrays = [x for x, source in wants]
    sent = sum(x.size * x.dtype.itemsize for x in arrays)
    return pl.pallas_call(
        functools.partial(line_gather_kernel, n, tuple(source for x, source in wants)),
        out_shape=[jax.ShapeDtypeStruct((n,) + x.shape, x.dtype) for x in arrays],
        in_specs=[pl.BlockSpec(memory_space=pl.ANY)] * len(arrays),
        out_specs=[pl.BlockSpec(memory_space=pl.ANY)] * len(arrays),
        scratch_shapes=scratch,
        compiler_params=pltpu.CompilerParams(collective_id=number, has_side_effects=True),
        cost_estimate=pl.CostEstimate(flops=0, bytes_accessed=200 * sent, transcendentals=0),
        name=name,
    )(*arrays)


def line_sum_kernel(n, small, *refs):
    if small:
        x, extra, total, extras, *scratch = refs
        extra_send, extra_recv, extra_local = scratch[-3:]
    else:
        x, total, *scratch = refs
    sends, recvs, send, recv = scratch[:4]
    me = lax.axis_index("head")
    greet(others(me, n))
    f32 = jnp.float32

    def extra_copy(step):
        return pltpu.make_async_remote_copy(
            src_ref=extra,
            dst_ref=extras.at[me],
            send_sem=extra_send.at[step],
            recv_sem=extra_recv.at[step],
            device_id={"head": lax.rem(me + step, n)},
            device_id_type=MESH,
        )

    if small:
        for step in range(1, n):
            extra_copy(step).start()
        extra_own = pltpu.make_async_copy(extra, extras.at[me], extra_local)
        extra_own.start()

    def copy_of(side, block):
        return pltpu.make_async_remote_copy(
            src_ref=sends.at[side, block],
            dst_ref=recvs.at[side, block],
            send_sem=send.at[side, block],
            recv_sem=recv.at[side, block],
            device_id={"head": me + (1 if side == 0 else -1)},
            device_id_type=MESH,
        )

    def pass_on(side, block, inner):
        copy = copy_of(side, block)

        @pl.when(inner)
        def _():
            copy.wait_recv()
            sends[side, block] = (
                x[block].astype(f32) + recvs[side, block].astype(f32)
            ).astype(sends.dtype)

        @pl.when(jnp.logical_not(inner))
        def _():
            sends[side, block] = x[block]

        copy.start()

    for step in range(n - 1):
        high, low = n - 1 - step, step
        pl.when(me < high)(lambda: pass_on(0, high, me > 0))
        pl.when(me > low)(lambda: pass_on(1, low, me < n - 1))

    total[...] = x[me].astype(f32)

    @pl.when(me > 0)
    def _():
        copy_of(0, me).wait_recv()
        total[...] += recvs[0, me].astype(f32)

    @pl.when(me < n - 1)
    def _():
        copy_of(1, me).wait_recv()
        total[...] += recvs[1, me].astype(f32)

    for step in range(n - 1):
        high, low = n - 1 - step, step
        pl.when(me < high)(lambda: copy_of(0, high).wait_send())
        pl.when(me > low)(lambda: copy_of(1, low).wait_send())
    if small:
        for step in range(1, n):
            origin = lax.rem(me + n - step, n)
            extra_copy(step).wait_send()
            pltpu.make_async_remote_copy(
                src_ref=extra,
                dst_ref=extras.at[origin],
                send_sem=extra_send.at[step],
                recv_sem=extra_recv.at[step],
                device_id={"head": origin},
                device_id_type=MESH,
            ).wait_recv()
        extra_own.wait()


def line_sum(number, name, x, extra=None):
    n, block = x.shape[0], x.shape[1:]
    small = extra is not None
    arrays = [x, extra] if small else [x]
    shapes = [jax.ShapeDtypeStruct(block, jnp.float32)]
    scratch = [
        pltpu.VMEM((2,) + x.shape, x.dtype),
        pltpu.VMEM((2,) + x.shape, x.dtype),
        pltpu.SemaphoreType.DMA((2, n)),
        pltpu.SemaphoreType.DMA((2, n)),
    ]
    if small:
        shapes.append(jax.ShapeDtypeStruct((n,) + extra.shape, extra.dtype))
        scratch += [
            pltpu.SemaphoreType.DMA((n,)),
            pltpu.SemaphoreType.DMA((n,)),
            pltpu.SemaphoreType.DMA,
        ]
    return pl.pallas_call(
        functools.partial(line_sum_kernel, n, small),
        out_shape=shapes,
        in_specs=[pl.BlockSpec(memory_space=pltpu.VMEM)] * len(arrays),
        out_specs=[pl.BlockSpec(memory_space=pltpu.VMEM)] * len(shapes),
        scratch_shapes=scratch,
        compiler_params=pltpu.CompilerParams(
            collective_id=number, has_side_effects=True, vmem_limit_bytes=40 * 1024 * 1024
        ),
        cost_estimate=pl.CostEstimate(
            flops=0, bytes_accessed=50 * x.size * x.dtype.itemsize, transcendentals=0
        ),
        name=name,
    )(*arrays)


def attention_kernel(q_ref, k_ref, v_ref, g_ref, o_ref, dq_ref, dk_ref, dv_ref):
    scaling = HD ** (-0.5)
    query, cot = q_ref[...], g_ref[...]
    keys = k_ref[...].reshape(-1, HD)
    values = v_ref[...].reshape(-1, HD)
    last = (((1,), (1,)), ((), ()))
    first = (((0,), (0,)), ((), ()))
    scores = lax.dot_general(query, keys, last, preferred_element_type=jnp.float32) * scaling
    top = jnp.max(scores, axis=-1, keepdims=True)
    weights = jnp.exp(scores - top)
    inverse = 1.0 / jnp.sum(weights, axis=-1, keepdims=True)
    out = jnp.dot(weights.astype(jnp.bfloat16), values, preferred_element_type=jnp.float32)
    out = (out * inverse).astype(jnp.bfloat16)
    o_ref[...] = out
    dsum = jnp.sum(cot.astype(jnp.float32) * out.astype(jnp.float32), axis=-1, keepdims=True)
    probs = weights * inverse
    dprobs = lax.dot_general(cot, values, last, preferred_element_type=jnp.float32)
    dscores = (probs * (dprobs - dsum)).astype(jnp.bfloat16)
    dquery = jnp.dot(dscores, keys, preferred_element_type=jnp.float32) * scaling
    dq_ref[...] = dquery.astype(jnp.bfloat16)
    dkey = lax.dot_general(dscores, query, first, preferred_element_type=jnp.float32) * scaling
    dk_ref[...] = dkey.astype(jnp.bfloat16).reshape(dk_ref.shape)
    dval = lax.dot_general(
        probs.astype(jnp.bfloat16), cot, first, preferred_element_type=jnp.float32
    )
    dv_ref[...] = dval.astype(jnp.bfloat16).reshape(dv_ref.shape)


def attention(query, keys, values, cot):
    tok, width = query.shape
    rows = keys.shape[0]
    own = pl.BlockSpec((tok, HD), lambda h: (0, h))
    every = pl.BlockSpec((rows, tok, HD), lambda h: (0, 0, h))
    small = jax.ShapeDtypeStruct((tok, width), jnp.bfloat16)
    large = jax.ShapeDtypeStruct((rows, tok, width), jnp.bfloat16)
    return pl.pallas_call(
        attention_kernel,
        grid=(width // HD,),
        out_shape=[small, small, large, large],
        in_specs=[own, every, every, own],
        out_specs=[own, own, every, every],
        compiler_params=pltpu.CompilerParams(vmem_limit_bytes=50 * 1024 * 1024),
        name="attention",
    )(query, keys, values, cot)


def dot(a, b, dims):
    return lax.dot_general(a, b, (dims, ((), ())), preferred_element_type=jnp.float32)


def row_bits():
    bits, bit = [], lax.axis_size("row") // 2
    while bit:
        bits.append(bit)
        bit //= 2
    return bits


def row_swap(x, bit):
    return lax.ppermute(x, "row", [(row, row ^ bit) for row in range(lax.axis_size("row"))])


def cube_gather(x, dim):
    for bit in row_bits():
        x = jnp.concatenate([x, row_swap(x, bit)], axis=dim)
    return x


def cube_deal(x):
    row = lax.axis_index("row")
    for bit in row_bits():
        cols = x.shape[1] // 2
        upper = (row // bit) % 2 == 1
        low, high = x[:, :cols], x[:, cols:]
        kept, sent = jnp.where(upper, high, low), jnp.where(upper, low, high)
        x = jnp.concatenate([kept, row_swap(sent, bit)], axis=0)
    return x


def on_device(latent, hint, timestep, modulation, qkv_weight, out_weight, zero_weight, cotangent):
    f32, bf16 = jnp.float32, jnp.bfloat16
    tok, width = latent.shape
    half = tok // 2
    n_head, n_row = lax.axis_size("head"), lax.axis_size("row")
    full_width = n_head * width
    group_pos = lax.axis_index("group")
    control = group_pos == 0
    head_pos = lax.axis_index("head")
    steps_count = modulation.shape[1]
    pick = (lax.broadcasted_iota(jnp.int32, (steps_count,), 0) == timestep[0]).astype(f32)
    mods = jnp.sum(modulation[0] * pick[:, None, None], axis=0)
    shift, scale, gate = (mods[0], mods[1], mods[2])
    gate_dev = lax.dynamic_slice_in_dim(gate, head_pos * width, width, 0)
    scale_dev = lax.dynamic_slice_in_dim(scale, head_pos * width, width, 0)
    w_qkv, w_out = qkv_weight[0], out_weight[0]

    def widen(blocks):
        return jnp.concatenate([blocks[index] for index in range(n_head)], axis=1)

    def swap(x):
        return lax.ppermute(x, "group", [(0, 1), (1, 0)])

    def near(x):
        return jnp.where(control, x, lax.ppermute(x, "group", [(0, 1)]))

    def near_cols(x):
        cols = x.shape[1] // 2
        return jnp.where(control, x[:, :cols], lax.ppermute(x[:, cols:], "group", [(0, 1)]))

    def head_terms(x, weight):
        return jnp.stack(
            [
                dot(x, weight[index * width : (index + 1) * width], ((1,), (1,))).astype(bf16)
                for index in range(n_head)
            ]
        )

    summed = (latent.astype(f32) + hint.astype(f32)).astype(bf16)
    inputs = jnp.where(control, summed, latent)
    cot_own = jnp.where(control, cotangent[:half], cotangent[half:])
    cot_half, whole = line_gather(0, "gather_inputs", (cot_own, None), (inputs, None))
    cot_half = widen(cot_half)
    hint_half = dot(cot_half, zero_weight, ((1,), (0,))).astype(bf16)
    hint_other = swap(hint_half)
    cot_other = swap(cot_half)

    whole_f = widen(whole).astype(f32)
    mean = jnp.mean(whole_f, axis=-1, keepdims=True)
    centred = whole_f - mean
    var = jnp.mean(centred * centred, axis=-1, keepdims=True)
    rstd = lax.rsqrt(var + EPS)
    nhat = centred * rstd
    normed = (nhat * (1.0 + scale) + shift).astype(bf16)
    keys, values, query = [
        dot(normed, w_qkv[index], ((1,), (0,))).astype(bf16) for index in (1, 2, 0)
    ]
    all_keys = cube_gather(keys[None], 0)
    all_values = cube_gather(values[None], 0)

    hint_back = jnp.concatenate([hint_half, hint_other])
    incoming = jnp.where(control, hint_back, cotangent)
    gated = (gate_dev * hint_back.astype(f32)).astype(bf16)
    (gated_blocks,) = line_gather(1, "gather_gated", (gated, 0))
    cot_full = jnp.where(
        control,
        jnp.concatenate([cot_half, cot_other]),
        jnp.concatenate([cot_other, cot_half]),
    )
    gated_main = (gate * cot_full.astype(f32)).astype(bf16)
    gated_full = jnp.where(control, widen(gated_blocks), gated_main)
    attn_grad = dot(gated_full, w_out, ((1,), (0,))).astype(bf16)
    attn, dquery, key_terms, value_terms = attention(query, all_keys, all_values, attn_grad)

    bits = row_bits()

    def row_sum(x):
        blocks = [x[index] for index in range(n_row)]
        for bit in bits[::-1]:
            count = len(blocks) // 2
            other = row_swap(jnp.stack(blocks[count:]), bit)
            blocks = [
                (blocks[index].astype(f32) + other[index].astype(f32)).astype(bf16)
                for index in range(count)
            ]
        return blocks[0]

    dkey, dval = row_sum(key_terms), row_sum(value_terms)
    (branch,) = line_sum(2, "sum_branch", head_terms(attn, w_out))
    state = (inputs.astype(f32) + gate_dev * branch).astype(bf16)
    grads = [dquery, dkey, dval]

    scaled_nhat = nhat * (1.0 + scale)
    terms = []
    first, second = 0.0, 0.0
    for index in range(n_head):
        cols = slice(index * width, (index + 1) * width)
        term = sum(dot(grads[c], w_qkv[c, cols], ((1,), (1,))) for c in range(3))
        first = first + jnp.sum(term * (1.0 + scale[cols]), axis=-1)
        second = second + jnp.sum(term * scaled_nhat[:, cols], axis=-1)
        terms.append(term.astype(bf16))
    sums = jnp.concatenate([first[None], second[None], jnp.zeros((6, tok), f32)])
    dnorm, sum_parts = line_sum(3, "sum_norm", jnp.stack(terms), sums)
    sums = jnp.sum(sum_parts, axis=0) / full_width
    nhat_dev = lax.dynamic_slice_in_dim(nhat, head_pos * width, width, 1)
    scaled = dnorm * (1.0 + scale_dev)
    d_in = incoming.astype(f32) + rstd * (
        scaled - sums[0][:, None] - nhat_dev * sums[1][:, None]
    )
    own_half = jnp.where(control, d_in[:half], d_in[half:])
    sent_half = jnp.where(control, d_in[half:], d_in[:half])
    other_half = swap(sent_half.astype(bf16)).astype(f32)
    latent_grad = (own_half + other_half)[None, None]
    hint_grad = jnp.where(control, own_half, other_half)[None, None]

    near_state = near(state)
    state_half = jnp.where(control, near_state[:half], near_state[half:])
    (projected,) = line_sum(4, "sum_hint", head_terms(state_half, zero_weight))
    main_state = lax.ppermute(state[:half], "group", [(1, 0)])
    main_half = jnp.where(control, main_state, state[half:])
    mixed_half = (main_half.astype(f32) + projected).astype(bf16)
    mixed_other = swap(mixed_half)
    mixed = jnp.where(
        control,
        jnp.concatenate([mixed_half, mixed_other]),
        jnp.concatenate([mixed_other, mixed_half]),
    )

    tokens = ((0,), (0,))
    normed_cols = cube_deal(near_cols(normed))
    qkv_grad = jnp.stack(
        [dot(normed_cols, cube_gather(near(grads[c]), 0), tokens) for c in range(3)], axis=1
    )
    out_grad = dot(cube_deal(near_cols(gated_full)), cube_gather(near(attn), 0), tokens)
    cot_cols = jnp.where(
        control, cot_full[:, : full_width // 2], cot_full[:, full_width // 2 :]
    )
    zero_grad = dot(cube_deal(cot_cols), cube_gather(near_state, 0), tokens)
    return (mixed, latent_grad, hint_grad, qkv_grad, out_grad, zero_grad)


def solution(mesh):
    placed = (
        P("row", "head"),
        P("row", "head"),
        P(),
        P("group", None, None, None),
        P("group", None, None, "head"),
        P("group", None, "head"),
        P(None, "head"),
        P("row", "head"),
    )
    return jax.shard_map(
        on_device,
        mesh=mesh,
        in_specs=placed,
        out_specs=(
            P("row", "head"),
            P("row", "group", None, "head"),
            P("row", "group", None, "head"),
            P(("group", "row"), None, "head"),
            P(("group", "row"), "head"),
            P(("group", "row"), "head"),
        ),
        check_vma=False,
    )
```

time: 486 us -> 372 us (0.77)
  Pallas kernels: 336 us -> 183 us
  waiting for transfers between devices: 0.01 us -> 55.7 us
  matrix products: 71.7 us -> 36.3 us
  starting transfers between devices: 3.62 us -> 36.4 us
  local copies, waits for them, and re-layouts: 31.7 us -> 5.49 us
  other arithmetic: 38.7 us -> 51.2 us
    pallas_call x5, Pallas kernels: 326 us -> 173 us  [the longest x3 102 us: line_sum(): pl.pallas_call(functools.partial(line_sum_kernel, n, small), out_shape=sh...]
    ppermute x3 -> x36, waiting for transfers between devices: 0.01 us -> 55.7 us  [the longest x24 35.7 us: row_swap(): lax.ppermute(x, 'row', [(row, row ^ bit) for row in range(lax.axis_size('...]
    dot_general x30, matrix products: 71.7 us -> 36.3 us  [dot(): lax.dot_general(a, b, (dims, ((), ())), preferred_element_type=jnp.float32)]
    ppermute x3 -> x36, starting transfers between devices: 3.62 us -> 36.4 us  [the longest x5 12.3 us: near(): return jnp.where(control, x, lax.ppermute(x, 'group', [(0, 1)]))]
    concatenate x0 -> x11, other arithmetic: none -> 11 us  [the longest x9 9.93 us: cube_gather(): x = jnp.concatenate([x, row_swap(x, bit)], axis=dim)]
    select_n x1, other arithmetic: 2.98 us -> 13.6 us  [on_device(): gated_full = jnp.where(control, widen(gated_blocks), gated_main)]
    select_n x0 -> x16, other arithmetic: none -> 9.61 us  [the longest x6 7.38 us: cube_deal(): kept, sent = (jnp.where(upper, high, low), jnp.where(upper, low, high))]
    convert_element_type x5 -> x0, local copies, waits for them, and re-layouts: 6.49 us -> none  [the longest x3 5.08 us: on_device(): whole_f = widen(whole).astype(f32)]
  transfers between devices with their start and end apart: 3 -> 36, of which waited for: 0 -> 11; matrix products, arithmetic and copies ran while one was open for 12% -> 22% of each run, Pallas kernels for 14% -> 37%
where the time goes in v2:
time: 372 us; the launch traced here: 371 us
  Pallas kernels  183 us (49%)
  waiting for transfers between devices  55.7 us (15%)
  other arithmetic  51.2 us (14%)
  starting transfers between devices  36.4 us (10%)
  matrix products  36.3 us (10%)
  local copies, waits for them, and re-layouts  5.49 us (1%)
    pallas_call x3, Pallas kernels, line_sum(): pl.pallas_call(functools.partial(line_sum_kernel, n, small), out_shape=sh...  102 us
    pallas_call x2, Pallas kernels, line_gather(): pl.pallas_call(functools.partial(line_gather_kernel, n, tuple((source for...  70.5 us
    dot_general x30, matrix products, dot(): lax.dot_general(a, b, (dims, ((), ())), preferred_element_type=jnp.float32)  36.3 us
    ppermute x24, waiting for transfers between devices, row_swap(): lax.ppermute(x, 'row', [(row, row ^ bit) for row in range(lax.axis_size('...  35.7 us
    select_n x1, other arithmetic, on_device(): gated_full = jnp.where(control, widen(gated_blocks), gated_main)  13.6 us
    ppermute x5, starting transfers between devices, near(): return jnp.where(control, x, lax.ppermute(x, 'group', [(0, 1)]))  12.3 us
    ppermute x24, starting transfers between devices, row_swap(): lax.ppermute(x, 'row', [(row, row ^ bit) for row in range(lax.axis_size('...  12.2 us
    pallas_call x1, Pallas kernels, attention(): pl.pallas_call(attention_kernel, grid=(width // HD,), out_shape=[small, s...  10.4 us
  transfers between devices with their start and end apart: 36, of which 11 were waited for; matrix products, arithmetic and copies ran while one was open for 22% of the time, Pallas kernels for 37%

profile of v2, /device:TPU:0, one launch (start us, length us, event | category | flops | bytes accessed | tf_op | source)
XLA Modules:
  0.0 370.6 jit_solution(8315940285874693253)
XLA Ops:
  0.6 1.7 slice_select_fusion.6.refs_0_
  2.4 2.1 fusion.138.refs_1_
  4.5 44.6 %gather_inputs.1 = (bf16[4,128,768]{2,1,0:T(8,128)(2,1)}, bf16[4,256,768]{2,1,0:T(8,128)(2,1)}) custom-call(bf16[128,768]{1,0:T(8,128)(2,1)} %slice_select_fusion.6.refs_0_, bf16[256,768]{1,0:T(8,128)(2,1)} %fusion.138.refs_1_), custom_call_target="tpu_custom_call" | custom-call | bytes 117964800 | tf_op jit(solution)/shard_map/gather_inputs/pallas_call | solution.py:121
  49.1 1.4 slice_bitcast_fusion.35
  50.6 4.0 %convolution_convert_fusion.4 = bf16[128,768]{1,0:T(8,128)(2,1)} fusion(bf16[3072,768]{1,0:T(8,128)(2,1)} %param.14, bf16[128,768]{1,0:T(8,128)(2,1)S(1)} %get-tuple-element.66, bf16[128,768]{1,0:T(8,128)(2,1)S(1)} %get-tuple-element.67, bf16[128,768]{1,0:T(8,128)(2,1)S(1)} %get-tuple-element.68, bf16[128,768]{1,0:T(8,128)(2,1)S(1)} %get-tuple-element.65), kind=kOutput, calls=%fused_computation.122 | convolution fusion | flops 607223808 | bytes 5701632 | tf_op jit(solution)/shard_map/dot_general | solution.py:303
  54.5 1.5 collective-permute-start.4
  56.1 1.0 pad_maximum_fusion.8
  60.0 3.3 add_convert_fusion
  63.4 1.5 fusion.74
  64.8 1.6 collective-permute-start.2
  66.4 1.5 fusion.77
  69.4 4.3 %collective-permute-start.14 = (bf16[256,1536]{1,0:T(8,128)(2,1)}, bf16[256,1536]{1,0:T(8,128)(2,1)}, u32[]{:S(2)}, u32[]{:S(2)}) collective-permute-start(bf16[256,1536]{1,0:T(8,128)(2,1)} %slice.399), channel_id=1, source_target_pairs={{0,16},{1,17},{2,18},{3,19},{4,20},{5,21},{6,22},{7,23},{8,24},{9,... | collective-permute-start | bytes 2359304 | tf_op jit(solution)/shard_map/ppermute | solution.py:363
  73.7 1.4 fusion.58.q_ref
  75.2 1.8 multiply_convert_fusion.1.refs_0_
  77.0 25.9 %gather_gated.1 = bf16[4,256,768]{2,1,0:T(8,128)(2,1)} custom-call(bf16[256,768]{1,0:T(8,128)(2,1)} %multiply_convert_fusion.1.refs_0_), custom_call_target="tpu_custom_call" | custom-call | bytes 78643200 | tf_op jit(solution)/shard_map/gather_gated/pallas_call | solution.py:121
  103.0 1.5 slice_bitcast_fusion.27
  104.4 1.1 pad_maximum_fusion.7
  105.6 1.1 pad_maximum_fusion.6
  107.2 13.6 %fusion.14 = (bf16[256,3072]{1,0:T(8,128)(2,1)S(1)}, bf16[256,3072]{1,0:T(8,128)(2,1)S(1)}) fusion(bf16[256,768]{1,0:T(8,128)(2,1)S(1)} %get-tuple-element.40, bf16[256,768]{1,0:T(8,128)(2,1)S(1)} %get-tuple-element.41, bf16[256,768]{1,0:T(8,128)(2,1)S(1)} %get-tuple-element.42, bf16[256,768]{1,0:T(8,128)(2,1)S(1)} %get-tuple-element.39, ...), kind=kLoop, calls=%fused_computation.19 | loop fusion | flops 25952256 | bytes 6303745 | tf_op jit(solution)/shard_map/jit(_where)/select_n | solution.py:405
  121.9 1.5 collective-permute-start.32
  125.0 1.4 fusion.67.g_ref
  126.4 2.3 pad_maximum_fusion.3.v_ref
  128.7 2.4 pad_maximum_fusion.2.k_ref
  131.1 10.4 %attention.1 = (bf16[256,768]{1,0:T(8,128)(2,1)S(1)}, bf16[256,768]{1,0:T(8,128)(2,1)S(1)}, bf16[4,256,768]{2,1,0:T(8,128)(2,1)S(1)}, bf16[4,256,768]{2,1,0:T(8,128)(2,1)}) custom-call(bf16[256,768]{1,0:T(8,128)(2,1)S(1)} %fusion.58.q_ref, bf16[4,256,768]{2,1,0:T(8,128)(2,1)} %pad_maximum_fusion.2.k_ref, bf16[4,256,768]{2,1,0:T(8,128)(2,1)} %pad_maximum_fusion.3.v_ref, ...), custom_call_target="tpu_custom_call" | custom-call | tf_op jit(solution)/shard_map/attention/pallas_call | solution.py:291
  143.8 39.0 %sum_branch.1 = f32[256,768]{1,0:T(8,128)S(1)} custom-call(bf16[4,256,768]{2,1,0:T(8,128)(2,1)S(1)} %pad_maximum_fusion.4.refs_0_), custom_call_target="tpu_custom_call" | custom-call | bytes 78643200 | tf_op jit(solution)/shard_map/sum_branch/pallas_call | solution.py:240
  182.9 1.3 collective-permute-start.7
  185.8 1.2 slice.405
  187.0 1.3 collective-permute-start.26
  188.4 1.5 collective-permute-start.29
  189.9 2.3 broadcast_select_fusion.7
  192.4 1.3 collective-permute-start.17
  193.7 2.1 broadcast_select_fusion.11
  196.5 2.0 fusion.116
  198.4 1.8 fusion.119
  200.2 8.8 %collective-permute-done.26 = bf16[256,1536]{1,0:T(8,128)(2,1)S(1)} collective-permute-done((bf16[256,1536]{1,0:T(8,128)(2,1)S(1)}, bf16[256,1536]{1,0:T(8,128)(2,1)S(1)}, u32[]{:S(2)}, u32[]{:S(2)}) %collective-permute-start.26) | collective-permute-done | bytes 786464 | tf_op jit(solution)/shard_map/ppermute | solution.py:363
  209.2 2.0 fusion.122
  211.2 2.1 collective-permute-done.29
  213.3 1.3 collective-permute-start.6
  214.6 1.8 fusion.125
  216.6 24.8 %sum_hint.1 = f32[128,768]{1,0:T(8,128)S(1)} custom-call(bf16[4,128,768]{2,1,0:T(8,128)(2,1)S(1)} %pad_maximum_fusion.9.refs_0_), custom_call_target="tpu_custom_call" | custom-call | bytes 39321600 | tf_op jit(solution)/shard_map/sum_hint/pallas_call | solution.py:240
  241.4 1.5 collective-permute-start.34
  243.0 2.9 collective-permute-start.8
  246.0 3.6 collective-permute-done.8
  251.0 2.6 collective-permute-done.34
  253.6 1.4 collective-permute-start.27
  256.7 5.3 %collective-permute-done.30 = bf16[256,768]{1,0:T(8,128)(2,1)S(1)} collective-permute-done((bf16[256,768]{1,0:T(8,128)(2,1)S(1)}, bf16[256,768]{1,0:T(8,128)(2,1)S(1)}, u32[]{:S(2)}, u32[]{:S(2)}) %collective-permute-start.30) | collective-permute-done | bytes 393248 | tf_op jit(solution)/shard_map/ppermute | solution.py:315
  262.0 1.0 pad_maximum_fusion.14
  263.0 6.8 %collective-permute-done.27 = bf16[256,768]{1,0:T(8,128)(2,1)S(1)} collective-permute-done((bf16[256,768]{1,0:T(8,128)(2,1)S(1)}, bf16[256,768]{1,0:T(8,128)(2,1)S(1)}, u32[]{:S(2)}, u32[]{:S(2)}) %collective-permute-start.27) | collective-permute-done | bytes 393248 | tf_op jit(solution)/shard_map/ppermute | solution.py:315
  269.8 1.0 broadcast_select_fusion.9
  271.0 7.3 %collective-permute-done.18 = bf16[256,768]{1,0:T(8,128)(2,1)S(1)} collective-permute-done((bf16[256,768]{1,0:T(8,128)(2,1)S(1)}, bf16[256,768]{1,0:T(8,128)(2,1)S(1)}, u32[]{:S(2)}, u32[]{:S(2)}) %collective-permute-start.18) | collective-permute-done | bytes 393248 | tf_op jit(solution)/shard_map/ppermute | solution.py:315
  278.3 1.0 pad_maximum_fusion.11
  279.3 5.6 %collective-permute-done.10 = bf16[1,256,768]{2,1,0:T(8,128)(2,1)S(1)} collective-permute-done((bf16[1,256,768]{2,1,0:T(8,128)(2,1)S(1)}, bf16[1,256,768]{2,1,0:T(8,128)(2,1)S(1)}, u32[]{:S(2)}, u32[]{:S(2)}) %collective-permute-start.10) | collective-permute-done | bytes 393248 | tf_op jit(solution)/shard_map/ppermute | solution.py:315
  285.0 4.1 %collective-permute-start.20 = (bf16[256,768]{1,0:T(8,128)(2,1)S(1)}, bf16[256,768]{1,0:T(8,128)(2,1)}, u32[]{:S(2)}, u32[]{:S(2)}) collective-permute-start(bf16[256,768]{1,0:T(8,128)(2,1)S(1)} %fusion.141), channel_id=1, source_target_pairs={{0,16},{1,17},{2,18},{3,19},{4,20},{5,21},{6,22},{7,23},{8,24},{9,... | collective-permute-start | bytes 1179656 | tf_op jit(solution)/shard_map/ppermute | solution.py:359
  289.3 4.0 %collective-permute-start.23 = (bf16[256,768]{1,0:T(8,128)(2,1)S(1)}, bf16[256,768]{1,0:T(8,128)(2,1)}, u32[]{:S(2)}, u32[]{:S(2)}) collective-permute-start(bf16[256,768]{1,0:T(8,128)(2,1)S(1)} %fusion.142), channel_id=1, source_target_pairs={{0,16},{1,17},{2,18},{3,19},{4,20},{5,21},{6,22},{7,23},{8,24},{9,... | collective-permute-start | bytes 1179656 | tf_op jit(solution)/shard_map/ppermute | solution.py:359
  298.9 3.0 fusion.130
  302.2 38.4 %sum_norm.1 = (f32[256,768]{1,0:T(8,128)S(1)}, f32[4,8,256]{2,1,0:T(8,128)S(1)}) custom-call(bf16[4,256,768]{2,1,0:T(8,128)(2,1)S(1)} %pad_maximum_fusion.5.refs_0_, f32[8,256]{1,0:T(8,128)S(1)} %maximum_maximum_fusion.refs_1_), custom_call_target="tpu_custom_call" | custom-call | bytes 78643200 | tf_op jit(solution)/shard_map/sum_norm/pallas_call | solution.py:240
  340.9 2.1 collective-permute-start.24
  343.0 1.6 multiply_add_fusion
  344.7 3.8 %collective-permute-done.21 = bf16[256,768]{1,0:T(8,128)(2,1)S(1)} collective-permute-done((bf16[256,768]{1,0:T(8,128)(2,1)S(1)}, bf16[256,768]{1,0:T(8,128)(2,1)S(1)}, u32[]{:S(2)}, u32[]{:S(2)}) %collective-permute-start.21) | collective-permute-done | bytes 393248 | tf_op jit(solution)/shard_map/ppermute | solution.py:315
  348.6 4.2 %collective-permute-done.24 = bf16[256,768]{1,0:T(8,128)(2,1)S(1)} collective-permute-done((bf16[256,768]{1,0:T(8,128)(2,1)S(1)}, bf16[256,768]{1,0:T(8,128)(2,1)S(1)}, u32[]{:S(2)}, u32[]{:S(2)}) %collective-permute-start.24) | collective-permute-done | bytes 393248 | tf_op jit(solution)/shard_map/ppermute | solution.py:315
  353.0 5.4 %collective-permute-done.13 = bf16[128,768]{1,0:T(8,128)(2,1)S(1)} collective-permute-done((bf16[128,768]{1,0:T(8,128)(2,1)S(1)}, bf16[128,768]{1,0:T(8,128)(2,1)S(1)}, u32[]{:S(2)}, u32[]{:S(2)}) %collective-permute-start.13) | collective-permute-done | bytes 196640 | tf_op jit(solution)/shard_map/ppermute | solution.py:356
  359.9 3.2 fusion.39
  363.1 2.9 fusion.33
  368.6 2.0 pad_maximum_fusion
  (188 shorter events, 25.9 us)
Async XLA Ops:
  49.1 14.2 %slice-start = ((s8[14155776]{0:T(1024)(128)(4,1)}), s8[4194304]{0:T(1024)(128)(4,1)S(1)}, s32[]{:S(2)}) async-start(s8[14155776]{0:T(1024)(128)(4,1)} %bitcast.179), calls=%async_computation | async-start | bytes 8388608
  50.5 7.7 %copy-start.22 = (f32[1,8,3,3072]{3,1,2,0:T(8,128)S(1)}, f32[1,8,3,3072]{3,1,2,0:T(8,128)}, u32[]{:S(2)}) copy-start(f32[1,8,3,3072]{3,1,2,0:T(8,128)} %param.11) | copy-start | bytes 884740
  50.5 12.8 %slice-start.1 = ((s8[14155776]{0:T(1024)(128)(4,1)}), s8[4194304]{0:T(1024)(128)(4,1)S(1)}, s32[]{:S(2)}) async-start(s8[14155776]{0:T(1024)(128)(4,1)} %bitcast.179), calls=%async_computation.1 | async-start | bytes 8388608
  54.5 4.5 %copy-start.3 = (bf16[4,256,768]{2,1,0:T(8,128)(2,1)S(1)}, bf16[4,256,768]{2,1,0:T(8,128)(2,1)}, u32[]{:S(2)}) copy-start(bf16[4,256,768]{2,1,0:T(8,128)(2,1)} %get-tuple-element.14) | copy-start | bytes 4718596
  54.5 20.6 %collective-permute-start.4 = (bf16[128,768]{1,0:T(8,128)(2,1)}, bf16[128,768]{1,0:T(8,128)(2,1)}, u32[]{:S(2)}, u32[]{:S(2)}) collective-permute-start(bf16[128,768]{1,0:T(8,128)(2,1)} %convolution_convert_fusion.4), channel_id=1, source_target_pairs={{0,16},{16,0},{1,17},{17,1},{2,18},{18,2},{3,19},{19,3},{4,20},{20... | collective-permute-start | bytes 589832 | tf_op jit(solution)/shard_map/ppermute | solution.py:356
  57.0 50.2 %collective-permute-start.5 = (bf16[128,3072]{1,0:T(8,128)(2,1)}, bf16[128,3072]{1,0:T(8,128)(2,1)}, u32[]{:S(2)}, u32[]{:S(2)}) collective-permute-start(bf16[128,3072]{1,0:T(8,128)(2,1)} %pad_maximum_fusion.8), channel_id=1, source_target_pairs={{0,16},{16,0},{1,17},{17,1},{2,18},{18,2},{3,19},{19,3},{4,20},{20... | collective-permute-start | bytes 2359304 | tf_op jit(solution)/shard_map/ppermute | solution.py:356
  58.4 4.9 %copy-start.23 = (f32[3,3072]{1,0:T(4,128)}, f32[3,3072]{1,0:T(4,128)S(1)}, u32[]{:S(2)}) copy-start(f32[3,3072]{1,0:T(4,128)S(1)} %fusion.146) | copy-start | bytes 110596
  59.0 4.3 %slice-start.2 = ((s8[14155776]{0:T(1024)(128)(4,1)}), s8[4194304]{0:T(1024)(128)(4,1)S(1)}, s32[]{:S(2)}) async-start(s8[14155776]{0:T(1024)(128)(4,1)} %bitcast.179), calls=%async_computation.2 | async-start | bytes 8388608
  60.0 3.3 copy-start.24
  60.0 3.3 slice-start.3
  64.8 39.6 %collective-permute-start.2 = (bf16[1,256,768]{2,1,0:T(8,128)(2,1)S(1)}, bf16[1,256,768]{2,1,0:T(8,128)(2,1)}, u32[]{:S(2)}, u32[]{:S(2)}) collective-permute-start(bf16[1,256,768]{2,1,0:T(8,128)(2,1)S(1)} %fusion.74), channel_id=1, source_target_pairs={{0,8},{4,12},{8,0},{12,4},{1,9},{5,13},{9,1},{13,5},{2,10},{6,14},... | collective-permute-start | bytes 1179656 | tf_op jit(solution)/shard_map/ppermute | solution.py:315
  67.8 37.8 %collective-permute-start = (bf16[1,256,768]{2,1,0:T(8,128)(2,1)S(1)}, bf16[1,256,768]{2,1,0:T(8,128)(2,1)}, u32[]{:S(2)}, u32[]{:S(2)}) collective-permute-start(bf16[1,256,768]{2,1,0:T(8,128)(2,1)S(1)} %fusion.77), channel_id=1, source_target_pairs={{0,8},{4,12},{8,0},{12,4},{1,9},{5,13},{9,1},{13,5},{2,10},{6,14},... | collective-permute-start | bytes 1179656 | tf_op jit(solution)/shard_map/ppermute | solution.py:315
  69.4 54.1 %collective-permute-start.14 = (bf16[256,1536]{1,0:T(8,128)(2,1)}, bf16[256,1536]{1,0:T(8,128)(2,1)}, u32[]{:S(2)}, u32[]{:S(2)}) collective-permute-start(bf16[256,1536]{1,0:T(8,128)(2,1)} %slice.399), channel_id=1, source_target_pairs={{0,16},{1,17},{2,18},{3,19},{4,20},{5,21},{6,22},{7,23},{8,24},{9,... | collective-permute-start | bytes 2359304 | tf_op jit(solution)/shard_map/ppermute | solution.py:363
  105.5 20.9 %collective-permute-start.3 = (bf16[2,256,768]{2,1,0:T(8,128)(2,1)S(1)}, bf16[2,256,768]{2,1,0:T(8,128)(2,1)S(1)}, u32[]{:S(2)}, u32[]{:S(2)}) collective-permute-start(bf16[2,256,768]{2,1,0:T(8,128)(2,1)S(1)} %pad_maximum_fusion.7), channel_id=1, source_target_pairs={{0,4},{4,0},{8,12},{12,8},{1,5},{5,1},{9,13},{13,9},{2,6},{6,2},{1... | collective-permute-start | bytes 2359304 | tf_op jit(solution)/shard_map/ppermute | solution.py:315
  106.7 22.1 %collective-permute-start.1 = (bf16[2,256,768]{2,1,0:T(8,128)(2,1)S(1)}, bf16[2,256,768]{2,1,0:T(8,128)(2,1)S(1)}, u32[]{:S(2)}, u32[]{:S(2)}) collective-permute-start(bf16[2,256,768]{2,1,0:T(8,128)(2,1)S(1)} %pad_maximum_fusion.6), channel_id=1, source_target_pairs={{0,4},{4,0},{8,12},{12,8},{1,5},{5,1},{9,13},{13,9},{2,6},{6,2},{1... | collective-permute-start | bytes 2359304 | tf_op jit(solution)/shard_map/ppermute | solution.py:315
  107.2 17.7 %slice-start.8 = ((s8[4718592]{0:T(1024)(128)(4,1)}), s8[4194304]{0:T(1024)(128)(4,1)S(1)}, s32[]{:S(2)}) async-start(s8[4718592]{0:T(1024)(128)(4,1)} %bitcast.202), calls=%async_computation.8 | async-start | bytes 8388608
  120.9 4.1 %copy-start = (bf16[256,3072]{1,0:T(8,128)(2,1)}, bf16[256,3072]{1,0:T(8,128)(2,1)S(1)}, u32[]{:S(2)}) copy-start(bf16[256,3072]{1,0:T(8,128)(2,1)S(1)} %get-tuple-element.34) | copy-start | bytes 4718596
  120.9 4.1 %slice-start.9 = ((s8[4718592]{0:T(1024)(128)(4,1)}), s8[524288]{0:T(1024)(128)(4,1)S(1)}, s32[]{:S(2)}) async-start(s8[4718592]{0:T(1024)(128)(4,1)} %bitcast.202), calls=%async_computation.9 | async-start | bytes 1048576
  121.9 68.0 %collective-permute-start.32 = (bf16[256,768]{1,0:T(8,128)(2,1)}, bf16[256,768]{1,0:T(8,128)(2,1)}, u32[]{:S(2)}, u32[]{:S(2)}) collective-permute-start(bf16[256,768]{1,0:T(8,128)(2,1)} %get-tuple-element.52), channel_id=1, source_target_pairs={{0,8},{4,12},{8,0},{12,4},{1,9},{5,13},{9,1},{13,5},{2,10},{6,14},... | collective-permute-start | bytes 1179656 | tf_op jit(solution)/shard_map/ppermute | solution.py:315
  124.4 67.9 %collective-permute-start.15 = (bf16[256,768]{1,0:T(8,128)(2,1)}, bf16[256,768]{1,0:T(8,128)(2,1)}, u32[]{:S(2)}, u32[]{:S(2)}) collective-permute-start(bf16[256,768]{1,0:T(8,128)(2,1)} %get-tuple-element.60), channel_id=1, source_target_pairs={{0,8},{4,12},{8,0},{12,4},{1,9},{5,13},{9,1},{13,5},{2,10},{6,14},... | collective-permute-start | bytes 1179656 | tf_op jit(solution)/shard_map/ppermute | solution.py:315
  143.7 39.0 %copy-start.2 = (bf16[256,768]{1,0:T(8,128)(2,1)S(1)}, bf16[256,768]{1,0:T(8,128)(2,1)}, u32[]{:S(2)}) copy-start(bf16[256,768]{1,0:T(8,128)(2,1)} %fusion.138.refs_1_) | copy-start | bytes 1179652
  182.8 7.2 %copy-start.9 = (bf16[256,768]{1,0:T(8,128)(2,1)S(1)}, bf16[256,768]{1,0:T(8,128)(2,1)}, u32[]{:S(2)}) copy-start(bf16[256,768]{1,0:T(8,128)(2,1)} %get-tuple-element.51) | copy-start | bytes 1179652
  182.9 13.0 %collective-permute-start.7 = (bf16[256,768]{1,0:T(8,128)(2,1)S(1)}, bf16[256,768]{1,0:T(8,128)(2,1)S(1)}, u32[]{:S(2)}, u32[]{:S(2)}) collective-permute-start(bf16[256,768]{1,0:T(8,128)(2,1)S(1)} %add_convert_fusion.7), channel_id=1, source_target_pairs={{0,16},{1,17},{2,18},{3,19},{4,20},{5,21},{6,22},{7,23},{8,24},{9,... | collective-permute-start | bytes 1179656 | tf_op jit(solution)/shard_map/ppermute | solution.py:359
  187.0 22.1 %collective-permute-start.26 = (bf16[256,1536]{1,0:T(8,128)(2,1)S(1)}, bf16[256,1536]{1,0:T(8,128)(2,1)S(1)}, u32[]{:S(2)}, u32[]{:S(2)}) collective-permute-start(bf16[256,1536]{1,0:T(8,128)(2,1)S(1)} %slice.405), channel_id=1, source_target_pairs={{0,16},{1,17},{2,18},{3,19},{4,20},{5,21},{6,22},{7,23},{8,24},{9,... | collective-permute-start | bytes 2359304 | tf_op jit(solution)/shard_map/ppermute | solution.py:363
  188.4 24.9 %collective-permute-start.29 = (bf16[256,768]{1,0:T(8,128)(2,1)S(1)}, bf16[256,768]{1,0:T(8,128)(2,1)S(1)}, u32[]{:S(2)}, u32[]{:S(2)}) collective-permute-start(bf16[256,768]{1,0:T(8,128)(2,1)S(1)} %get-tuple-element.16), channel_id=1, source_target_pairs={{0,16},{1,17},{2,18},{3,19},{4,20},{5,21},{6,22},{7,23},{8,24},{9,... | collective-permute-start | bytes 1179656 | tf_op jit(solution)/shard_map/ppermute | solution.py:359
  192.2 152.3 %collective-permute-start.33 = (bf16[512,384]{1,0:T(8,128)(2,1)}, bf16[512,384]{1,0:T(8,128)(2,1)}, u32[]{:S(2)}, u32[]{:S(2)}) collective-permute-start(bf16[512,384]{1,0:T(8,128)(2,1)} %get-tuple-element.50), channel_id=1, source_target_pairs={{0,4},{4,0},{8,12},{12,8},{1,5},{5,1},{9,13},{13,9},{2,6},{6,2},{1... | collective-permute-start | bytes 1179656 | tf_op jit(solution)/shard_map/ppermute | solution.py:315
  192.4 50.6 %collective-permute-start.17 = (bf16[256,768]{1,0:T(8,128)(2,1)S(1)}, bf16[256,768]{1,0:T(8,128)(2,1)S(1)}, u32[]{:S(2)}, u32[]{:S(2)}) collective-permute-start(bf16[256,768]{1,0:T(8,128)(2,1)S(1)} %get-tuple-element.17), channel_id=1, source_target_pairs={{0,16},{1,17},{2,18},{3,19},{4,20},{5,21},{6,22},{7,23},{8,24},{9,... | collective-permute-start | bytes 1179656 | tf_op jit(solution)/shard_map/ppermute | solution.py:359
  195.9 60.1 %collective-permute-start.9 = (bf16[2,256,768]{2,1,0:T(8,128)(2,1)S(1)}, bf16[2,256,768]{2,1,0:T(8,128)(2,1)S(1)}, u32[]{:S(2)}, u32[]{:S(2)}) collective-permute-start(bf16[2,256,768]{2,1,0:T(8,128)(2,1)S(1)} %stack.75), channel_id=1, source_target_pairs={{0,4},{4,0},{8,12},{12,8},{1,5},{5,1},{9,13},{13,9},{2,6},{6,2},{1... | collective-permute-start | bytes 2359304 | tf_op jit(solution)/shard_map/ppermute | solution.py:315
  196.4 96.9 %slice-start.4 = ((s8[14155776]{0:T(1024)(128)(4,1)}), s8[1572864]{0:T(1024)(128)(4,1)S(1)}, s32[]{:S(2)}) async-start(s8[14155776]{0:T(1024)(128)(4,1)} %bitcast.181), calls=%async_computation.4 | async-start | bytes 3145728
  196.5 12.6 %copy-start.1 = (bf16[256,3072]{1,0:T(8,128)(2,1)S(1)}, bf16[256,3072]{1,0:T(8,128)(2,1)}, u32[]{:S(2)}) copy-start(bf16[256,3072]{1,0:T(8,128)(2,1)} %copy-done) | copy-start | bytes 4718596
  209.1 61.8 %collective-permute-start.11 = (bf16[2,256,768]{2,1,0:T(8,128)(2,1)S(1)}, bf16[2,256,768]{2,1,0:T(8,128)(2,1)S(1)}, u32[]{:S(2)}, u32[]{:S(2)}) collective-permute-start(bf16[2,256,768]{2,1,0:T(8,128)(2,1)S(1)} %stack.76), channel_id=1, source_target_pairs={{0,4},{4,0},{8,12},{12,8},{1,5},{5,1},{9,13},{13,9},{2,6},{6,2},{1... | collective-permute-start | bytes 2359304 | tf_op jit(solution)/shard_map/ppermute | solution.py:315
  209.2 84.1 %slice-start.5 = ((s8[14155776]{0:T(1024)(128)(4,1)}), s8[4194304]{0:T(1024)(128)(4,1)S(1)}, s32[]{:S(2)}) async-start(s8[14155776]{0:T(1024)(128)(4,1)} %bitcast.181), calls=%async_computation.5 | async-start | bytes 8388608
  213.3 28.1 %collective-permute-start.6 = (bf16[128,768]{1,0:T(8,128)(2,1)S(1)}, bf16[128,768]{1,0:T(8,128)(2,1)S(1)}, u32[]{:S(2)}, u32[]{:S(2)}) collective-permute-start(bf16[128,768]{1,0:T(8,128)(2,1)S(1)} %slice.366), channel_id=1, source_target_pairs={{16,0},{17,1},{18,2},{19,3},{20,4},{21,5},{22,6},{23,7},{24,8},{25... | collective-permute-start | bytes 589832 | tf_op jit(solution)/shard_map/ppermute | solution.py:453
  216.6 76.7 %slice-start.6 = ((s8[14155776]{0:T(1024)(128)(4,1)}), s8[4194304]{0:T(1024)(128)(4,1)S(1)}, s32[]{:S(2)}) async-start(s8[14155776]{0:T(1024)(128)(4,1)} %bitcast.181), calls=%async_computation.6 | async-start | bytes 8388608
  241.4 12.1 %collective-permute-start.34 = (bf16[256,768]{1,0:T(8,128)(2,1)S(1)}, bf16[256,768]{1,0:T(8,128)(2,1)S(1)}, u32[]{:S(2)}, u32[]{:S(2)}) collective-permute-start(bf16[256,768]{1,0:T(8,128)(2,1)S(1)} %broadcast_select_fusion.16), channel_id=1, source_target_pairs={{0,8},{4,12},{8,0},{12,4},{1,9},{5,13},{9,1},{13,5},{2,10},{6,14},... | collective-permute-start | bytes 1179656 | tf_op jit(solution)/shard_map/ppermute | solution.py:315
  243.0 6.5 %collective-permute-start.8 = (bf16[128,768]{1,0:T(8,128)(2,1)S(1)}, bf16[128,768]{1,0:T(8,128)(2,1)S(1)}, u32[]{:S(2)}, u32[]{:S(2)}) collective-permute-start(bf16[128,768]{1,0:T(8,128)(2,1)S(1)} %add_convert_fusion.9), channel_id=1, source_target_pairs={{0,16},{16,0},{1,17},{17,1},{2,18},{18,2},{3,19},{19,3},{4,20},{20... | collective-permute-start | bytes 589832 | tf_op jit(solution)/shard_map/ppermute | solution.py:356
  245.9 32.3 %copy-start.6 = (bf16[256,768]{1,0:T(8,128)(2,1)}, bf16[256,768]{1,0:T(8,128)(2,1)S(1)}, u32[]{:S(2)}) copy-start(bf16[256,768]{1,0:T(8,128)(2,1)S(1)} %broadcast_select_fusion.15) | copy-start | bytes 1179652
  249.5 12.4 %collective-permute-start.30 = (bf16[256,768]{1,0:T(8,128)(2,1)S(1)}, bf16[256,768]{1,0:T(8,128)(2,1)S(1)}, u32[]{:S(2)}, u32[]{:S(2)}) collective-permute-start(bf16[256,768]{1,0:T(8,128)(2,1)S(1)} %broadcast_select_fusion.12), channel_id=1, source_target_pairs={{0,8},{4,12},{8,0},{12,4},{1,9},{5,13},{9,1},{13,5},{2,10},{6,14},... | collective-permute-start | bytes 1179656 | tf_op jit(solution)/shard_map/ppermute | solution.py:315
  253.6 9.5 %copy-start.15 = (bf16[256,768]{1,0:T(8,128)(2,1)}, bf16[256,768]{1,0:T(8,128)(2,1)S(1)}, u32[]{:S(2)}) copy-start(bf16[256,768]{1,0:T(8,128)(2,1)S(1)} %collective-permute-done.34) | copy-start | bytes 1179652
  253.6 16.3 %collective-permute-start.27 = (bf16[256,768]{1,0:T(8,128)(2,1)S(1)}, bf16[256,768]{1,0:T(8,128)(2,1)S(1)}, u32[]{:S(2)}, u32[]{:S(2)}) collective-permute-start(bf16[256,768]{1,0:T(8,128)(2,1)S(1)} %get-tuple-element.56), channel_id=1, source_target_pairs={{0,8},{4,12},{8,0},{12,4},{1,9},{5,13},{9,1},{13,5},{2,10},{6,14},... | collective-permute-start | bytes 1179656 | tf_op jit(solution)/shard_map/ppermute | solution.py:315
  256.0 22.3 %collective-permute-start.18 = (bf16[256,768]{1,0:T(8,128)(2,1)S(1)}, bf16[256,768]{1,0:T(8,128)(2,1)S(1)}, u32[]{:S(2)}, u32[]{:S(2)}) collective-permute-start(bf16[256,768]{1,0:T(8,128)(2,1)S(1)} %broadcast_select_fusion.15), channel_id=1, source_target_pairs={{0,8},{4,12},{8,0},{12,4},{1,9},{5,13},{9,1},{13,5},{2,10},{6,14},... | collective-permute-start | bytes 1179656 | tf_op jit(solution)/shard_map/ppermute | solution.py:315
  256.7 36.6 %slice-start.7 = ((s8[14155776]{0:T(1024)(128)(4,1)}), s8[4194304]{0:T(1024)(128)(4,1)S(1)}, s32[]{:S(2)}) async-start(s8[14155776]{0:T(1024)(128)(4,1)} %bitcast.181), calls=%async_computation.7 | async-start | bytes 8388608
  262.0 8.9 %copy-start.17 = (bf16[256,768]{1,0:T(8,128)(2,1)}, bf16[256,768]{1,0:T(8,128)(2,1)S(1)}, u32[]{:S(2)}) copy-start(bf16[256,768]{1,0:T(8,128)(2,1)S(1)} %collective-permute-done.30) | copy-start | bytes 1179652
  262.0 96.5 %collective-permute-start.35 = (bf16[512,768]{1,0:T(8,128)(2,1)}, bf16[512,768]{1,0:T(8,128)(2,1)}, u32[]{:S(2)}, u32[]{:S(2)}) collective-permute-start(bf16[512,768]{1,0:T(8,128)(2,1)} %pad_maximum_fusion.15), channel_id=1, source_target_pairs={{0,4},{4,0},{8,12},{12,8},{1,5},{5,1},{9,13},{13,9},{2,6},{6,2},{1... | collective-permute-start | bytes 2359304 | tf_op jit(solution)/shard_map/ppermute | solution.py:315
  269.8 15.0 %collective-permute-start.10 = (bf16[1,256,768]{2,1,0:T(8,128)(2,1)S(1)}, bf16[1,256,768]{2,1,0:T(8,128)(2,1)S(1)}, u32[]{:S(2)}, u32[]{:S(2)}) collective-permute-start(bf16[1,256,768]{2,1,0:T(8,128)(2,1)S(1)} %add_convert_fusion.5), channel_id=1, source_target_pairs={{0,8},{4,12},{8,0},{12,4},{1,9},{5,13},{9,1},{13,5},{2,10},{6,14},... | collective-permute-start | bytes 1179656 | tf_op jit(solution)/shard_map/ppermute | solution.py:315
  270.9 82.1 %collective-permute-start.28 = (bf16[512,384]{1,0:T(8,128)(2,1)}, bf16[512,384]{1,0:T(8,128)(2,1)}, u32[]{:S(2)}, u32[]{:S(2)}) collective-permute-start(bf16[512,384]{1,0:T(8,128)(2,1)} %get-tuple-element.54), channel_id=1, source_target_pairs={{0,4},{4,0},{8,12},{12,8},{1,5},{5,1},{9,13},{13,9},{2,6},{6,2},{1... | collective-permute-start | bytes 1179656 | tf_op jit(solution)/shard_map/ppermute | solution.py:315
  278.3 6.7 %copy-start.19 = (bf16[256,768]{1,0:T(8,128)(2,1)}, bf16[256,768]{1,0:T(8,128)(2,1)S(1)}, u32[]{:S(2)}) copy-start(bf16[256,768]{1,0:T(8,128)(2,1)S(1)} %collective-permute-done.18) | copy-start | bytes 1179652
  278.3 10.8 %collective-permute-start.12 = (bf16[1,256,768]{2,1,0:T(8,128)(2,1)S(1)}, bf16[1,256,768]{2,1,0:T(8,128)(2,1)S(1)}, u32[]{:S(2)}, u32[]{:S(2)}) collective-permute-start(bf16[1,256,768]{2,1,0:T(8,128)(2,1)S(1)} %add_convert_fusion.2), channel_id=1, source_target_pairs={{0,8},{4,12},{8,0},{12,4},{1,9},{5,13},{9,1},{13,5},{2,10},{6,14},... | collective-permute-start | bytes 1179656 | tf_op jit(solution)/shard_map/ppermute | solution.py:315
  285.0 55.7 %collective-permute-start.20 = (bf16[256,768]{1,0:T(8,128)(2,1)S(1)}, bf16[256,768]{1,0:T(8,128)(2,1)}, u32[]{:S(2)}, u32[]{:S(2)}) collective-permute-start(bf16[256,768]{1,0:T(8,128)(2,1)S(1)} %fusion.141), channel_id=1, source_target_pairs={{0,16},{1,17},{2,18},{3,19},{4,20},{5,21},{6,22},{7,23},{8,24},{9,... | collective-permute-start | bytes 1179656 | tf_op jit(solution)/shard_map/ppermute | solution.py:359
  289.3 51.6 %collective-permute-start.23 = (bf16[256,768]{1,0:T(8,128)(2,1)S(1)}, bf16[256,768]{1,0:T(8,128)(2,1)}, u32[]{:S(2)}, u32[]{:S(2)}) collective-permute-start(bf16[256,768]{1,0:T(8,128)(2,1)S(1)} %fusion.142), channel_id=1, source_target_pairs={{0,16},{1,17},{2,18},{3,19},{4,20},{5,21},{6,22},{7,23},{8,24},{9,... | collective-permute-start | bytes 1179656 | tf_op jit(solution)/shard_map/ppermute | solution.py:359
  340.7 7.8 %collective-permute-start.21 = (bf16[256,768]{1,0:T(8,128)(2,1)S(1)}, bf16[256,768]{1,0:T(8,128)(2,1)S(1)}, u32[]{:S(2)}, u32[]{:S(2)}) collective-permute-start(bf16[256,768]{1,0:T(8,128)(2,1)S(1)} %broadcast_select_fusion.14), channel_id=1, source_target_pairs={{0,8},{4,12},{8,0},{12,4},{1,9},{5,13},{9,1},{13,5},{2,10},{6,14},... | collective-permute-start | bytes 1179656 | tf_op jit(solution)/shard_map/ppermute | solution.py:315
  340.9 11.9 %collective-permute-start.24 = (bf16[256,768]{1,0:T(8,128)(2,1)S(1)}, bf16[256,768]{1,0:T(8,128)(2,1)S(1)}, u32[]{:S(2)}, u32[]{:S(2)}) collective-permute-start(bf16[256,768]{1,0:T(8,128)(2,1)S(1)} %broadcast_select_fusion.13), channel_id=1, source_target_pairs={{0,8},{4,12},{8,0},{12,4},{1,9},{5,13},{9,1},{13,5},{2,10},{6,14},... | collective-permute-start | bytes 1179656 | tf_op jit(solution)/shard_map/ppermute | solution.py:315
  343.0 5.6 %copy-start.11 = (bf16[512,768]{1,0:T(8,128)(2,1)S(1)}, bf16[512,768]{1,0:T(8,128)(2,1)}, u32[]{:S(2)}) copy-start(bf16[512,768]{1,0:T(8,128)(2,1)} %pad_maximum_fusion.11) | copy-start | bytes 2359300
  344.6 18.5 %collective-permute-start.31 = (bf16[512,768]{1,0:T(8,128)(2,1)S(1)}, bf16[512,768]{1,0:T(8,128)(2,1)S(1)}, u32[]{:S(2)}, u32[]{:S(2)}) collective-permute-start(bf16[512,768]{1,0:T(8,128)(2,1)S(1)} %copy-done.10), channel_id=1, source_target_pairs={{0,4},{4,0},{8,12},{12,8},{1,5},{5,1},{9,13},{13,9},{2,6},{6,2},{1... | collective-permute-start | bytes 2359304 | tf_op jit(solution)/shard_map/ppermute | solution.py:315
  344.7 8.2 %copy-start.14 = (bf16[512,384]{1,0:T(8,128)(2,1)S(1)}, bf16[512,384]{1,0:T(8,128)(2,1)}, u32[]{:S(2)}) copy-start(bf16[512,384]{1,0:T(8,128)(2,1)} %get-tuple-element.58) | copy-start | bytes 1179652
  348.6 17.5 %collective-permute-start.19 = (bf16[512,768]{1,0:T(8,128)(2,1)S(1)}, bf16[512,768]{1,0:T(8,128)(2,1)S(1)}, u32[]{:S(2)}, u32[]{:S(2)}) collective-permute-start(bf16[512,768]{1,0:T(8,128)(2,1)S(1)} %copy-done.11), channel_id=1, source_target_pairs={{0,4},{4,0},{8,12},{12,8},{1,5},{5,1},{9,13},{13,9},{2,6},{6,2},{1... | collective-permute-start | bytes 2359304 | tf_op jit(solution)/shard_map/ppermute | solution.py:315
  352.8 5.7 %collective-permute-start.13 = (bf16[128,768]{1,0:T(8,128)(2,1)S(1)}, bf16[128,768]{1,0:T(8,128)(2,1)S(1)}, u32[]{:S(2)}, u32[]{:S(2)}) collective-permute-start(bf16[128,768]{1,0:T(8,128)(2,1)S(1)} %select_convert_fusion), channel_id=1, source_target_pairs={{0,16},{16,0},{1,17},{17,1},{2,18},{18,2},{3,19},{19,3},{4,20},{20... | collective-permute-start | bytes 589832 | tf_op jit(solution)/shard_map/ppermute | solution.py:356
  352.9 7.1 %copy-start.13 = (bf16[512,384]{1,0:T(8,128)(2,1)S(1)}, bf16[512,384]{1,0:T(8,128)(2,1)}, u32[]{:S(2)}) copy-start(bf16[512,384]{1,0:T(8,128)(2,1)} %get-tuple-element.49) | copy-start | bytes 1179652
  352.9 7.1 %copy-start.16 = (bf16[256,768]{1,0:T(8,128)(2,1)S(1)}, bf16[256,768]{1,0:T(8,128)(2,1)}, u32[]{:S(2)}) copy-start(bf16[256,768]{1,0:T(8,128)(2,1)} %copy-done.15) | copy-start | bytes 1179652
  353.0 13.1 %collective-permute-start.16 = (bf16[512,384]{1,0:T(8,128)(2,1)S(1)}, bf16[512,384]{1,0:T(8,128)(2,1)S(1)}, u32[]{:S(2)}, u32[]{:S(2)}) collective-permute-start(bf16[512,384]{1,0:T(8,128)(2,1)S(1)} %copy-done.14), channel_id=1, source_target_pairs={{0,4},{4,0},{8,12},{12,8},{1,5},{5,1},{9,13},{13,9},{2,6},{6,2},{1... | collective-permute-start | bytes 1179656 | tf_op jit(solution)/shard_map/ppermute | solution.py:315
  358.5 8.5 %collective-permute-start.22 = (bf16[512,768]{1,0:T(8,128)(2,1)S(1)}, bf16[512,768]{1,0:T(8,128)(2,1)S(1)}, u32[]{:S(2)}, u32[]{:S(2)}) collective-permute-start(bf16[512,768]{1,0:T(8,128)(2,1)S(1)} %pad_maximum_fusion.12), channel_id=1, source_target_pairs={{0,4},{4,0},{8,12},{12,8},{1,5},{5,1},{9,13},{13,9},{2,6},{6,2},{1... | collective-permute-start | bytes 2359304 | tf_op jit(solution)/shard_map/ppermute | solution.py:315
  358.5 9.3 %collective-permute-start.25 = (bf16[512,768]{1,0:T(8,128)(2,1)S(1)}, bf16[512,768]{1,0:T(8,128)(2,1)S(1)}, u32[]{:S(2)}, u32[]{:S(2)}) collective-permute-start(bf16[512,768]{1,0:T(8,128)(2,1)S(1)} %pad_maximum_fusion.13), channel_id=1, source_target_pairs={{0,4},{4,0},{8,12},{12,8},{1,5},{5,1},{9,13},{13,9},{2,6},{6,2},{1... | collective-permute-start | bytes 2359304 | tf_op jit(solution)/shard_map/ppermute | solution.py:315
  359.9 3.2 copy-start.18
  359.9 3.2 copy-start.21
  (8 other events, 19.0 us)

commit v3 on v2

--- a/solution.py
+++ b/solution.py
@@ -15,11 +15,18 @@
 MESH = pl.DeviceIdType.MESH
 
 
-def greet(peers):
+def greet(peers, row_peers=()):
     barrier = pltpu.get_barrier_semaphore()
     for peer in peers:
         pl.semaphore_signal(barrier, inc=1, device_id={"head": peer}, device_id_type=MESH)
-    pl.semaphore_wait(barrier, len(peers))
+    for peer in row_peers:
+        pl.semaphore_signal(barrier, inc=1, device_id={"row": peer}, device_id_type=MESH)
+    pl.semaphore_wait(barrier, len(peers) + len(row_peers))
+
+
+def row_partner(bit):
+    row = lax.axis_index("row")
+    return row + bit - 2 * bit * ((row // bit) % 2)
 
 
 def others(me, n):
@@ -130,16 +137,44 @@
     )(*arrays)
 
 
-def line_sum_kernel(n, small, *refs):
-    if small:
+def line_sum_kernel(n, small, bits, *refs):
+    if bits:
+        x, keyed, total, key_total, *scratch = refs
+        acc, taken, key_send, key_recv = scratch[-4:]
+    elif small:
         x, extra, total, extras, *scratch = refs
         extra_send, extra_recv, extra_local = scratch[-3:]
     else:
         x, total, *scratch = refs
     sends, recvs, send, recv = scratch[:4]
     me = lax.axis_index("head")
-    greet(others(me, n))
+    greet(others(me, n), [row_partner(bit) for bit in bits])
     f32 = jnp.float32
+
+    def key_copy(stage):
+        size = 1 << (len(bits) - 1 - stage)
+        return pltpu.make_async_remote_copy(
+            src_ref=(acc if stage else keyed).at[pl.ds(size, size)],
+            dst_ref=taken.at[pl.ds(size, size)],
+            send_sem=key_send.at[stage],
+            recv_sem=key_recv.at[stage],
+            device_id={"row": row_partner(bits[stage])},
+            device_id_type=MESH,
+        )
+
+    def key_add(stage):
+        size = 1 << (len(bits) - 1 - stage)
+        key_copy(stage).wait_recv()
+        for index in range(size):
+            block = keyed[index] if stage == 0 else acc[index]
+            both = block.astype(f32) + taken[size + index].astype(f32)
+            if stage == len(bits) - 1:
+                key_total[...] = both.astype(key_total.dtype)
+            else:
+                acc[index] = both.astype(acc.dtype)
+
+    if bits:
+        key_copy(0).start()
 
     def extra_copy(step):
         return pltpu.make_async_remote_copy(
@@ -187,6 +222,10 @@
         high, low = n - 1 - step, step
         pl.when(me < high)(lambda: pass_on(0, high, me > 0))
         pl.when(me > low)(lambda: pass_on(1, low, me < n - 1))
+        if step == 0:
+            for stage in range(len(bits) - 1):
+                key_add(stage)
+                key_copy(stage + 1).start()
 
     total[...] = x[me].astype(f32)
 
@@ -204,6 +243,10 @@
         high, low = n - 1 - step, step
         pl.when(me < high)(lambda: copy_of(0, high).wait_send())
         pl.when(me > low)(lambda: copy_of(1, low).wait_send())
+    if bits:
+        key_add(len(bits) - 1)
+        for stage in range(len(bits)):
+            key_copy(stage).wait_send()
     if small:
         for step in range(1, n):
             origin = lax.rem(me + n - step, n)
@@ -219,10 +262,11 @@
         extra_own.wait()
 
 
-def line_sum(number, name, x, extra=None):
+def line_sum(number, name, x, extra=None, keyed=None):
     n, block = x.shape[0], x.shape[1:]
     small = extra is not None
-    arrays = [x, extra] if small else [x]
+    bits = row_bits()[::-1] if keyed is not None else []
+    arrays = [x] + [array for array in (extra, keyed) if array is not None]
     shapes = [jax.ShapeDtypeStruct(block, jnp.float32)]
     scratch = [
         pltpu.VMEM((2,) + x.shape, x.dtype),
@@ -237,8 +281,16 @@
             pltpu.SemaphoreType.DMA((n,)),
             pltpu.SemaphoreType.DMA,
         ]
+    if bits:
+        shapes.append(jax.ShapeDtypeStruct(keyed.shape[1:], keyed.dtype))
+        scratch += [
+            pltpu.VMEM(keyed.shape, keyed.dtype),
+            pltpu.VMEM(keyed.shape, keyed.dtype),
+            pltpu.SemaphoreType.DMA((len(bits),)),
+            pltpu.SemaphoreType.DMA((len(bits),)),
+        ]
     return pl.pallas_call(
-        functools.partial(line_sum_kernel, n, small),
+        functools.partial(line_sum_kernel, n, small, tuple(bits)),
         out_shape=shapes,
         in_specs=[pl.BlockSpec(memory_space=pltpu.VMEM)] * len(arrays),
         out_specs=[pl.BlockSpec(memory_space=pltpu.VMEM)] * len(shapes),
@@ -253,7 +305,7 @@
     )(*arrays)
 
 
-def attention_kernel(q_ref, k_ref, v_ref, g_ref, o_ref, dq_ref, dk_ref, dv_ref):
+def attention_kernel(q_ref, k_ref, v_ref, g_ref, o_ref, dq_ref, dkv_ref):
     scaling = HD ** (-0.5)
     query, cot = q_ref[...], g_ref[...]
     keys = k_ref[...].reshape(-1, HD)
@@ -274,11 +326,12 @@
     dquery = jnp.dot(dscores, keys, preferred_element_type=jnp.float32) * scaling
     dq_ref[...] = dquery.astype(jnp.bfloat16)
     dkey = lax.dot_general(dscores, query, first, preferred_element_type=jnp.float32) * scaling
-    dk_ref[...] = dkey.astype(jnp.bfloat16).reshape(dk_ref.shape)
+    rows, unused, tok, unused = dkv_ref.shape
+    dkv_ref[:, 0] = dkey.astype(jnp.bfloat16).reshape(rows, tok, HD)
     dval = lax.dot_general(
         probs.astype(jnp.bfloat16), cot, first, preferred_element_type=jnp.float32
     )
-    dv_ref[...] = dval.astype(jnp.bfloat16).reshape(dv_ref.shape)
+    dkv_ref[:, 1] = dval.astype(jnp.bfloat16).reshape(rows, tok, HD)
 
 
 def attention(query, keys, values, cot):
@@ -287,13 +340,14 @@
     own = pl.BlockSpec((tok, HD), lambda h: (0, h))
     every = pl.BlockSpec((rows, tok, HD), lambda h: (0, 0, h))
     small = jax.ShapeDtypeStruct((tok, width), jnp.bfloat16)
-    large = jax.ShapeDtypeStruct((rows, tok, width), jnp.bfloat16)
+    large = jax.ShapeDtypeStruct((rows, 2, tok, width), jnp.bfloat16)
+    pair = pl.BlockSpec((rows, 2, tok, HD), lambda h: (0, 0, 0, h))
     return pl.pallas_call(
         attention_kernel,
         grid=(width // HD,),
-        out_shape=[small, small, large, large],
+        out_shape=[small, small, large],
         in_specs=[own, every, every, own],
-        out_specs=[own, own, every, every],
+        out_specs=[own, own, pair],
         compiler_params=pltpu.CompilerParams(vmem_limit_bytes=50 * 1024 * 1024),
         name="attention",
     )(query, keys, values, cot)
@@ -402,26 +456,16 @@
         jnp.concatenate([cot_other, cot_half]),
     )
     gated_main = (gate * cot_full.astype(f32)).astype(bf16)
-    gated_full = jnp.where(control, widen(gated_blocks), gated_main)
+    gated_full = lax.optimization_barrier(
+        jnp.where(control, widen(gated_blocks), gated_main)
+    )
     attn_grad = dot(gated_full, w_out, ((1,), (0,))).astype(bf16)
-    attn, dquery, key_terms, value_terms = attention(query, all_keys, all_values, attn_grad)
-
-    bits = row_bits()
-
-    def row_sum(x):
-        blocks = [x[index] for index in range(n_row)]
-        for bit in bits[::-1]:
-            count = len(blocks) // 2
-            other = row_swap(jnp.stack(blocks[count:]), bit)
-            blocks = [
-                (blocks[index].astype(f32) + other[index].astype(f32)).astype(bf16)
-                for index in range(count)
-            ]
-        return blocks[0]
-
-    dkey, dval = row_sum(key_terms), row_sum(value_terms)
-    (branch,) = line_sum(2, "sum_branch", head_terms(attn, w_out))
+    attn, dquery, key_terms = attention(query, all_keys, all_values, attn_grad)
+
+    branch, dkv = line_sum(2, "sum_branch", head_terms(attn, w_out), keyed=key_terms)
     state = (inputs.astype(f32) + gate_dev * branch).astype(bf16)
+    near_state = near(state)
+    dkey, dval = dkv[0], dkv[1]
     grads = [dquery, dkey, dval]
 
     scaled_nhat = nhat * (1.0 + scale)
@@ -434,7 +478,15 @@
         second = second + jnp.sum(term * scaled_nhat[:, cols], axis=-1)
         terms.append(term.astype(bf16))
     sums = jnp.concatenate([first[None], second[None], jnp.zeros((6, tok), f32)])
-    dnorm, sum_parts = line_sum(3, "sum_norm", jnp.stack(terms), sums)
+    state_half = jnp.where(control, near_state[:half], near_state[half:])
+    hint_terms = head_terms(state_half, zero_weight)
+    near_attn, near_query, near_gated = near(attn), near(dquery), near_cols(gated_full)
+    terms, hint_terms, near_attn, near_query, near_gated = lax.optimization_barrier(
+        (terms, hint_terms, near_attn, near_query, near_gated)
+    )
+    both = jnp.concatenate([jnp.stack(terms), hint_terms], axis=1)
+    both, sum_parts = line_sum(3, "sum_norm_hint", both, sums)
+    dnorm, projected = both[:tok], both[tok:]
     sums = jnp.sum(sum_parts, axis=0) / full_width
     nhat_dev = lax.dynamic_slice_in_dim(nhat, head_pos * width, width, 1)
     scaled = dnorm * (1.0 + scale_dev)
@@ -447,9 +499,6 @@
     latent_grad = (own_half + other_half)[None, None]
     hint_grad = jnp.where(control, own_half, other_half)[None, None]
 
-    near_state = near(state)
-    state_half = jnp.where(control, near_state[:half], near_state[half:])
-    (projected,) = line_sum(4, "sum_hint", head_terms(state_half, zero_weight))
     main_state = lax.ppermute(state[:half], "group", [(1, 0)])
     main_half = jnp.where(control, main_state, state[half:])
     mixed_half = (main_half.astype(f32) + projected).astype(bf16)
@@ -462,10 +511,11 @@
 
     tokens = ((0,), (0,))
     normed_cols = cube_deal(near_cols(normed))
+    near_grads = [near_query, near(dkey), near(dval)]
     qkv_grad = jnp.stack(
-        [dot(normed_cols, cube_gather(near(grads[c]), 0), tokens) for c in range(3)], axis=1
-    )
-    out_grad = dot(cube_deal(near_cols(gated_full)), cube_gather(near(attn), 0), tokens)
+        [dot(normed_cols, cube_gather(x, 0), tokens) for x in near_grads], axis=1
+    )
+    out_grad = dot(cube_deal(near_gated), cube_gather(near_attn, 0), tokens)
     cot_cols = jnp.where(
         control, cot_full[:, : full_width // 2], cot_full[:, full_width // 2 :]
     )

time: 372 us -> 339 us (0.911)
  waiting for transfers between devices: 55.7 us -> 17.8 us
  matrix products: 36.3 us -> 51.5 us
  Pallas kernels: 183 us -> 175 us
  other arithmetic: 51.2 us -> 46.2 us
    ppermute x24 -> x20, waiting for transfers between devices: 35.7 us -> 17.8 us  [row_swap(): lax.ppermute(x, 'row', [(row, row ^ bit) for row in range(lax.axis_size('...]
    dot_general x30, matrix products: 36.3 us -> 51.5 us  [dot(): lax.dot_general(a, b, (dims, ((), ())), preferred_element_type=jnp.float32)]
    ppermute x4, waiting for transfers between devices: 9.03 us -> 0.01 us  [swap(): return lax.ppermute(x, 'group', [(0, 1), (1, 0)])]
    ppermute x2, waiting for transfers between devices: 8.85 us -> 0.01 us  [near_cols(): lax.ppermute(x[:, cols:], 'group', [(0, 1)])]
    pallas_call x3 -> x2, Pallas kernels: 102 us -> 94.5 us  [line_sum(): pl.pallas_call(functools.partial(line_sum_kernel, n, small, tuple(bits)),...]
    select_n x6, other arithmetic: 7.38 us -> 3.11 us  [cube_deal(): kept, sent = (jnp.where(upper, high, low), jnp.where(upper, low, high))]
    ppermute x24 -> x20, starting transfers between devices: 12.2 us -> 12.9 us  [row_swap(): lax.ppermute(x, 'row', [(row, row ^ bit) for row in range(lax.axis_size('...]
  transfers between devices with their start and end apart: 36 -> 32, of which waited for: 11 -> 5; matrix products, arithmetic and copies ran while one was open for 22% -> 27% of each run, Pallas kernels for 37% -> 39%
where the time goes in v3:
time: 339 us; the launch traced here: 338 us
  Pallas kernels  175 us (52%)
  matrix products  51.5 us (15%)
  other arithmetic  46.2 us (14%)
  starting transfers between devices  36.3 us (11%)
  waiting for transfers between devices  17.8 us (5%)
  local copies, waits for them, and re-layouts  8.09 us (2%)
    pallas_call x2, Pallas kernels, line_sum(): pl.pallas_call(functools.partial(line_sum_kernel, n, small, tuple(bits)),...  94.5 us
    pallas_call x2, Pallas kernels, line_gather(): pl.pallas_call(functools.partial(line_gather_kernel, n, tuple((source for...  70.5 us
    dot_general x30, matrix products, dot(): lax.dot_general(a, b, (dims, ((), ())), preferred_element_type=jnp.float32)  51.5 us
    ppermute x20, waiting for transfers between devices, row_swap(): lax.ppermute(x, 'row', [(row, row ^ bit) for row in range(lax.axis_size('...  17.8 us
    select_n x1, other arithmetic, on_device(): jnp.where(control, widen(gated_blocks), gated_main)  13.5 us
    ppermute x20, starting transfers between devices, row_swap(): lax.ppermute(x, 'row', [(row, row ^ bit) for row in range(lax.axis_size('...  12.9 us
    ppermute x5, starting transfers between devices, near(): return jnp.where(control, x, lax.ppermute(x, 'group', [(0, 1)]))  11.3 us
    pallas_call x1, Pallas kernels, attention(): pl.pallas_call(attention_kernel, grid=(width // HD,), out_shape=[small, s...  10.3 us
  transfers between devices with their start and end apart: 32, of which 5 were waited for; matrix products, arithmetic and copies ran while one was open for 27% of the time, Pallas kernels for 39%

profile of v3, /device:TPU:0, one launch (start us, length us, event | category | flops | bytes accessed | tf_op | source)
XLA Modules:
  0.0 337.6 jit_solution(5250552117956955582)
XLA Ops:
  0.6 1.7 slice_select_fusion.6.refs_0_
  2.4 2.1 fusion.138.refs_1_
  4.5 44.6 %gather_inputs.1 = (bf16[4,128,768]{2,1,0:T(8,128)(2,1)}, bf16[4,256,768]{2,1,0:T(8,128)(2,1)}) custom-call(bf16[128,768]{1,0:T(8,128)(2,1)} %slice_select_fusion.6.refs_0_, bf16[256,768]{1,0:T(8,128)(2,1)} %fusion.138.refs_1_), custom_call_target="tpu_custom_call" | custom-call | bytes 117964800 | tf_op jit(solution)/shard_map/gather_inputs/pallas_call | solution.py:128
  49.1 1.3 slice_bitcast_fusion.37
  50.4 3.9 %convolution_convert_fusion.4 = bf16[128,768]{1,0:T(8,128)(2,1)} fusion(bf16[3072,768]{1,0:T(8,128)(2,1)} %param.14, bf16[128,768]{1,0:T(8,128)(2,1)S(1)} %get-tuple-element.88, bf16[128,768]{1,0:T(8,128)(2,1)S(1)} %get-tuple-element.89, bf16[128,768]{1,0:T(8,128)(2,1)S(1)} %get-tuple-element.90, bf16[128,768]{1,0:T(8,128)(2,1)S(1)} %get-tuple-element.87), kind=kOutput, calls=%fused_computation.122 | convolution fusion | flops 607223808 | bytes 5701632 | tf_op jit(solution)/shard_map/dot_general | solution.py:357
  54.3 1.5 collective-permute-start.4
  59.8 3.4 %add_convert_fusion = (bf16[256,3072]{1,0:T(8,128)(2,1)S(1)}, f32[256,3072]{1,0:T(8,128)}, f32[256,3072]{1,0:T(8,128)}) fusion(f32[3072]{0:T(1024)S(1)} %bitcast.199, f32[3072]{0:T(1024)S(1)} %bitcast.198, f32[256]{0:T(256)S(1)} %add_rsqrt_fusion, f32[256]{0:T(256)S(1)} %broadcast_multiply_fusion.2, bf16[256,768]{1,0:T(8,128)(2,1)S(1)} %get-tuple-element.62, ...), kind=kLoop, calls=%fused_computation.18 | loop fusion | flops 10223616 | bytes 9463808 | tf_op jit(solution)/shard_map/convert_element_type | solution.py:442
  63.2 3.9 %fusion.77 = bf16[1,256,768]{2,1,0:T(8,128)(2,1)S(1)} fusion(bf16[256,3072]{1,0:T(8,128)(2,1)S(1)} %get-tuple-element.54, bf16[1,3,3072,768]{3,2,1,0:T(8,128)(2,1)} %param.12), kind=kOutput, calls=%fused_computation.81 | convolution fusion | flops 1208156160 | bytes 6684672 | tf_op jit(solution)/shard_map/dot_general | solution.py:357
  67.1 1.6 collective-permute-start
  68.7 1.4 fusion.74
  71.7 4.3 %collective-permute-start.13 = (bf16[256,1536]{1,0:T(8,128)(2,1)}, bf16[256,1536]{1,0:T(8,128)(2,1)}, u32[]{:S(2)}, u32[]{:S(2)}) collective-permute-start(bf16[256,1536]{1,0:T(8,128)(2,1)} %slice.375), channel_id=1, source_target_pairs={{0,16},{1,17},{2,18},{3,19},{4,20},{5,21},{6,22},{7,23},{8,24},{9,... | collective-permute-start | bytes 2359304 | tf_op jit(solution)/shard_map/ppermute | solution.py:417
  76.0 1.4 fusion.58.q_ref
  78.8 1.3 add_reduce_fusion
  80.0 1.8 multiply_convert_fusion.1.refs_0_
  81.9 25.9 %gather_gated.1 = bf16[4,256,768]{2,1,0:T(8,128)(2,1)} custom-call(bf16[256,768]{1,0:T(8,128)(2,1)} %multiply_convert_fusion.1.refs_0_), custom_call_target="tpu_custom_call" | custom-call | bytes 78643200 | tf_op jit(solution)/shard_map/gather_gated/pallas_call | solution.py:128
  107.8 1.5 slice_bitcast_fusion.29
  109.3 1.1 pad_maximum_fusion.6
  110.5 1.1 pad_maximum_fusion.7
  112.1 13.5 %fusion.14 = (bf16[256,3072]{1,0:T(8,128)(2,1)S(1)}, bf16[256,3072]{1,0:T(8,128)(2,1)S(1)}) fusion(bf16[256,768]{1,0:T(8,128)(2,1)S(1)} %get-tuple-element.58, bf16[256,768]{1,0:T(8,128)(2,1)S(1)} %get-tuple-element.59, bf16[256,768]{1,0:T(8,128)(2,1)S(1)} %get-tuple-element.60, bf16[256,768]{1,0:T(8,128)(2,1)S(1)} %get-tuple-element.57, ...), kind=kLoop, calls=%fused_computation.20 | loop fusion | flops 25952256 | bytes 6303745 | tf_op jit(solution)/shard_map/jit(_where)/select_n | solution.py:460
  126.6 1.5 collective-permute-start.28
  128.1 1.3 collective-permute-start.10
  130.2 1.4 fusion.67.g_ref
  131.6 1.2 pad_maximum_fusion.3.k_ref
  132.8 2.3 pad_maximum_fusion.4.v_ref
  135.1 10.3 %attention.1 = (bf16[256,768]{1,0:T(8,128)(2,1)S(1)}, bf16[256,768]{1,0:T(8,128)(2,1)S(1)}, bf16[4,2,256,768]{3,2,1,0:T(8,128)(2,1)}) custom-call(bf16[256,768]{1,0:T(8,128)(2,1)S(1)} %fusion.58.q_ref, bf16[4,256,768]{2,1,0:T(8,128)(2,1)S(1)} %pad_maximum_fusion.3.k_ref, bf16[4,256,768]{2,1,0:T(8,128)(2,1)} %pad_maximum_fusion.4.v_ref, ...), custom_call_target="tpu_custom_call" | custom-call | tf_op jit(solution)/shard_map/attention/pallas_call | solution.py:345
  145.5 1.8 fusion.73
  147.2 1.8 fusion.72
  149.0 1.8 fusion.71
  150.8 1.8 fusion.70
  152.8 1.7 copy-done
  154.5 39.8 %sum_branch.1 = (f32[256,768]{1,0:T(8,128)S(1)}, bf16[2,256,768]{2,1,0:T(8,128)(2,1)S(1)}) custom-call(bf16[4,256,768]{2,1,0:T(8,128)(2,1)S(1)} %pad_maximum_fusion.5.refs_0_, bf16[4,2,256,768]{3,2,1,0:T(8,128)(2,1)S(1)} %copy-done), custom_call_target="tpu_custom_call" | custom-call | bytes 78643200 | tf_op jit(solution)/shard_map/sum_branch/pallas_call | solution.py:292
  194.3 1.8 fusion.82
  196.1 1.8 fusion.80
  197.9 1.8 fusion.86
  199.7 1.8 fusion.87
  201.4 1.8 fusion.85
  203.2 1.8 fusion.83
  205.0 1.8 fusion.81
  206.8 1.8 fusion.84
  208.7 1.3 collective-permute-start.7
  210.1 1.8 fusion.57
  211.8 1.8 fusion.55
  213.7 1.9 fusion.54
  215.7 3.4 fusion.130
  219.8 1.3 collective-permute-start.8
  221.1 1.3 collective-permute-start.9
  223.5 1.3 collective-permute-start.6
  226.8 5.3 %collective-permute-start.18 = (bf16[256,768]{1,0:T(8,128)(2,1)}, bf16[256,768]{1,0:T(8,128)(2,1)}, u32[]{:S(2)}, u32[]{:S(2)}) collective-permute-start(bf16[256,768]{1,0:T(8,128)(2,1)} %get-tuple-element.77), channel_id=1, source_target_pairs={{0,16},{1,17},{2,18},{3,19},{4,20},{5,21},{6,22},{7,23},{8,24},{9,... | collective-permute-start | bytes 1179656 | tf_op jit(solution)/shard_map/ppermute | solution.py:413
  234.4 2.1 collective-permute-start.21
  237.3 1.1 collective-permute-start.30
  240.4 54.7 %sum_norm_hint.1 = (f32[384,768]{1,0:T(8,128)S(1)}, f32[4,8,256]{2,1,0:T(8,128)S(1)}) custom-call(bf16[4,384,768]{2,1,0:T(8,128)(2,1)S(1)} %pad_maximum_fusion.1.refs_0_, f32[8,256]{1,0:T(8,128)S(1)} %maximum_maximum_fusion.refs_1_), custom_call_target="tpu_custom_call" | custom-call | bytes 117964800 | tf_op jit(solution)/shard_map/sum_norm_hint/pallas_call | solution.py:292
  295.2 1.5 multiply_add_fusion
  298.0 3.2 collective-permute-start.11
  301.1 1.2 collective-permute-start.22
  302.4 2.5 collective-permute-done.19
  305.8 1.2 collective-permute-start.26
  307.9 1.1 collective-permute-done.22
  310.1 5.2 %collective-permute-done.16 = bf16[256,768]{1,0:T(8,128)(2,1)S(1)} collective-permute-done((bf16[256,768]{1,0:T(8,128)(2,1)S(1)}, bf16[256,768]{1,0:T(8,128)(2,1)S(1)}, u32[]{:S(2)}, u32[]{:S(2)}) %collective-permute-start.16) | collective-permute-done | bytes 393248 | tf_op jit(solution)/shard_map/ppermute | solution.py:369
  316.8 4.8 %collective-permute-done.26 = bf16[256,768]{1,0:T(8,128)(2,1)S(1)} collective-permute-done((bf16[256,768]{1,0:T(8,128)(2,1)S(1)}, bf16[256,768]{1,0:T(8,128)(2,1)S(1)}, u32[]{:S(2)}, u32[]{:S(2)}) %collective-permute-start.26) | collective-permute-done | bytes 393248 | tf_op jit(solution)/shard_map/ppermute | solution.py:369
  321.7 4.1 %collective-permute-done.24 = bf16[256,768]{1,0:T(8,128)(2,1)S(1)} collective-permute-done((bf16[256,768]{1,0:T(8,128)(2,1)S(1)}, bf16[256,768]{1,0:T(8,128)(2,1)S(1)}, u32[]{:S(2)}, u32[]{:S(2)}) %collective-permute-start.24) | collective-permute-done | bytes 393248 | tf_op jit(solution)/shard_map/ppermute | solution.py:369
  325.9 1.0 pad_maximum_fusion.15
  330.9 1.8 fusion.33
  332.7 2.0 pad_maximum_fusion
  334.7 2.8 fusion.39
  (157 shorter events, 27.4 us)
Async XLA Ops:
  50.4 7.6 %copy-start.11 = (f32[1,8,3,3072]{3,1,2,0:T(8,128)S(1)}, f32[1,8,3,3072]{3,1,2,0:T(8,128)}, u32[]{:S(2)}) copy-start(f32[1,8,3,3072]{3,1,2,0:T(8,128)} %param.11) | copy-start | bytes 884740
  50.4 18.3 %slice-start = ((s8[14155776]{0:T(1024)(128)(4,1)}), s8[1572864]{0:T(1024)(128)(4,1)S(1)}, s32[]{:S(2)}) async-start(s8[14155776]{0:T(1024)(128)(4,1)} %bitcast.195), calls=%async_computation | async-start | bytes 3145728
  54.3 4.5 %copy-start.3 = (bf16[4,256,768]{2,1,0:T(8,128)(2,1)S(1)}, bf16[4,256,768]{2,1,0:T(8,128)(2,1)}, u32[]{:S(2)}) copy-start(bf16[4,256,768]{2,1,0:T(8,128)(2,1)} %get-tuple-element.23) | copy-start | bytes 4718596
  54.3 14.3 %slice-start.1 = ((s8[14155776]{0:T(1024)(128)(4,1)}), s8[4194304]{0:T(1024)(128)(4,1)S(1)}, s32[]{:S(2)}) async-start(s8[14155776]{0:T(1024)(128)(4,1)} %bitcast.195), calls=%async_computation.1 | async-start | bytes 8388608
  54.3 25.7 %collective-permute-start.4 = (bf16[128,768]{1,0:T(8,128)(2,1)}, bf16[128,768]{1,0:T(8,128)(2,1)}, u32[]{:S(2)}, u32[]{:S(2)}) collective-permute-start(bf16[128,768]{1,0:T(8,128)(2,1)} %convolution_convert_fusion.4), channel_id=1, source_target_pairs={{0,16},{16,0},{1,17},{17,1},{2,18},{18,2},{3,19},{19,3},{4,20},{20... | collective-permute-start | bytes 589832 | tf_op jit(solution)/shard_map/ppermute | solution.py:410
  56.8 55.3 %collective-permute-start.5 = (bf16[128,3072]{1,0:T(8,128)(2,1)}, bf16[128,3072]{1,0:T(8,128)(2,1)}, u32[]{:S(2)}, u32[]{:S(2)}) collective-permute-start(bf16[128,3072]{1,0:T(8,128)(2,1)} %pad_maximum_fusion.8), channel_id=1, source_target_pairs={{0,16},{16,0},{1,17},{17,1},{2,18},{18,2},{3,19},{19,3},{4,20},{20... | collective-permute-start | bytes 2359304 | tf_op jit(solution)/shard_map/ppermute | solution.py:410
  59.8 3.4 %copy-start.17 = (f32[256]{0:T(256)}, f32[256]{0:T(256)S(1)}, u32[]{:S(2)}) copy-start(f32[256]{0:T(256)S(1)} %add_rsqrt_fusion) | copy-start | bytes 3076
  59.8 8.9 %slice-start.2 = ((s8[14155776]{0:T(1024)(128)(4,1)}), s8[4194304]{0:T(1024)(128)(4,1)S(1)}, s32[]{:S(2)}) async-start(s8[14155776]{0:T(1024)(128)(4,1)} %bitcast.195), calls=%async_computation.2 | async-start | bytes 8388608
  63.2 5.5 %slice-start.3 = ((s8[14155776]{0:T(1024)(128)(4,1)}), s8[4194304]{0:T(1024)(128)(4,1)S(1)}, s32[]{:S(2)}) async-start(s8[14155776]{0:T(1024)(128)(4,1)} %bitcast.195), calls=%async_computation.3 | async-start | bytes 8388608
  67.1 42.2 %collective-permute-start = (bf16[1,256,768]{2,1,0:T(8,128)(2,1)S(1)}, bf16[1,256,768]{2,1,0:T(8,128)(2,1)}, u32[]{:S(2)}, u32[]{:S(2)}) collective-permute-start(bf16[1,256,768]{2,1,0:T(8,128)(2,1)S(1)} %fusion.77), channel_id=1, source_target_pairs={{0,8},{4,12},{8,0},{12,4},{1,9},{5,13},{9,1},{13,5},{2,10},{6,14},... | collective-permute-start | bytes 1179656 | tf_op jit(solution)/shard_map/ppermute | solution.py:369
  70.1 40.3 %collective-permute-start.2 = (bf16[1,256,768]{2,1,0:T(8,128)(2,1)S(1)}, bf16[1,256,768]{2,1,0:T(8,128)(2,1)}, u32[]{:S(2)}, u32[]{:S(2)}) collective-permute-start(bf16[1,256,768]{2,1,0:T(8,128)(2,1)S(1)} %fusion.74), channel_id=1, source_target_pairs={{0,8},{4,12},{8,0},{12,4},{1,9},{5,13},{9,1},{13,5},{2,10},{6,14},... | collective-permute-start | bytes 1179656 | tf_op jit(solution)/shard_map/ppermute | solution.py:369
  71.7 57.8 %collective-permute-start.13 = (bf16[256,1536]{1,0:T(8,128)(2,1)}, bf16[256,1536]{1,0:T(8,128)(2,1)}, u32[]{:S(2)}, u32[]{:S(2)}) collective-permute-start(bf16[256,1536]{1,0:T(8,128)(2,1)} %slice.375), channel_id=1, source_target_pairs={{0,16},{1,17},{2,18},{3,19},{4,20},{5,21},{6,22},{7,23},{8,24},{9,... | collective-permute-start | bytes 2359304 | tf_op jit(solution)/shard_map/ppermute | solution.py:417
  110.4 21.3 %collective-permute-start.1 = (bf16[2,256,768]{2,1,0:T(8,128)(2,1)S(1)}, bf16[2,256,768]{2,1,0:T(8,128)(2,1)S(1)}, u32[]{:S(2)}, u32[]{:S(2)}) collective-permute-start(bf16[2,256,768]{2,1,0:T(8,128)(2,1)S(1)} %pad_maximum_fusion.6), channel_id=1, source_target_pairs={{0,4},{4,0},{8,12},{12,8},{1,5},{5,1},{9,13},{13,9},{2,6},{6,2},{1... | collective-permute-start | bytes 2359304 | tf_op jit(solution)/shard_map/ppermute | solution.py:369
  111.5 21.3 %collective-permute-start.3 = (bf16[2,256,768]{2,1,0:T(8,128)(2,1)S(1)}, bf16[2,256,768]{2,1,0:T(8,128)(2,1)S(1)}, u32[]{:S(2)}, u32[]{:S(2)}) collective-permute-start(bf16[2,256,768]{2,1,0:T(8,128)(2,1)S(1)} %pad_maximum_fusion.7), channel_id=1, source_target_pairs={{0,4},{4,0},{8,12},{12,8},{1,5},{5,1},{9,13},{13,9},{2,6},{6,2},{1... | collective-permute-start | bytes 2359304 | tf_op jit(solution)/shard_map/ppermute | solution.py:369
  112.1 18.1 %slice-start.4 = ((s8[4718592]{0:T(1024)(128)(4,1)}), s8[524288]{0:T(1024)(128)(4,1)S(1)}, s32[]{:S(2)}) async-start(s8[4718592]{0:T(1024)(128)(4,1)} %bitcast.204), calls=%async_computation.4 | async-start | bytes 1048576
  125.6 4.6 %slice-start.5 = ((s8[4718592]{0:T(1024)(128)(4,1)}), s8[4194304]{0:T(1024)(128)(4,1)S(1)}, s32[]{:S(2)}) async-start(s8[4718592]{0:T(1024)(128)(4,1)} %bitcast.204), calls=%async_computation.5 | async-start | bytes 8388608
  126.6 94.5 %collective-permute-start.28 = (bf16[256,768]{1,0:T(8,128)(2,1)}, bf16[256,768]{1,0:T(8,128)(2,1)S(1)}, u32[]{:S(2)}, u32[]{:S(2)}) collective-permute-start(bf16[256,768]{1,0:T(8,128)(2,1)} %get-tuple-element.70), channel_id=1, source_target_pairs={{0,8},{4,12},{8,0},{12,4},{1,9},{5,13},{9,1},{13,5},{2,10},{6,14},... | collective-permute-start | bytes 1179656 | tf_op jit(solution)/shard_map/ppermute | solution.py:369
  128.1 109.2 %collective-permute-start.10 = (bf16[256,1536]{1,0:T(8,128)(2,1)S(1)}, bf16[256,1536]{1,0:T(8,128)(2,1)S(1)}, u32[]{:S(2)}, u32[]{:S(2)}) collective-permute-start(bf16[256,1536]{1,0:T(8,128)(2,1)S(1)} %slice.361), channel_id=1, source_target_pairs={{0,16},{1,17},{2,18},{3,19},{4,20},{5,21},{6,22},{7,23},{8,24},{9,... | collective-permute-start | bytes 2359304 | tf_op jit(solution)/shard_map/ppermute | solution.py:417
  129.6 93.9 %collective-permute-start.14 = (bf16[256,768]{1,0:T(8,128)(2,1)S(1)}, bf16[256,768]{1,0:T(8,128)(2,1)S(1)}, u32[]{:S(2)}, u32[]{:S(2)}) collective-permute-start(bf16[256,768]{1,0:T(8,128)(2,1)S(1)} %get-tuple-element.82), channel_id=1, source_target_pairs={{0,8},{4,12},{8,0},{12,4},{1,9},{5,13},{9,1},{13,5},{2,10},{6,14},... | collective-permute-start | bytes 1179656 | tf_op jit(solution)/shard_map/ppermute | solution.py:369
  152.6 1.9 copy-start
  206.8 1.8 copy-start.1
  208.7 18.0 %collective-permute-start.7 = (bf16[256,768]{1,0:T(8,128)(2,1)S(1)}, bf16[256,768]{1,0:T(8,128)(2,1)S(1)}, u32[]{:S(2)}, u32[]{:S(2)}) collective-permute-start(bf16[256,768]{1,0:T(8,128)(2,1)S(1)} %add_convert_fusion.1), channel_id=1, source_target_pairs={{0,16},{1,17},{2,18},{3,19},{4,20},{5,21},{6,22},{7,23},{8,24},{9,... | collective-permute-start | bytes 1179656 | tf_op jit(solution)/shard_map/ppermute | solution.py:413
  213.6 2.0 copy-start.12
  213.7 2.0 copy-start.13
  213.7 2.0 copy-start.14
  213.7 2.0 copy-start.15
  213.7 18.4 %slice-start.6 = ((s8[4718592]{0:T(1024)(128)(4,1)}), s8[4194304]{0:T(1024)(128)(4,1)S(1)}, s32[]{:S(2)}) async-start(s8[4718592]{0:T(1024)(128)(4,1)} %bitcast.206), calls=%async_computation.6 | async-start | bytes 8388608
  215.7 16.5 %slice-start.7 = ((s8[4718592]{0:T(1024)(128)(4,1)}), s8[524288]{0:T(1024)(128)(4,1)S(1)}, s32[]{:S(2)}) async-start(s8[4718592]{0:T(1024)(128)(4,1)} %bitcast.206), calls=%async_computation.7 | async-start | bytes 1048576
  219.1 4.4 %copy-start.19 = (f32[8]{0:T(128)S(1)}, f32[8]{0:T(128)}, u32[]{:S(2)}) copy-start(f32[8]{0:T(128)} %pad.46.clone) | copy-start | bytes 100
  219.8 14.7 %collective-permute-start.8 = (bf16[256,768]{1,0:T(8,128)(2,1)S(1)}, bf16[256,768]{1,0:T(8,128)(2,1)S(1)}, u32[]{:S(2)}, u32[]{:S(2)}) collective-permute-start(bf16[256,768]{1,0:T(8,128)(2,1)S(1)} %get-tuple-element.25), channel_id=1, source_target_pairs={{0,16},{1,17},{2,18},{3,19},{4,20},{5,21},{6,22},{7,23},{8,24},{9,... | collective-permute-start | bytes 1179656 | tf_op jit(solution)/shard_map/ppermute | solution.py:413
  221.1 18.3 %collective-permute-start.9 = (bf16[256,768]{1,0:T(8,128)(2,1)S(1)}, bf16[256,768]{1,0:T(8,128)(2,1)S(1)}, u32[]{:S(2)}, u32[]{:S(2)}) collective-permute-start(bf16[256,768]{1,0:T(8,128)(2,1)S(1)} %get-tuple-element.28), channel_id=1, source_target_pairs={{0,16},{1,17},{2,18},{3,19},{4,20},{5,21},{6,22},{7,23},{8,24},{9,... | collective-permute-start | bytes 1179656 | tf_op jit(solution)/shard_map/ppermute | solution.py:413
  223.5 74.4 %collective-permute-start.6 = (bf16[128,768]{1,0:T(8,128)(2,1)}, bf16[128,768]{1,0:T(8,128)(2,1)S(1)}, u32[]{:S(2)}, u32[]{:S(2)}) collective-permute-start(bf16[128,768]{1,0:T(8,128)(2,1)} %slice.344), channel_id=1, source_target_pairs={{16,0},{17,1},{18,2},{19,3},{20,4},{21,5},{22,6},{23,7},{24,8},{25... | collective-permute-start | bytes 589832 | tf_op jit(solution)/shard_map/ppermute | solution.py:502
  226.8 70.1 %collective-permute-start.18 = (bf16[256,768]{1,0:T(8,128)(2,1)}, bf16[256,768]{1,0:T(8,128)(2,1)}, u32[]{:S(2)}, u32[]{:S(2)}) collective-permute-start(bf16[256,768]{1,0:T(8,128)(2,1)} %get-tuple-element.77), channel_id=1, source_target_pairs={{0,16},{1,17},{2,18},{3,19},{4,20},{5,21},{6,22},{7,23},{8,24},{9,... | collective-permute-start | bytes 1179656 | tf_op jit(solution)/shard_map/ppermute | solution.py:413
  234.4 62.4 %collective-permute-start.21 = (bf16[256,768]{1,0:T(8,128)(2,1)}, bf16[256,768]{1,0:T(8,128)(2,1)}, u32[]{:S(2)}, u32[]{:S(2)}) collective-permute-start(bf16[256,768]{1,0:T(8,128)(2,1)} %get-tuple-element.78), channel_id=1, source_target_pairs={{0,16},{1,17},{2,18},{3,19},{4,20},{5,21},{6,22},{7,23},{8,24},{9,... | collective-permute-start | bytes 1179656 | tf_op jit(solution)/shard_map/ppermute | solution.py:413
  237.3 78.1 %collective-permute-start.30 = (bf16[256,768]{1,0:T(8,128)(2,1)S(1)}, bf16[256,768]{1,0:T(8,128)(2,1)}, u32[]{:S(2)}, u32[]{:S(2)}) collective-permute-start(bf16[256,768]{1,0:T(8,128)(2,1)S(1)} %broadcast_select_fusion.16), channel_id=1, source_target_pairs={{0,8},{4,12},{8,0},{12,4},{1,9},{5,13},{9,1},{13,5},{2,10},{6,14},... | collective-permute-start | bytes 1179656 | tf_op jit(solution)/shard_map/ppermute | solution.py:369
  240.4 54.8 %copy-start.4 = (bf16[256,768]{1,0:T(8,128)(2,1)S(1)}, bf16[256,768]{1,0:T(8,128)(2,1)}, u32[]{:S(2)}) copy-start(bf16[256,768]{1,0:T(8,128)(2,1)} %param.15) | copy-start | bytes 1179652
  240.4 54.8 %copy-start.16 = (f32[768]{0:T(1024)S(1)}, f32[768]{0:T(1024)}, u32[]{:S(2)}) copy-start(f32[768]{0:T(1024)} %add_reduce_fusion) | copy-start | bytes 9220
  240.4 54.8 %copy-start.18 = (f32[256]{0:T(256)S(1)}, f32[256]{0:T(256)}, u32[]{:S(2)}) copy-start(f32[256]{0:T(256)} %copy-done.17) | copy-start | bytes 3076
  296.7 5.6 %copy-start.2 = (bf16[256,1536]{1,0:T(8,128)(2,1)S(1)}, bf16[256,1536]{1,0:T(8,128)(2,1)}, u32[]{:S(2)}) copy-start(bf16[256,1536]{1,0:T(8,128)(2,1)} %slice_select_fusion.2) | copy-start | bytes 2359300
  296.8 9.0 %collective-permute-start.12 = (bf16[128,768]{1,0:T(8,128)(2,1)S(1)}, bf16[128,768]{1,0:T(8,128)(2,1)S(1)}, u32[]{:S(2)}, u32[]{:S(2)}) collective-permute-start(bf16[128,768]{1,0:T(8,128)(2,1)S(1)} %select_convert_fusion), channel_id=1, source_target_pairs={{0,16},{16,0},{1,17},{17,1},{2,18},{18,2},{3,19},{19,3},{4,20},{20... | collective-permute-start | bytes 589832 | tf_op jit(solution)/shard_map/ppermute | solution.py:410
  297.0 7.9 %copy-start.6 = (bf16[256,768]{1,0:T(8,128)(2,1)S(1)}, bf16[256,768]{1,0:T(8,128)(2,1)}, u32[]{:S(2)}) copy-start(bf16[256,768]{1,0:T(8,128)(2,1)} %broadcast_select_fusion.14) | copy-start | bytes 1179652
  297.0 7.8 %collective-permute-start.19 = (bf16[256,768]{1,0:T(8,128)(2,1)S(1)}, bf16[256,768]{1,0:T(8,128)(2,1)S(1)}, u32[]{:S(2)}, u32[]{:S(2)}) collective-permute-start(bf16[256,768]{1,0:T(8,128)(2,1)S(1)} %get-tuple-element.75), channel_id=1, source_target_pairs={{0,8},{4,12},{8,0},{12,4},{1,9},{5,13},{9,1},{13,5},{2,10},{6,14},... | collective-permute-start | bytes 1179656 | tf_op jit(solution)/shard_map/ppermute | solution.py:369
  298.0 9.0 %collective-permute-start.11 = (bf16[128,768]{1,0:T(8,128)(2,1)S(1)}, bf16[128,768]{1,0:T(8,128)(2,1)S(1)}, u32[]{:S(2)}, u32[]{:S(2)}) collective-permute-start(bf16[128,768]{1,0:T(8,128)(2,1)S(1)} %add_convert_fusion.3), channel_id=1, source_target_pairs={{0,16},{16,0},{1,17},{17,1},{2,18},{18,2},{3,19},{19,3},{4,20},{20... | collective-permute-start | bytes 589832 | tf_op jit(solution)/shard_map/ppermute | solution.py:410
  301.1 4.6 %copy-start.5 = (bf16[256,768]{1,0:T(8,128)(2,1)S(1)}, bf16[256,768]{1,0:T(8,128)(2,1)}, u32[]{:S(2)}) copy-start(bf16[256,768]{1,0:T(8,128)(2,1)} %broadcast_select_fusion.15) | copy-start | bytes 1179652
  301.1 7.9 %collective-permute-start.22 = (bf16[256,768]{1,0:T(8,128)(2,1)S(1)}, bf16[256,768]{1,0:T(8,128)(2,1)S(1)}, u32[]{:S(2)}, u32[]{:S(2)}) collective-permute-start(bf16[256,768]{1,0:T(8,128)(2,1)S(1)} %get-tuple-element.76), channel_id=1, source_target_pairs={{0,8},{4,12},{8,0},{12,4},{1,9},{5,13},{9,1},{13,5},{2,10},{6,14},... | collective-permute-start | bytes 1179656 | tf_op jit(solution)/shard_map/ppermute | solution.py:369
  304.8 10.6 %collective-permute-start.16 = (bf16[256,768]{1,0:T(8,128)(2,1)S(1)}, bf16[256,768]{1,0:T(8,128)(2,1)S(1)}, u32[]{:S(2)}, u32[]{:S(2)}) collective-permute-start(bf16[256,768]{1,0:T(8,128)(2,1)S(1)} %copy-done.6), channel_id=1, source_target_pairs={{0,8},{4,12},{8,0},{12,4},{1,9},{5,13},{9,1},{13,5},{2,10},{6,14},... | collective-permute-start | bytes 1179656 | tf_op jit(solution)/shard_map/ppermute | solution.py:369
  305.8 15.9 %collective-permute-start.26 = (bf16[256,768]{1,0:T(8,128)(2,1)S(1)}, bf16[256,768]{1,0:T(8,128)(2,1)S(1)}, u32[]{:S(2)}, u32[]{:S(2)}) collective-permute-start(bf16[256,768]{1,0:T(8,128)(2,1)S(1)} %copy-done.5), channel_id=1, source_target_pairs={{0,8},{4,12},{8,0},{12,4},{1,9},{5,13},{9,1},{13,5},{2,10},{6,14},... | collective-permute-start | bytes 1179656 | tf_op jit(solution)/shard_map/ppermute | solution.py:369
  307.0 20.7 %collective-permute-start.20 = (bf16[512,768]{1,0:T(8,128)(2,1)S(1)}, bf16[512,768]{1,0:T(8,128)(2,1)S(1)}, u32[]{:S(2)}, u32[]{:S(2)}) collective-permute-start(bf16[512,768]{1,0:T(8,128)(2,1)S(1)} %pad_maximum_fusion.12), channel_id=1, source_target_pairs={{0,4},{4,0},{8,12},{12,8},{1,5},{5,1},{9,13},{13,9},{2,6},{6,2},{1... | collective-permute-start | bytes 2359304 | tf_op jit(solution)/shard_map/ppermute | solution.py:369
  309.0 16.9 %collective-permute-start.24 = (bf16[256,768]{1,0:T(8,128)(2,1)S(1)}, bf16[256,768]{1,0:T(8,128)(2,1)S(1)}, u32[]{:S(2)}, u32[]{:S(2)}) collective-permute-start(bf16[256,768]{1,0:T(8,128)(2,1)S(1)} %get-tuple-element.74), channel_id=1, source_target_pairs={{0,8},{4,12},{8,0},{12,4},{1,9},{5,13},{9,1},{13,5},{2,10},{6,14},... | collective-permute-start | bytes 1179656 | tf_op jit(solution)/shard_map/ppermute | solution.py:369
  310.1 11.5 %copy-start.10 = (bf16[512,384]{1,0:T(8,128)(2,1)S(1)}, bf16[512,384]{1,0:T(8,128)(2,1)}, u32[]{:S(2)}) copy-start(bf16[512,384]{1,0:T(8,128)(2,1)} %get-tuple-element.80) | copy-start | bytes 1179652
  315.4 13.2 %collective-permute-start.23 = (bf16[512,768]{1,0:T(8,128)(2,1)S(1)}, bf16[512,768]{1,0:T(8,128)(2,1)S(1)}, u32[]{:S(2)}, u32[]{:S(2)}) collective-permute-start(bf16[512,768]{1,0:T(8,128)(2,1)S(1)} %pad_maximum_fusion.13), channel_id=1, source_target_pairs={{0,4},{4,0},{8,12},{12,8},{1,5},{5,1},{9,13},{13,9},{2,6},{6,2},{1... | collective-permute-start | bytes 2359304 | tf_op jit(solution)/shard_map/ppermute | solution.py:369
  315.4 14.6 %collective-permute-start.17 = (bf16[512,768]{1,0:T(8,128)(2,1)S(1)}, bf16[512,768]{1,0:T(8,128)(2,1)S(1)}, u32[]{:S(2)}, u32[]{:S(2)}) collective-permute-start(bf16[512,768]{1,0:T(8,128)(2,1)S(1)} %pad_maximum_fusion.11), channel_id=1, source_target_pairs={{0,4},{4,0},{8,12},{12,8},{1,5},{5,1},{9,13},{13,9},{2,6},{6,2},{1... | collective-permute-start | bytes 2359304 | tf_op jit(solution)/shard_map/ppermute | solution.py:369
  321.7 5.4 %collective-permute-start.15 = (bf16[512,384]{1,0:T(8,128)(2,1)S(1)}, bf16[512,384]{1,0:T(8,128)(2,1)S(1)}, u32[]{:S(2)}, u32[]{:S(2)}) collective-permute-start(bf16[512,384]{1,0:T(8,128)(2,1)S(1)} %copy-done.10), channel_id=1, source_target_pairs={{0,4},{4,0},{8,12},{12,8},{1,5},{5,1},{9,13},{13,9},{2,6},{6,2},{1... | collective-permute-start | bytes 1179656 | tf_op jit(solution)/shard_map/ppermute | solution.py:369
  321.7 6.0 %copy-start.9 = (bf16[512,384]{1,0:T(8,128)(2,1)S(1)}, bf16[512,384]{1,0:T(8,128)(2,1)}, u32[]{:S(2)}) copy-start(bf16[512,384]{1,0:T(8,128)(2,1)} %get-tuple-element.79) | copy-start | bytes 1179652
  325.9 5.0 %collective-permute-start.27 = (bf16[512,768]{1,0:T(8,128)(2,1)S(1)}, bf16[512,768]{1,0:T(8,128)(2,1)S(1)}, u32[]{:S(2)}, u32[]{:S(2)}) collective-permute-start(bf16[512,768]{1,0:T(8,128)(2,1)S(1)} %pad_maximum_fusion.14), channel_id=1, source_target_pairs={{0,4},{4,0},{8,12},{12,8},{1,5},{5,1},{9,13},{13,9},{2,6},{6,2},{1... | collective-permute-start | bytes 2359304 | tf_op jit(solution)/shard_map/ppermute | solution.py:369
  327.1 3.7 %collective-permute-start.25 = (bf16[512,384]{1,0:T(8,128)(2,1)S(1)}, bf16[512,384]{1,0:T(8,128)(2,1)S(1)}, u32[]{:S(2)}, u32[]{:S(2)}) collective-permute-start(bf16[512,384]{1,0:T(8,128)(2,1)S(1)} %get-tuple-element.72), channel_id=1, source_target_pairs={{0,4},{4,0},{8,12},{12,8},{1,5},{5,1},{9,13},{13,9},{2,6},{6,2},{1... | collective-permute-start | bytes 1179656 | tf_op jit(solution)/shard_map/ppermute | solution.py:369
  327.7 7.1 %collective-permute-start.31 = (bf16[512,768]{1,0:T(8,128)(2,1)S(1)}, bf16[512,768]{1,0:T(8,128)(2,1)S(1)}, u32[]{:S(2)}, u32[]{:S(2)}) collective-permute-start(bf16[512,768]{1,0:T(8,128)(2,1)S(1)} %pad_maximum_fusion.15), channel_id=1, source_target_pairs={{0,4},{4,0},{8,12},{12,8},{1,5},{5,1},{9,13},{13,9},{2,6},{6,2},{1... | collective-permute-start | bytes 2359304 | tf_op jit(solution)/shard_map/ppermute | solution.py:369
  327.8 1.0 copy-start.8
  328.8 6.0 %collective-permute-start.29 = (bf16[512,384]{1,0:T(8,128)(2,1)S(1)}, bf16[512,384]{1,0:T(8,128)(2,1)S(1)}, u32[]{:S(2)}, u32[]{:S(2)}) collective-permute-start(bf16[512,384]{1,0:T(8,128)(2,1)S(1)} %copy-done.8), channel_id=1, source_target_pairs={{0,4},{4,0},{8,12},{12,8},{1,5},{5,1},{9,13},{13,9},{2,6},{6,2},{1... | collective-permute-start | bytes 1179656 | tf_op jit(solution)/shard_map/ppermute | solution.py:369
  332.7 2.0 copy-start.7

commit v4 on v3

--- a/solution.py
+++ b/solution.py
@@ -40,13 +40,16 @@
     greet(others(me, n))
     group = lax.axis_index("group")
 
+    def part(number, block):
+        width = ins[number].shape[1]
+        return outs[number].at[:, pl.ds(pl.multiple_of(block * width, 128), width)]
+
     def copy_of(number, block, way):
-        x, out = ins[number], outs[number]
         send, recv = sems[3 * number : 3 * number + 2]
         side = 0 if way > 0 else 1
         return pltpu.make_async_remote_copy(
-            src_ref=out.at[block],
-            dst_ref=out.at[block],
+            src_ref=part(number, block),
+            dst_ref=part(number, block),
             send_sem=send.at[side, block],
             recv_sem=recv.at[side, block],
             device_id={"head": me + way},
@@ -54,12 +57,11 @@
         )
 
     def own_copy(number, way):
-        x, out = ins[number], outs[number]
         send, recv = sems[3 * number : 3 * number + 2]
         side = 0 if way > 0 else 1
         return pltpu.make_async_remote_copy(
-            src_ref=x,
-            dst_ref=out.at[me],
+            src_ref=ins[number],
+            dst_ref=part(number, me),
             send_sem=send.at[side, me],
             recv_sem=recv.at[side, me],
             device_id={"head": me + way},
@@ -74,7 +76,7 @@
             pl.when(group == source)(work)
 
     def local_copy(number):
-        return pltpu.make_async_copy(ins[number], outs[number].at[me], sems[3 * number + 2])
+        return pltpu.make_async_copy(ins[number], part(number, me), sems[3 * number + 2])
 
     def begin(number):
         pl.when(me < n - 1)(lambda: own_copy(number, 1).start())
@@ -127,7 +129,7 @@
     sent = sum(x.size * x.dtype.itemsize for x in arrays)
     return pl.pallas_call(
         functools.partial(line_gather_kernel, n, tuple(source for x, source in wants)),
-        out_shape=[jax.ShapeDtypeStruct((n,) + x.shape, x.dtype) for x in arrays],
+        out_shape=[jax.ShapeDtypeStruct((x.shape[0], n * x.shape[1]), x.dtype) for x in arrays],
         in_specs=[pl.BlockSpec(memory_space=pl.ANY)] * len(arrays),
         out_specs=[pl.BlockSpec(memory_space=pl.ANY)] * len(arrays),
         scratch_shapes=scratch,
@@ -150,6 +152,7 @@
     me = lax.axis_index("head")
     greet(others(me, n), [row_partner(bit) for bit in bits])
     f32 = jnp.float32
+    width = total.shape[1]
 
     def key_copy(stage):
         size = 1 << (len(bits) - 1 - stage)
@@ -192,6 +195,9 @@
         extra_own = pltpu.make_async_copy(extra, extras.at[me], extra_local)
         extra_own.start()
 
+    def part(block):
+        return x[:, pl.ds(pl.multiple_of(block * width, 128), width)]
+
     def copy_of(side, block):
         return pltpu.make_async_remote_copy(
             src_ref=sends.at[side, block],
@@ -209,25 +215,25 @@
         def _():
             copy.wait_recv()
             sends[side, block] = (
-                x[block].astype(f32) + recvs[side, block].astype(f32)
+                part(block).astype(f32) + recvs[side, block].astype(f32)
             ).astype(sends.dtype)
 
         @pl.when(jnp.logical_not(inner))
         def _():
-            sends[side, block] = x[block]
+            sends[side, block] = part(block)
 
         copy.start()
 
     for step in range(n - 1):
-        high, low = n - 1 - step, step
-        pl.when(me < high)(lambda: pass_on(0, high, me > 0))
-        pl.when(me > low)(lambda: pass_on(1, low, me < n - 1))
+        high, low = n - 1 + me - step, step + me - (n - 1)
+        pl.when(me <= step)(functools.partial(pass_on, 0, high, me > 0))
+        pl.when(low >= 0)(functools.partial(pass_on, 1, low, me < n - 1))
         if step == 0:
             for stage in range(len(bits) - 1):
                 key_add(stage)
                 key_copy(stage + 1).start()
 
-    total[...] = x[me].astype(f32)
+    total[...] = part(me).astype(f32)
 
     @pl.when(me > 0)
     def _():
@@ -263,14 +269,15 @@
 
 
 def line_sum(number, name, x, extra=None, keyed=None):
-    n, block = x.shape[0], x.shape[1:]
+    n = lax.axis_size("head")
+    block = (x.shape[0], x.shape[1] // n)
     small = extra is not None
     bits = row_bits()[::-1] if keyed is not None else []
     arrays = [x] + [array for array in (extra, keyed) if array is not None]
     shapes = [jax.ShapeDtypeStruct(block, jnp.float32)]
     scratch = [
-        pltpu.VMEM((2,) + x.shape, x.dtype),
-        pltpu.VMEM((2,) + x.shape, x.dtype),
+        pltpu.VMEM((2, n) + block, x.dtype),
+        pltpu.VMEM((2, n) + block, x.dtype),
         pltpu.SemaphoreType.DMA((2, n)),
         pltpu.SemaphoreType.DMA((2, n)),
     ]
@@ -403,9 +410,6 @@
     scale_dev = lax.dynamic_slice_in_dim(scale, head_pos * width, width, 0)
     w_qkv, w_out = qkv_weight[0], out_weight[0]
 
-    def widen(blocks):
-        return jnp.concatenate([blocks[index] for index in range(n_head)], axis=1)
-
     def swap(x):
         return lax.ppermute(x, "group", [(0, 1), (1, 0)])
 
@@ -417,23 +421,17 @@
         return jnp.where(control, x[:, :cols], lax.ppermute(x[:, cols:], "group", [(0, 1)]))
 
     def head_terms(x, weight):
-        return jnp.stack(
-            [
-                dot(x, weight[index * width : (index + 1) * width], ((1,), (1,))).astype(bf16)
-                for index in range(n_head)
-            ]
-        )
+        return dot(x, weight, ((1,), (1,))).astype(bf16)
 
     summed = (latent.astype(f32) + hint.astype(f32)).astype(bf16)
     inputs = jnp.where(control, summed, latent)
     cot_own = jnp.where(control, cotangent[:half], cotangent[half:])
     cot_half, whole = line_gather(0, "gather_inputs", (cot_own, None), (inputs, None))
-    cot_half = widen(cot_half)
     hint_half = dot(cot_half, zero_weight, ((1,), (0,))).astype(bf16)
     hint_other = swap(hint_half)
     cot_other = swap(cot_half)
 
-    whole_f = widen(whole).astype(f32)
+    whole_f = whole.astype(f32)
     mean = jnp.mean(whole_f, axis=-1, keepdims=True)
     centred = whole_f - mean
     var = jnp.mean(centred * centred, axis=-1, keepdims=True)
@@ -449,15 +447,14 @@
     hint_back = jnp.concatenate([hint_half, hint_other])
     incoming = jnp.where(control, hint_back, cotangent)
     gated = (gate_dev * hint_back.astype(f32)).astype(bf16)
-    (gated_blocks,) = line_gather(1, "gather_gated", (gated, 0))
-    cot_full = jnp.where(
-        control,
-        jnp.concatenate([cot_half, cot_other]),
-        jnp.concatenate([cot_other, cot_half]),
-    )
+    (gated_full,) = line_gather(1, "gather_gated", (gated, 0))
+    cot_full = jnp.concatenate(
+        [jnp.where(control, cot_half, cot_other), jnp.where(control, cot_other, cot_half)]
+    )
+    cot_full = lax.optimization_barrier(cot_full)
     gated_main = (gate * cot_full.astype(f32)).astype(bf16)
     gated_full = lax.optimization_barrier(
-        jnp.where(control, widen(gated_blocks), gated_main)
+        jnp.where(control, gated_full, gated_main)
     )
     attn_grad = dot(gated_full, w_out, ((1,), (0,))).astype(bf16)
     attn, dquery, key_terms = attention(query, all_keys, all_values, attn_grad)
@@ -468,15 +465,12 @@
     dkey, dval = dkv[0], dkv[1]
     grads = [dquery, dkey, dval]
 
-    scaled_nhat = nhat * (1.0 + scale)
-    terms = []
-    first, second = 0.0, 0.0
-    for index in range(n_head):
-        cols = slice(index * width, (index + 1) * width)
-        term = sum(dot(grads[c], w_qkv[c, cols], ((1,), (1,))) for c in range(3))
-        first = first + jnp.sum(term * (1.0 + scale[cols]), axis=-1)
-        second = second + jnp.sum(term * scaled_nhat[:, cols], axis=-1)
-        terms.append(term.astype(bf16))
+    terms = sum(dot(grads[c], w_qkv[c], ((1,), (1,))) for c in range(3))
+    terms = lax.optimization_barrier(terms)
+    scaled_terms = terms * (1.0 + scale)
+    first = jnp.sum(scaled_terms, axis=-1)
+    second = jnp.sum(scaled_terms * nhat, axis=-1)
+    terms = terms.astype(bf16)
     sums = jnp.concatenate([first[None], second[None], jnp.zeros((6, tok), f32)])
     state_half = jnp.where(control, near_state[:half], near_state[half:])
     hint_terms = head_terms(state_half, zero_weight)
@@ -484,7 +478,7 @@
     terms, hint_terms, near_attn, near_query, near_gated = lax.optimization_barrier(
         (terms, hint_terms, near_attn, near_query, near_gated)
     )
-    both = jnp.concatenate([jnp.stack(terms), hint_terms], axis=1)
+    both = jnp.concatenate([terms, hint_terms])
     both, sum_parts = line_sum(3, "sum_norm_hint", both, sums)
     dnorm, projected = both[:tok], both[tok:]
     sums = jnp.sum(sum_parts, axis=0) / full_width

time: 339 us -> 307 us (0.906)
  Pallas kernels: 175 us -> 151 us
  waiting for transfers between devices: 17.8 us -> 31.9 us
  other arithmetic: 46.2 us -> 37.7 us
  matrix products: 51.5 us -> 44.2 us
  starting transfers between devices: 36.3 us -> 32.6 us
    pallas_call x2, Pallas kernels: 94.5 us -> 70.4 us  [line_sum(): pl.pallas_call(functools.partial(line_sum_kernel, n, small, tuple(bits)),...]
    ppermute x5, waiting for transfers between devices: 0.01 us -> 17 us  [near(): return jnp.where(control, x, lax.ppermute(x, 'group', [(0, 1)]))]
    select_n x2, other arithmetic: 13.6 us -> 1.92 us  [the longest x1 1.34 us: on_device(): jnp.where(control, cot_half, cot_other)]
    dot_general x30 -> x15, matrix products: 51.5 us -> 44.2 us  [dot(): lax.dot_general(a, b, (dims, ((), ())), preferred_element_type=jnp.float32)]
    ppermute x20, waiting for transfers between devices: 17.8 us -> 12 us  [row_swap(): lax.ppermute(x, 'row', [(row, row ^ bit) for row in range(lax.axis_size('...]
    ppermute x5, starting transfers between devices: 11.3 us -> 6.92 us  [near(): return jnp.where(control, x, lax.ppermute(x, 'group', [(0, 1)]))]
    convert_element_type x1 -> x0, other arithmetic: 3.42 us -> none  [on_device(): normed = (nhat * (1.0 + scale) + shift).astype(bf16)]
  transfers between devices with their start and end apart: 32 -> 32, of which waited for: 5 -> 9; matrix products, arithmetic and copies ran while one was open for 27% -> 26% of each run, Pallas kernels for 39% -> 35%
where the time goes in v4:
time: 307 us; the launch traced here: 305 us
  Pallas kernels  151 us (49%)
  matrix products  44.2 us (14%)
  other arithmetic  37.7 us (12%)
  starting transfers between devices  32.6 us (11%)
  waiting for transfers between devices  31.9 us (10%)
  local copies, waits for them, and re-layouts  5.66 us (2%)
    pallas_call x2, Pallas kernels, line_gather(): pl.pallas_call(functools.partial(line_gather_kernel, n, tuple((source for...  70.5 us
    pallas_call x2, Pallas kernels, line_sum(): pl.pallas_call(functools.partial(line_sum_kernel, n, small, tuple(bits)),...  70.4 us
    dot_general x15, matrix products, dot(): lax.dot_general(a, b, (dims, ((), ())), preferred_element_type=jnp.float32)  44.2 us
    ppermute x5, waiting for transfers between devices, near(): return jnp.where(control, x, lax.ppermute(x, 'group', [(0, 1)]))  17 us
    ppermute x20, starting transfers between devices, row_swap(): lax.ppermute(x, 'row', [(row, row ^ bit) for row in range(lax.axis_size('...  13 us
    ppermute x20, waiting for transfers between devices, row_swap(): lax.ppermute(x, 'row', [(row, row ^ bit) for row in range(lax.axis_size('...  12 us
    pallas_call x1, Pallas kernels, attention(): pl.pallas_call(attention_kernel, grid=(width // HD,), out_shape=[small, s...  10.3 us
    concatenate x9, other arithmetic, cube_gather(): x = jnp.concatenate([x, row_swap(x, bit)], axis=dim)  9.62 us
  transfers between devices with their start and end apart: 32, of which 9 were waited for; matrix products, arithmetic and copies ran while one was open for 26% of the time, Pallas kernels for 35%

profile of v4, /device:TPU:0, one launch (start us, length us, event | category | flops | bytes accessed | tf_op | source)
XLA Modules:
  0.0 305.5 jit_solution(5229030842806529046)
XLA Ops:
  0.6 1.7 slice_select_fusion.7.refs_0_
  2.4 2.1 fusion.98.refs_1_
  4.5 44.6 %gather_inputs.1 = (bf16[128,3072]{1,0:T(8,128)(2,1)}, bf16[256,3072]{1,0:T(8,128)(2,1)}) custom-call(bf16[128,768]{1,0:T(8,128)(2,1)} %slice_select_fusion.7.refs_0_, bf16[256,768]{1,0:T(8,128)(2,1)} %fusion.98.refs_1_), custom_call_target="tpu_custom_call" | custom-call | bytes 117964800 | tf_op jit(solution)/shard_map/gather_inputs/pallas_call | solution.py:130
  49.1 1.6 collective-permute-start.5
  50.7 4.0 %convolution_convert_fusion.1 = bf16[128,768]{1,0:T(8,128)(2,1)} fusion(bf16[128,3072]{1,0:T(8,128)(2,1)} %get-tuple-element.21, bf16[3072,768]{1,0:T(8,128)(2,1)} %param.14), kind=kOutput, calls=%fused_computation.80 | convolution fusion | flops 604078080 | bytes 5701632 | tf_op jit(solution)/shard_map/dot_general | solution.py:364
  57.6 2.6 fusion.31
  60.2 4.5 %fusion.86 = bf16[1,256,768]{2,1,0:T(8,128)(2,1)} fusion(bf16[256,3072]{1,0:T(8,128)(2,1)S(1)} %get-tuple-element.38, bf16[1,3,3072,768]{3,2,1,0:T(8,128)(2,1)} %param.12), kind=kOutput, calls=%fused_computation.78 | convolution fusion | flops 1208156160 | bytes 6684672 | tf_op jit(solution)/shard_map/dot_general | solution.py:364
  64.6 1.5 collective-permute-start.2
  66.1 4.5 %fusion.89 = bf16[1,256,768]{2,1,0:T(8,128)(2,1)} fusion(bf16[256,3072]{1,0:T(8,128)(2,1)S(1)} %get-tuple-element.38, bf16[1,3,3072,768]{3,2,1,0:T(8,128)(2,1)} %param.12), kind=kOutput, calls=%fused_computation.79 | convolution fusion | flops 1208156160 | bytes 6684672 | tf_op jit(solution)/shard_map/dot_general | solution.py:364
  72.1 4.3 %collective-permute-start.13 = (bf16[256,1536]{1,0:T(8,128)(2,1)}, bf16[256,1536]{1,0:T(8,128)(2,1)}, u32[]{:S(2)}, u32[]{:S(2)}) collective-permute-start(bf16[256,1536]{1,0:T(8,128)(2,1)} %slice.174), channel_id=1, source_target_pairs={{0,16},{1,17},{2,18},{3,19},{4,20},{5,21},{6,22},{7,23},{8,24},{9,... | collective-permute-start | bytes 2359304 | tf_op jit(solution)/shard_map/ppermute | solution.py:421
  76.4 3.7 %fusion.74.q_ref = bf16[256,768]{1,0:T(8,128)(2,1)S(1)} fusion(bf16[256,3072]{1,0:T(8,128)(2,1)S(1)} %get-tuple-element.38, bf16[1,3,3072,768]{3,2,1,0:T(8,128)(2,1)} %param.12), kind=kOutput, calls=%fused_computation.74 | convolution fusion | flops 1208156160 | bytes 6684672 | tf_op jit(solution)/shard_map/dot_general | solution.py:364
  81.4 1.3 add_reduce_fusion
  82.7 1.8 multiply_convert_fusion.1.refs_0_
  84.6 25.9 %gather_gated.1 = bf16[256,3072]{1,0:T(8,128)(2,1)} custom-call(bf16[256,768]{1,0:T(8,128)(2,1)} %multiply_convert_fusion.1.refs_0_), custom_call_target="tpu_custom_call" | custom-call | bytes 78643200 | tf_op jit(solution)/shard_map/gather_gated/pallas_call | solution.py:130
  110.5 1.3 pad_maximum_fusion.6
  111.9 1.2 pad_maximum_fusion.5
  113.6 1.3 broadcast_select_fusion.1
  115.1 1.3 copy-done.2
  117.9 1.5 collective-permute-start.28
  120.3 2.2 collective-permute-start.10
  123.2 1.4 fusion.83.g_ref
  124.7 2.4 pad_maximum_fusion.3.v_ref
  127.1 1.3 pad_maximum_fusion.2.k_ref
  128.4 10.3 %attention.1 = (bf16[256,768]{1,0:T(8,128)(2,1)S(1)}, bf16[256,768]{1,0:T(8,128)(2,1)S(1)}, bf16[4,2,256,768]{3,2,1,0:T(8,128)(2,1)}) custom-call(bf16[256,768]{1,0:T(8,128)(2,1)S(1)} %fusion.74.q_ref, bf16[4,256,768]{2,1,0:T(8,128)(2,1)S(1)} %pad_maximum_fusion.2.k_ref, bf16[4,256,768]{2,1,0:T(8,128)(2,1)} %pad_maximum_fusion.3.v_ref, ...), custom_call_target="tpu_custom_call" | custom-call | tf_op jit(solution)/shard_map/attention/pallas_call | solution.py:352
  138.7 3.9 %fusion.28.refs_0_ = bf16[256,3072]{1,0:T(8,128)(2,1)S(1)} fusion(bf16[256,768]{1,0:T(8,128)(2,1)S(1)} %get-tuple-element.22, bf16[1,3072,768]{2,1,0:T(8,128)(2,1)} %param.13), kind=kOutput, calls=%fused_computation.26 | convolution fusion | flops 1208745984 | bytes 6684672 | tf_op jit(solution)/shard_map/dot_general | solution.py:364
  142.6 29.8 %sum_branch.1 = (f32[256,768]{1,0:T(8,128)S(1)}, bf16[2,256,768]{2,1,0:T(8,128)(2,1)S(1)}) custom-call(bf16[256,3072]{1,0:T(8,128)(2,1)S(1)} %fusion.28.refs_0_, bf16[4,2,256,768]{3,2,1,0:T(8,128)(2,1)S(1)} %copy-done), custom_call_target="tpu_custom_call" | custom-call | bytes 78643200 | tf_op jit(solution)/shard_map/sum_branch/pallas_call | solution.py:299
  172.4 3.8 %fusion.4 = f32[256,3072]{1,0:T(8,128)S(1)} fusion(bf16[1,3,3072,768]{3,2,1,0:T(8,128)(2,1)} %param.12, bf16[2,256,768]{2,1,0:T(8,128)(2,1)S(1)} %get-tuple-element.26), kind=kOutput, calls=%fused_computation.4 | convolution fusion | flops 1207959552 | bytes 8257536 | tf_op jit(solution)/shard_map/dot_general | solution.py:364
  176.2 3.8 %fusion.8 = f32[256,3072]{1,0:T(8,128)S(1)} fusion(bf16[1,3,3072,768]{3,2,1,0:T(8,128)(2,1)} %param.12, bf16[2,256,768]{2,1,0:T(8,128)(2,1)S(1)} %get-tuple-element.26), kind=kOutput, calls=%fused_computation.8 | convolution fusion | flops 1207959552 | bytes 8257536 | tf_op jit(solution)/shard_map/dot_general | solution.py:364
  181.0 1.3 collective-permute-start.7
  182.4 1.3 collective-permute-start.9
  183.7 3.8 %fusion.25 = f32[256,3072]{1,0:T(8,128)S(1)} fusion(f32[256,3072]{1,0:T(8,128)S(1)} %fusion.4, f32[256,3072]{1,0:T(8,128)S(1)} %fusion.8, bf16[256,768]{1,0:T(8,128)(2,1)S(1)} %get-tuple-element.25, bf16[1,3,3072,768]{3,2,1,0:T(8,128)(2,1)} %param.12), kind=kOutput, calls=%fused_computation.25 | convolution fusion | flops 1209532416 | bytes 14548992 | tf_op jit(solution)/shard_map/dot_general | solution.py:364
  187.5 1.1 multiply_reduce_fusion.1
  188.7 1.4 collective-permute-start.8
  190.1 2.2 broadcast_select_fusion.9
  192.4 1.3 collective-permute-start.18
  193.7 1.0 broadcast_select_fusion.13
  194.7 1.5 collective-permute-start.21
  196.3 4.0 %collective-permute-done.9 = bf16[256,768]{1,0:T(8,128)(2,1)S(1)} collective-permute-done((bf16[256,768]{1,0:T(8,128)(2,1)S(1)}, bf16[256,768]{1,0:T(8,128)(2,1)S(1)}, u32[]{:S(2)}, u32[]{:S(2)}) %collective-permute-start.9) | collective-permute-done | bytes 393248 | tf_op jit(solution)/shard_map/ppermute | solution.py:417
  200.3 1.5 collective-permute-start.6
  202.6 1.5 collective-permute-start.30
  204.2 4.5 %collective-permute-done.8 = bf16[256,768]{1,0:T(8,128)(2,1)S(1)} collective-permute-done((bf16[256,768]{1,0:T(8,128)(2,1)S(1)}, bf16[256,768]{1,0:T(8,128)(2,1)S(1)}, u32[]{:S(2)}, u32[]{:S(2)}) %collective-permute-start.8) | collective-permute-done | bytes 393248 | tf_op jit(solution)/shard_map/ppermute | solution.py:417
  209.5 1.6 convolution_convert_fusion
  211.2 1.6 collective-permute-start.16
  212.7 4.3 %collective-permute-done.18 = bf16[256,768]{1,0:T(8,128)(2,1)S(1)} collective-permute-done((bf16[256,768]{1,0:T(8,128)(2,1)S(1)}, bf16[256,768]{1,0:T(8,128)(2,1)S(1)}, u32[]{:S(2)}, u32[]{:S(2)}) %collective-permute-start.18) | collective-permute-done | bytes 393248 | tf_op jit(solution)/shard_map/ppermute | solution.py:417
  217.0 4.2 %collective-permute-done.21 = bf16[256,768]{1,0:T(8,128)(2,1)S(1)} collective-permute-done((bf16[256,768]{1,0:T(8,128)(2,1)S(1)}, bf16[256,768]{1,0:T(8,128)(2,1)S(1)}, u32[]{:S(2)}, u32[]{:S(2)}) %collective-permute-start.21) | collective-permute-done | bytes 393248 | tf_op jit(solution)/shard_map/ppermute | solution.py:417
  221.2 1.0 broadcast_select_fusion.15
  222.2 1.5 collective-permute-start.19
  223.8 40.6 %sum_norm_hint.1 = (f32[384,768]{1,0:T(8,128)S(1)}, f32[4,8,256]{2,1,0:T(8,128)S(1)}) custom-call(bf16[384,3072]{1,0:T(8,128)(2,1)S(1)} %pad_maximum_fusion.1.refs_0_, f32[8,256]{1,0:T(8,128)S(1)} %maximum_maximum_fusion.refs_1_), custom_call_target="tpu_custom_call" | custom-call | bytes 117964800 | tf_op jit(solution)/shard_map/sum_norm_hint/pallas_call | solution.py:299
  264.5 1.5 multiply_add_fusion
  266.1 2.5 collective-permute-start.12
  268.6 1.0 add_convert_fusion.3
  270.4 1.2 pad_maximum_fusion.8
  273.1 2.2 collective-permute-done.11
  275.4 0.9 fusion.100
  276.8 1.2 pad_maximum_fusion.9
  278.0 2.3 collective-permute-done.22
  281.8 6.5 %collective-permute-done.24 = bf16[256,768]{1,0:T(8,128)(2,1)S(1)} collective-permute-done((bf16[256,768]{1,0:T(8,128)(2,1)S(1)}, bf16[256,768]{1,0:T(8,128)(2,1)S(1)}, u32[]{:S(2)}, u32[]{:S(2)}) %collective-permute-start.24) | collective-permute-done | bytes 393248 | tf_op jit(solution)/shard_map/ppermute | solution.py:376
  288.3 1.0 pad_maximum_fusion.12
  289.4 3.1 %collective-permute-done.26 = bf16[256,768]{1,0:T(8,128)(2,1)S(1)} collective-permute-done((bf16[256,768]{1,0:T(8,128)(2,1)S(1)}, bf16[256,768]{1,0:T(8,128)(2,1)S(1)}, u32[]{:S(2)}, u32[]{:S(2)}) %collective-permute-start.26) | collective-permute-done | bytes 393248 | tf_op jit(solution)/shard_map/ppermute | solution.py:376
  293.4 1.9 fusion.71
  295.9 1.9 fusion.68
  298.8 2.8 fusion.59
  301.6 2.0 pad_maximum_fusion
  303.7 1.8 fusion.53
  (127 shorter events, 18.7 us)
Async XLA Ops:
  49.1 6.8 %copy-start.12 = (f32[1,8,3,3072]{3,1,2,0:T(8,128)S(1)}, f32[1,8,3,3072]{3,1,2,0:T(8,128)}, u32[]{:S(2)}) copy-start(f32[1,8,3,3072]{3,1,2,0:T(8,128)} %param.11) | copy-start | bytes 884740
  49.1 7.6 %copy-start.1 = (bf16[256,3072]{1,0:T(8,128)(2,1)S(1)}, bf16[256,3072]{1,0:T(8,128)(2,1)}, u32[]{:S(2)}) copy-start(bf16[256,3072]{1,0:T(8,128)(2,1)} %get-tuple-element.20) | copy-start | bytes 4718596
  49.1 64.5 %collective-permute-start.5 = (bf16[128,3072]{1,0:T(8,128)(2,1)}, bf16[128,3072]{1,0:T(8,128)(2,1)}, u32[]{:S(2)}, u32[]{:S(2)}) collective-permute-start(bf16[128,3072]{1,0:T(8,128)(2,1)} %get-tuple-element.21), channel_id=1, source_target_pairs={{0,16},{16,0},{1,17},{17,1},{2,18},{18,2},{3,19},{19,3},{4,20},{20... | collective-permute-start | bytes 2359304 | tf_op jit(solution)/shard_map/ppermute | solution.py:414
  54.7 28.0 %collective-permute-start.4 = (bf16[128,768]{1,0:T(8,128)(2,1)}, bf16[128,768]{1,0:T(8,128)(2,1)}, u32[]{:S(2)}, u32[]{:S(2)}) collective-permute-start(bf16[128,768]{1,0:T(8,128)(2,1)} %convolution_convert_fusion.1), channel_id=1, source_target_pairs={{0,16},{16,0},{1,17},{17,1},{2,18},{18,2},{3,19},{19,3},{4,20},{20... | collective-permute-start | bytes 589832 | tf_op jit(solution)/shard_map/ppermute | solution.py:414
  57.0 3.1 %copy-start.16 = (f32[256]{0:T(256)}, f32[256]{0:T(256)S(1)}, u32[]{:S(2)}) copy-start(f32[256]{0:T(256)S(1)} %broadcast_multiply_fusion.1) | copy-start | bytes 3076
  57.6 2.6 copy-start.14
  64.6 45.9 %collective-permute-start.2 = (bf16[1,256,768]{2,1,0:T(8,128)(2,1)}, bf16[1,256,768]{2,1,0:T(8,128)(2,1)}, u32[]{:S(2)}, u32[]{:S(2)}) collective-permute-start(bf16[1,256,768]{2,1,0:T(8,128)(2,1)} %fusion.86), channel_id=1, source_target_pairs={{0,8},{4,12},{8,0},{12,4},{1,9},{5,13},{9,1},{13,5},{2,10},{6,14},... | collective-permute-start | bytes 1179656 | tf_op jit(solution)/shard_map/ppermute | solution.py:376
  70.6 41.3 %collective-permute-start = (bf16[1,256,768]{2,1,0:T(8,128)(2,1)}, bf16[1,256,768]{2,1,0:T(8,128)(2,1)}, u32[]{:S(2)}, u32[]{:S(2)}) collective-permute-start(bf16[1,256,768]{2,1,0:T(8,128)(2,1)} %fusion.89), channel_id=1, source_target_pairs={{0,8},{4,12},{8,0},{12,4},{1,9},{5,13},{9,1},{13,5},{2,10},{6,14},... | collective-permute-start | bytes 1179656 | tf_op jit(solution)/shard_map/ppermute | solution.py:376
  72.1 50.4 %collective-permute-start.13 = (bf16[256,1536]{1,0:T(8,128)(2,1)}, bf16[256,1536]{1,0:T(8,128)(2,1)}, u32[]{:S(2)}, u32[]{:S(2)}) collective-permute-start(bf16[256,1536]{1,0:T(8,128)(2,1)} %slice.174), channel_id=1, source_target_pairs={{0,16},{1,17},{2,18},{3,19},{4,20},{5,21},{6,22},{7,23},{8,24},{9,... | collective-permute-start | bytes 2359304 | tf_op jit(solution)/shard_map/ppermute | solution.py:421
  110.5 3.1 %copy-start.4 = (bf16[128,3072]{1,0:T(8,128)(2,1)S(1)}, bf16[128,3072]{1,0:T(8,128)(2,1)}, u32[]{:S(2)}) copy-start(bf16[128,3072]{1,0:T(8,128)(2,1)} %get-tuple-element.21) | copy-start | bytes 2359300
  111.8 12.9 %collective-permute-start.3 = (bf16[2,256,768]{2,1,0:T(8,128)(2,1)S(1)}, bf16[2,256,768]{2,1,0:T(8,128)(2,1)S(1)}, u32[]{:S(2)}, u32[]{:S(2)}) collective-permute-start(bf16[2,256,768]{2,1,0:T(8,128)(2,1)S(1)} %pad_maximum_fusion.6), channel_id=1, source_target_pairs={{0,4},{4,0},{8,12},{12,8},{1,5},{5,1},{9,13},{13,9},{2,6},{6,2},{1... | collective-permute-start | bytes 2359304 | tf_op jit(solution)/shard_map/ppermute | solution.py:376
  113.1 14.0 %collective-permute-start.1 = (bf16[2,256,768]{2,1,0:T(8,128)(2,1)S(1)}, bf16[2,256,768]{2,1,0:T(8,128)(2,1)S(1)}, u32[]{:S(2)}, u32[]{:S(2)}) collective-permute-start(bf16[2,256,768]{2,1,0:T(8,128)(2,1)S(1)} %pad_maximum_fusion.5), channel_id=1, source_target_pairs={{0,4},{4,0},{8,12},{12,8},{1,5},{5,1},{9,13},{13,9},{2,6},{6,2},{1... | collective-permute-start | bytes 2359304 | tf_op jit(solution)/shard_map/ppermute | solution.py:376
  115.0 1.4 copy-start.2
  115.0 1.4 copy-start.13
  116.4 6.8 %slice-start.2 = ((s8[4718592]{0:T(1024)(128)(4,1)}), s8[524288]{0:T(1024)(128)(4,1)S(1)}, s32[]{:S(2)}) async-start(s8[4718592]{0:T(1024)(128)(4,1)} %bitcast.94), calls=%async_computation.2 | async-start | bytes 1048576
  117.0 6.3 %slice-start.3 = ((s8[4718592]{0:T(1024)(128)(4,1)}), s8[4194304]{0:T(1024)(128)(4,1)S(1)}, s32[]{:S(2)}) async-start(s8[4718592]{0:T(1024)(128)(4,1)} %bitcast.94), calls=%async_computation.3 | async-start | bytes 8388608
  117.9 70.8 %collective-permute-start.28 = (bf16[256,768]{1,0:T(8,128)(2,1)}, bf16[256,768]{1,0:T(8,128)(2,1)}, u32[]{:S(2)}, u32[]{:S(2)}) collective-permute-start(bf16[256,768]{1,0:T(8,128)(2,1)} %get-tuple-element.46), channel_id=1, source_target_pairs={{0,8},{4,12},{8,0},{12,4},{1,9},{5,13},{9,1},{13,5},{2,10},{6,14},... | collective-permute-start | bytes 1179656 | tf_op jit(solution)/shard_map/ppermute | solution.py:376
  120.3 82.3 %collective-permute-start.10 = (bf16[256,1536]{1,0:T(8,128)(2,1)}, bf16[256,1536]{1,0:T(8,128)(2,1)}, u32[]{:S(2)}, u32[]{:S(2)}) collective-permute-start(bf16[256,1536]{1,0:T(8,128)(2,1)} %slice.168), channel_id=1, source_target_pairs={{0,16},{1,17},{2,18},{3,19},{4,20},{5,21},{6,22},{7,23},{8,24},{9,... | collective-permute-start | bytes 2359304 | tf_op jit(solution)/shard_map/ppermute | solution.py:421
  122.6 69.7 %collective-permute-start.14 = (bf16[256,768]{1,0:T(8,128)(2,1)S(1)}, bf16[256,768]{1,0:T(8,128)(2,1)S(1)}, u32[]{:S(2)}, u32[]{:S(2)}) collective-permute-start(bf16[256,768]{1,0:T(8,128)(2,1)S(1)} %get-tuple-element.58), channel_id=1, source_target_pairs={{0,8},{4,12},{8,0},{12,4},{1,9},{5,13},{9,1},{13,5},{2,10},{6,14},... | collective-permute-start | bytes 1179656 | tf_op jit(solution)/shard_map/ppermute | solution.py:376
  138.7 3.9 %copy-start = (bf16[4,2,256,768]{3,2,1,0:T(8,128)(2,1)S(1)}, bf16[4,2,256,768]{3,2,1,0:T(8,128)(2,1)}, u32[]{:S(2)}) copy-start(bf16[4,2,256,768]{3,2,1,0:T(8,128)(2,1)} %get-tuple-element.23.refs_1_) | copy-start | bytes 9437188
  179.9 1.0 copy-start.3
  181.0 13.7 %collective-permute-start.7 = (bf16[256,768]{1,0:T(8,128)(2,1)S(1)}, bf16[256,768]{1,0:T(8,128)(2,1)S(1)}, u32[]{:S(2)}, u32[]{:S(2)}) collective-permute-start(bf16[256,768]{1,0:T(8,128)(2,1)S(1)} %add_convert_fusion.1), channel_id=1, source_target_pairs={{0,16},{1,17},{2,18},{3,19},{4,20},{5,21},{6,22},{7,23},{8,24},{9,... | collective-permute-start | bytes 1179656 | tf_op jit(solution)/shard_map/ppermute | solution.py:417
  182.4 5.1 %copy-start.15 = (f32[256]{0:T(256)S(1)}, f32[256]{0:T(256)}, u32[]{:S(2)}) copy-start(f32[256]{0:T(256)} %copy-done.14) | copy-start | bytes 3076
  182.4 5.1 %copy-start.17 = (f32[256]{0:T(256)S(1)}, f32[256]{0:T(256)}, u32[]{:S(2)}) copy-start(f32[256]{0:T(256)} %copy-done.16) | copy-start | bytes 3076
  182.4 17.9 %collective-permute-start.9 = (bf16[256,768]{1,0:T(8,128)(2,1)S(1)}, bf16[256,768]{1,0:T(8,128)(2,1)S(1)}, u32[]{:S(2)}, u32[]{:S(2)}) collective-permute-start(bf16[256,768]{1,0:T(8,128)(2,1)S(1)} %get-tuple-element.25), channel_id=1, source_target_pairs={{0,16},{1,17},{2,18},{3,19},{4,20},{5,21},{6,22},{7,23},{8,24},{9,... | collective-permute-start | bytes 1179656 | tf_op jit(solution)/shard_map/ppermute | solution.py:417
  187.5 1.1 copy-start.19
  187.5 22.0 %slice-start = ((s8[4718592]{0:T(1024)(128)(4,1)}), s8[4194304]{0:T(1024)(128)(4,1)S(1)}, s32[]{:S(2)}) async-start(s8[4718592]{0:T(1024)(128)(4,1)} %bitcast.84), calls=%async_computation | async-start | bytes 8388608
  188.7 20.1 %collective-permute-start.8 = (bf16[256,768]{1,0:T(8,128)(2,1)S(1)}, bf16[256,768]{1,0:T(8,128)(2,1)S(1)}, u32[]{:S(2)}, u32[]{:S(2)}) collective-permute-start(bf16[256,768]{1,0:T(8,128)(2,1)S(1)} %get-tuple-element.22), channel_id=1, source_target_pairs={{0,16},{1,17},{2,18},{3,19},{4,20},{5,21},{6,22},{7,23},{8,24},{9,... | collective-permute-start | bytes 1179656 | tf_op jit(solution)/shard_map/ppermute | solution.py:417
  190.1 19.4 %slice-start.1 = ((s8[4718592]{0:T(1024)(128)(4,1)}), s8[524288]{0:T(1024)(128)(4,1)S(1)}, s32[]{:S(2)}) async-start(s8[4718592]{0:T(1024)(128)(4,1)} %bitcast.84), calls=%async_computation.1 | async-start | bytes 1048576
  192.4 24.6 %collective-permute-start.18 = (bf16[256,768]{1,0:T(8,128)(2,1)S(1)}, bf16[256,768]{1,0:T(8,128)(2,1)S(1)}, u32[]{:S(2)}, u32[]{:S(2)}) collective-permute-start(bf16[256,768]{1,0:T(8,128)(2,1)S(1)} %get-tuple-element.53), channel_id=1, source_target_pairs={{0,16},{1,17},{2,18},{3,19},{4,20},{5,21},{6,22},{7,23},{8,24},{9,... | collective-permute-start | bytes 1179656 | tf_op jit(solution)/shard_map/ppermute | solution.py:417
  194.7 26.5 %collective-permute-start.21 = (bf16[256,768]{1,0:T(8,128)(2,1)S(1)}, bf16[256,768]{1,0:T(8,128)(2,1)S(1)}, u32[]{:S(2)}, u32[]{:S(2)}) collective-permute-start(bf16[256,768]{1,0:T(8,128)(2,1)S(1)} %get-tuple-element.54), channel_id=1, source_target_pairs={{0,16},{1,17},{2,18},{3,19},{4,20},{5,21},{6,22},{7,23},{8,24},{9,... | collective-permute-start | bytes 1179656 | tf_op jit(solution)/shard_map/ppermute | solution.py:417
  200.3 68.3 %collective-permute-start.6 = (bf16[128,768]{1,0:T(8,128)(2,1)S(1)}, bf16[128,768]{1,0:T(8,128)(2,1)}, u32[]{:S(2)}, u32[]{:S(2)}) collective-permute-start(bf16[128,768]{1,0:T(8,128)(2,1)S(1)} %slice.163), channel_id=1, source_target_pairs={{16,0},{17,1},{18,2},{19,3},{20,4},{21,5},{22,6},{23,7},{24,8},{25... | collective-permute-start | bytes 589832 | tf_op jit(solution)/shard_map/ppermute | solution.py:496
  202.6 77.7 %collective-permute-start.30 = (bf16[256,768]{1,0:T(8,128)(2,1)S(1)}, bf16[256,768]{1,0:T(8,128)(2,1)}, u32[]{:S(2)}, u32[]{:S(2)}) collective-permute-start(bf16[256,768]{1,0:T(8,128)(2,1)S(1)} %broadcast_select_fusion.18), channel_id=1, source_target_pairs={{0,8},{4,12},{8,0},{12,4},{1,9},{5,13},{9,1},{13,5},{2,10},{6,14},... | collective-permute-start | bytes 1179656 | tf_op jit(solution)/shard_map/ppermute | solution.py:376
  211.2 58.6 %collective-permute-start.16 = (bf16[256,768]{1,0:T(8,128)(2,1)}, bf16[256,768]{1,0:T(8,128)(2,1)}, u32[]{:S(2)}, u32[]{:S(2)}) collective-permute-start(bf16[256,768]{1,0:T(8,128)(2,1)} %broadcast_select_fusion.16), channel_id=1, source_target_pairs={{0,8},{4,12},{8,0},{12,4},{1,9},{5,13},{9,1},{13,5},{2,10},{6,14},... | collective-permute-start | bytes 1179656 | tf_op jit(solution)/shard_map/ppermute | solution.py:376
  222.2 54.1 %collective-permute-start.19 = (bf16[256,768]{1,0:T(8,128)(2,1)}, bf16[256,768]{1,0:T(8,128)(2,1)}, u32[]{:S(2)}, u32[]{:S(2)}) collective-permute-start(bf16[256,768]{1,0:T(8,128)(2,1)} %get-tuple-element.51), channel_id=1, source_target_pairs={{0,8},{4,12},{8,0},{12,4},{1,9},{5,13},{9,1},{13,5},{2,10},{6,14},... | collective-permute-start | bytes 1179656 | tf_op jit(solution)/shard_map/ppermute | solution.py:376
  223.8 40.7 %copy-start.5 = (bf16[256,768]{1,0:T(8,128)(2,1)S(1)}, bf16[256,768]{1,0:T(8,128)(2,1)}, u32[]{:S(2)}) copy-start(bf16[256,768]{1,0:T(8,128)(2,1)} %param.15) | copy-start | bytes 1179652
  223.8 40.7 %copy-start.18 = (f32[768]{0:T(1024)S(1)}, f32[768]{0:T(1024)}, u32[]{:S(2)}) copy-start(f32[768]{0:T(1024)} %add_reduce_fusion) | copy-start | bytes 9220
  266.0 3.8 %copy-start.6 = (bf16[256,768]{1,0:T(8,128)(2,1)S(1)}, bf16[256,768]{1,0:T(8,128)(2,1)}, u32[]{:S(2)}) copy-start(bf16[256,768]{1,0:T(8,128)(2,1)} %get-tuple-element.52) | copy-start | bytes 1179652
  266.1 6.2 %collective-permute-start.12 = (bf16[128,768]{1,0:T(8,128)(2,1)S(1)}, bf16[128,768]{1,0:T(8,128)(2,1)S(1)}, u32[]{:S(2)}, u32[]{:S(2)}) collective-permute-start(bf16[128,768]{1,0:T(8,128)(2,1)S(1)} %select_convert_fusion), channel_id=1, source_target_pairs={{0,16},{16,0},{1,17},{17,1},{2,18},{18,2},{3,19},{19,3},{4,20},{20... | collective-permute-start | bytes 589832 | tf_op jit(solution)/shard_map/ppermute | solution.py:414
  269.6 5.7 %collective-permute-start.11 = (bf16[128,768]{1,0:T(8,128)(2,1)S(1)}, bf16[128,768]{1,0:T(8,128)(2,1)S(1)}, u32[]{:S(2)}, u32[]{:S(2)}) collective-permute-start(bf16[128,768]{1,0:T(8,128)(2,1)S(1)} %add_convert_fusion.3), channel_id=1, source_target_pairs={{0,16},{16,0},{1,17},{17,1},{2,18},{18,2},{3,19},{19,3},{4,20},{20... | collective-permute-start | bytes 589832 | tf_op jit(solution)/shard_map/ppermute | solution.py:414
  269.8 6.5 %copy-start.7 = (bf16[256,768]{1,0:T(8,128)(2,1)S(1)}, bf16[256,768]{1,0:T(8,128)(2,1)}, u32[]{:S(2)}) copy-start(bf16[256,768]{1,0:T(8,128)(2,1)} %broadcast_select_fusion.17) | copy-start | bytes 1179652
  269.8 10.5 %collective-permute-start.22 = (bf16[256,768]{1,0:T(8,128)(2,1)S(1)}, bf16[256,768]{1,0:T(8,128)(2,1)S(1)}, u32[]{:S(2)}, u32[]{:S(2)}) collective-permute-start(bf16[256,768]{1,0:T(8,128)(2,1)S(1)} %copy-done.6), channel_id=1, source_target_pairs={{0,8},{4,12},{8,0},{12,4},{1,9},{5,13},{9,1},{13,5},{2,10},{6,14},... | collective-permute-start | bytes 1179656 | tf_op jit(solution)/shard_map/ppermute | solution.py:376
  272.3 16.0 %collective-permute-start.24 = (bf16[256,768]{1,0:T(8,128)(2,1)S(1)}, bf16[256,768]{1,0:T(8,128)(2,1)S(1)}, u32[]{:S(2)}, u32[]{:S(2)}) collective-permute-start(bf16[256,768]{1,0:T(8,128)(2,1)S(1)} %get-tuple-element.50), channel_id=1, source_target_pairs={{0,8},{4,12},{8,0},{12,4},{1,9},{5,13},{9,1},{13,5},{2,10},{6,14},... | collective-permute-start | bytes 1179656 | tf_op jit(solution)/shard_map/ppermute | solution.py:376
  275.4 18.0 %collective-permute-start.17 = (bf16[512,768]{1,0:T(8,128)(2,1)S(1)}, bf16[512,768]{1,0:T(8,128)(2,1)S(1)}, u32[]{:S(2)}, u32[]{:S(2)}) collective-permute-start(bf16[512,768]{1,0:T(8,128)(2,1)S(1)} %pad_maximum_fusion.8), channel_id=1, source_target_pairs={{0,4},{4,0},{8,12},{12,8},{1,5},{5,1},{9,13},{13,9},{2,6},{6,2},{1... | collective-permute-start | bytes 2359304 | tf_op jit(solution)/shard_map/ppermute | solution.py:376
  276.3 16.2 %collective-permute-start.26 = (bf16[256,768]{1,0:T(8,128)(2,1)S(1)}, bf16[256,768]{1,0:T(8,128)(2,1)S(1)}, u32[]{:S(2)}, u32[]{:S(2)}) collective-permute-start(bf16[256,768]{1,0:T(8,128)(2,1)S(1)} %copy-done.7), channel_id=1, source_target_pairs={{0,8},{4,12},{8,0},{12,4},{1,9},{5,13},{9,1},{13,5},{2,10},{6,14},... | collective-permute-start | bytes 1179656 | tf_op jit(solution)/shard_map/ppermute | solution.py:376
  278.0 10.3 %copy-start.11 = (bf16[512,384]{1,0:T(8,128)(2,1)S(1)}, bf16[512,384]{1,0:T(8,128)(2,1)}, u32[]{:S(2)}) copy-start(bf16[512,384]{1,0:T(8,128)(2,1)} %get-tuple-element.56) | copy-start | bytes 1179652
  280.3 15.1 %collective-permute-start.20 = (bf16[512,768]{1,0:T(8,128)(2,1)S(1)}, bf16[512,768]{1,0:T(8,128)(2,1)S(1)}, u32[]{:S(2)}, u32[]{:S(2)}) collective-permute-start(bf16[512,768]{1,0:T(8,128)(2,1)S(1)} %pad_maximum_fusion.9), channel_id=1, source_target_pairs={{0,4},{4,0},{8,12},{12,8},{1,5},{5,1},{9,13},{13,9},{2,6},{6,2},{1... | collective-permute-start | bytes 2359304 | tf_op jit(solution)/shard_map/ppermute | solution.py:376
  280.4 17.4 %collective-permute-start.23 = (bf16[512,768]{1,0:T(8,128)(2,1)S(1)}, bf16[512,768]{1,0:T(8,128)(2,1)S(1)}, u32[]{:S(2)}, u32[]{:S(2)}) collective-permute-start(bf16[512,768]{1,0:T(8,128)(2,1)S(1)} %pad_maximum_fusion.10), channel_id=1, source_target_pairs={{0,4},{4,0},{8,12},{12,8},{1,5},{5,1},{9,13},{13,9},{2,6},{6,2},{1... | collective-permute-start | bytes 2359304 | tf_op jit(solution)/shard_map/ppermute | solution.py:376
  288.3 4.4 %collective-permute-start.15 = (bf16[512,384]{1,0:T(8,128)(2,1)S(1)}, bf16[512,384]{1,0:T(8,128)(2,1)S(1)}, u32[]{:S(2)}, u32[]{:S(2)}) collective-permute-start(bf16[512,384]{1,0:T(8,128)(2,1)S(1)} %copy-done.11), channel_id=1, source_target_pairs={{0,4},{4,0},{8,12},{12,8},{1,5},{5,1},{9,13},{13,9},{2,6},{6,2},{1... | collective-permute-start | bytes 1179656 | tf_op jit(solution)/shard_map/ppermute | solution.py:376
  289.4 3.4 %copy-start.9 = (bf16[512,384]{1,0:T(8,128)(2,1)S(1)}, bf16[512,384]{1,0:T(8,128)(2,1)}, u32[]{:S(2)}) copy-start(bf16[512,384]{1,0:T(8,128)(2,1)} %get-tuple-element.44) | copy-start | bytes 1179652
  289.4 4.0 %copy-start.10 = (bf16[512,384]{1,0:T(8,128)(2,1)S(1)}, bf16[512,384]{1,0:T(8,128)(2,1)}, u32[]{:S(2)}) copy-start(bf16[512,384]{1,0:T(8,128)(2,1)} %get-tuple-element.55) | copy-start | bytes 1179652
  292.5 6.1 %collective-permute-start.31 = (bf16[512,768]{1,0:T(8,128)(2,1)S(1)}, bf16[512,768]{1,0:T(8,128)(2,1)S(1)}, u32[]{:S(2)}, u32[]{:S(2)}) collective-permute-start(bf16[512,768]{1,0:T(8,128)(2,1)S(1)} %pad_maximum_fusion.12), channel_id=1, source_target_pairs={{0,4},{4,0},{8,12},{12,8},{1,5},{5,1},{9,13},{13,9},{2,6},{6,2},{1... | collective-permute-start | bytes 2359304 | tf_op jit(solution)/shard_map/ppermute | solution.py:376
  292.8 5.9 %collective-permute-start.29 = (bf16[512,384]{1,0:T(8,128)(2,1)S(1)}, bf16[512,384]{1,0:T(8,128)(2,1)S(1)}, u32[]{:S(2)}, u32[]{:S(2)}) collective-permute-start(bf16[512,384]{1,0:T(8,128)(2,1)S(1)} %copy-done.9), channel_id=1, source_target_pairs={{0,4},{4,0},{8,12},{12,8},{1,5},{5,1},{9,13},{13,9},{2,6},{6,2},{1... | collective-permute-start | bytes 1179656 | tf_op jit(solution)/shard_map/ppermute | solution.py:376
  293.3 10.3 %collective-permute-start.27 = (bf16[512,768]{1,0:T(8,128)(2,1)S(1)}, bf16[512,768]{1,0:T(8,128)(2,1)S(1)}, u32[]{:S(2)}, u32[]{:S(2)}) collective-permute-start(bf16[512,768]{1,0:T(8,128)(2,1)S(1)} %pad_maximum_fusion.11), channel_id=1, source_target_pairs={{0,4},{4,0},{8,12},{12,8},{1,5},{5,1},{9,13},{13,9},{2,6},{6,2},{1... | collective-permute-start | bytes 2359304 | tf_op jit(solution)/shard_map/ppermute | solution.py:376
  295.4 8.3 %collective-permute-start.25 = (bf16[512,384]{1,0:T(8,128)(2,1)S(1)}, bf16[512,384]{1,0:T(8,128)(2,1)S(1)}, u32[]{:S(2)}, u32[]{:S(2)}) collective-permute-start(bf16[512,384]{1,0:T(8,128)(2,1)S(1)} %get-tuple-element.48), channel_id=1, source_target_pairs={{0,4},{4,0},{8,12},{12,8},{1,5},{5,1},{9,13},{13,9},{2,6},{6,2},{1... | collective-permute-start | bytes 1179656 | tf_op jit(solution)/shard_map/ppermute | solution.py:376
  297.8 1.0 copy-start.8
